TPU v7x, 128 devices: a whole 4x4x4 slice. The times are simulated.
128 devices in a mesh: dp: 32 (over z, y, x_lo), section: 2 (over core), tensor: 2 (over x_hi).
Axes of the slice: x: 4 (x_hi: 2, x_lo: 2; x = x_hi * 2 + x_lo), y: 4, z: 4, core: 2. Of those that a mesh axis runs over, the one named last changes fastest.
Arguments:
- llm_grad: bfloat16 [2, 2048, 5120], P(None, 'dp', 'tensor'), may hold values from -6 to 6
- slots: int32 [2, 1536], P(None, 'dp'), may hold values from 0 to 2047, as said below
- frames: int32 [2, 64], P(None, 'dp'), may hold values from 0 to 12, as said below
- saved_in: bfloat16 [2, 2, 6144, 1280], P('section', None, 'dp'), may hold values from -6 to 6
- ln_gain: float32 [2, 1280], P('section'), may hold values from 0.1 to 1.9
- w_in: bfloat16 [2, 1280, 5120], P('section', None, 'tensor'), may hold values from -0.15625 to 0.15625
- w_out: bfloat16 [2, 5120, 1280], P('section', 'tensor'), may hold values from -0.078125 to 0.078125
Outputs:
- input_grads: bfloat16 [2, 2, 6144, 1280], P('section', None, 'dp')
- grad_in: bfloat16 [2, 1280, 5120], P('section', 'dp', 'tensor')
- grad_out: bfloat16 [2, 5120, 1280], P('section', 'tensor', 'dp')
Inputs may be any that keep to these rules, and one draw needn't show every extreme that they name: `frames`: within a replica's 2 samples of one micro-batch the frame counts sum to at most 12, and exactly one replica of each micro-batch reaches it; over all replicas of one micro-batch they sum to 132. Slot j of replica r holds one of the 64 positions of replica (r + j) mod 32; all slots of one micro-batch are distinct positions.
All inputs are finite; a program needn't handle non-finite values.
Results may differ from a plain program's by a relative error of at most 0.034.
Values may be sent and summed in bfloat16 or wider, within the bound.
No kernel may reach another device: no remote copies, remote signals or barrier semaphores. Data moves between devices by JAX's collectives and lax.ppermute only.
A program may use at most 128 MiB of HBM per device.

v0:
```python
import jax
import jax.numpy as jnp
from jax import lax
from jax.experimental import pallas as pl
from jax.experimental.pallas import tpu as pltpu
from jax.sharding import PartitionSpec as P

TPF = 4
BITS = 5
ORDERS = ((0, 1, 2, 3, 4), (1, 2, 0, 3, 4), (2, 3, 4, 0, 1), (3, 4, 2, 0, 1), (4, 0, 1, 2, 3))
SHARED = (
    ((0,), (1,), (2,), (3,), (4,)),
    ((0,), (1,), (2,), (3,), (4,)),
    ((0, 3), (1,), (2,), (4,)),
    ((0, 1), (2, 3), (4,)),
    ((0, 1), (2, 3), (4,)),
)
LAYOUTS = (
    ((32,), (0,)),
    ((2, 4, 4), (1, 0, 2)),
    ((4, 8), (1, 0)),
    ((4, 2, 4), (2, 1, 0)),
    ((16, 2), (1, 0)),
)


def gelu_and_slope(a):
    square = a * a
    tangent = jnp.tanh(0.7978845608 * a * (1.0 + 0.044715 * square))
    half = 0.5 * (1.0 + tangent)
    slope = half + (0.5 * 0.7978845608) * a * (1.0 - tangent * tangent) * (
        1.0 + (3.0 * 0.044715) * square
    )
    return (a * half).astype(jnp.bfloat16), slope.astype(jnp.bfloat16)


def split_index(r):
    return r // 8, (r // 2) % 4, r % 2


def to_code(r):
    z, y, x = split_index(r)
    return ((z ^ (z >> 1)) << 3) | ((y ^ (y >> 1)) << 1) | x


def from_code(q):
    gz, gy, x = q >> 3, (q >> 1) & 3, q & 1
    return ((gz ^ (gz >> 1)) << 3) | ((gy ^ (gy >> 1)) << 1) | x


def neighbour_pairs(bit):
    return [(r, from_code(to_code(r) ^ (1 << (BITS - 1 - bit)))) for r in range(1 << BITS)]


def dot(a, b, ca, cb):
    return lax.dot_general(a, b, (((ca,), (cb,)), ((), ())), preferred_element_type=jnp.float32)


def finish_kernel(g_ref, mine_ref, other_ref, x_ref, gain_ref, out_ref):
    x = x_ref[...].astype(jnp.float32)
    centered = x - jnp.mean(x, axis=-1, keepdims=True)
    rstd = lax.rsqrt(jnp.mean(centered * centered, axis=-1, keepdims=True) + 1e-05)
    xhat = centered * rstd
    scaled = (mine_ref[...].astype(jnp.float32) + other_ref[...].astype(jnp.float32)) * gain_ref[...]
    out_ref[...] = (
        g_ref[...].astype(jnp.float32)
        + rstd
        * (
            scaled
            - jnp.mean(scaled, axis=-1, keepdims=True)
            - xhat * jnp.mean(scaled * xhat, axis=-1, keepdims=True)
        )
    ).astype(jnp.bfloat16)


def finish(incoming, mine, other, x, gain, tile):
    rows, width = incoming.shape
    wide = pl.BlockSpec((tile, width), lambda i: (i, 0))
    return pl.pallas_call(
        finish_kernel,
        grid=(rows // tile,),
        in_specs=[wide, wide, wide, wide, pl.BlockSpec((1, width), lambda i: (0, 0))],
        out_specs=wide,
        out_shape=jax.ShapeDtypeStruct((rows, width), jnp.bfloat16),
        compiler_params=pltpu.CompilerParams(vmem_limit_bytes=8 * 1024 * 1024),
        cost_estimate=pl.CostEstimate(
            flops=20 * rows * width, bytes_accessed=10 * rows * width, transcendentals=0
        ),
    )(incoming, mine, other, x, gain)


def ask_tokens(seq_dev, slots, frames, sec, rep, peers):
    cap = slots.shape[1]
    per = -(-cap // peers)
    counts = TPF * jnp.sum(frames, axis=1)
    count = lax.dynamic_index_in_dim(counts, sec, 0, keepdims=False)
    wanted = lax.dynamic_index_in_dim(slots, sec, 0, keepdims=False)
    wanted = jnp.concatenate([wanted, jnp.zeros((per * peers - cap,), jnp.int32)])
    j = jnp.arange(per * peers)
    position = jnp.where(j < count, wanted - seq_dev * ((rep + j) % peers) + 1, 0)
    position = position.reshape(per, 1, peers)
    holder = jnp.arange(peers)
    turned = (jnp.arange(peers)[None, :] == ((holder - rep) % peers)[:, None]).astype(jnp.int32)
    requests = jnp.sum(position * turned[None], axis=2).T
    return lax.all_to_all(requests, "dp", 0, 0, tiled=True).reshape(-1)


def fetch_tokens(llm_grad, asked, cap, sec, ten, rep, peers):
    seq_dev, width = llm_grad.shape[1:]
    per = -(-cap // peers)
    pick = (asked[:, None] == jnp.arange(1, seq_dev + 1)[None, :]).astype(jnp.bfloat16)
    held = lax.dynamic_index_in_dim(llm_grad, sec, 0, keepdims=False)
    rows = dot(pick, held, 1, 0).astype(jnp.bfloat16)
    got = lax.all_to_all(rows, "dp", 0, 0, tiled=True)
    both = ("section", "tensor")
    first_own = lax.ppermute(got, both, [(0, 2), (1, 3)])
    first_other = lax.ppermute(got, both, [(0, 3), (1, 2)])
    second_other = lax.ppermute(got, both, [(2, 3), (3, 2)])
    half = width // 2
    row = jnp.arange(cap * 4)
    tok, part = row // 4, row % 4
    source = (
        ((part // 2 != ten).astype(jnp.int32) * 2 + part % 2) * (per * peers)
        + ((rep + tok) % peers) * per
        + tok // peers
    )
    spread = (source[:, None] == jnp.arange(4 * per * peers)[None, :]).astype(jnp.bfloat16)
    out = []
    for own, other in ((first_own, first_other), (got, second_other)):
        stacked = jnp.concatenate([own[:, :half], own[:, half:], other[:, :half], other[:, half:]])
        out.append(dot(spread, stacked, 1, 0).astype(jnp.bfloat16))
    return jnp.concatenate(out)


def reordered(left, stream):
    width = left.shape[1]
    sizes, axes = LAYOUTS[stream]
    split = left.reshape((2,) + sizes + (width >> BITS, -1))
    axes = (0,) + tuple(1 + a for a in axes) + (len(axes) + 1, len(axes) + 2)
    return split.transpose(axes).reshape(left.shape)


def after(value, *others):
    return lax.optimization_barrier((value, others))[0]


def reduce_weight_grads(left, right, between):
    width = left.shape[1]
    span = right.shape[2] // BITS
    lefts = [reordered(left, i) for i in range(BITS)]
    received = [[] for _ in range(BITS)]

    def group(i, lo, hi):
        total = lax.dot_general(
            lefts[i][:, lo:hi],
            right[:, :, i * span : (i + 1) * span],
            (((2,), (1,)), ((0,), (0,))),
            preferred_element_type=jnp.float32,
        )
        for piece in received[i]:
            total = total + piece[:, lo:hi].astype(jnp.float32)
        return total.astype(jnp.bfloat16)

    last = None
    for t in range(BITS):
        for streams in SHARED[t]:
            if t:
                for i in streams:
                    received[i][-1] = after(received[i][-1], last)
            sends = [group(i, width >> (t + 1), width >> t) for i in streams]
            last = sends[0] if len(sends) == 1 else jnp.concatenate(sends, axis=2)
            piece = lax.ppermute(last, "dp", neighbour_pairs(ORDERS[streams[0]][t]))
            for k, i in enumerate(streams):
                received[i].append(piece[:, :, k * span : (k + 1) * span])
        if t == 0:
            middle = between(last)
    result = jnp.concatenate([group(i, 0, width >> BITS) for i in range(BITS)], axis=2)
    return result, after(middle, last)


def per_device(llm_grad, slots, frames, saved_in, ln_gain, w_in, w_out):
    peers = lax.axis_size("dp")
    sec = lax.axis_index("section")
    ten = lax.axis_index("tensor")
    rep = lax.axis_index("dp")
    micro_count, tok_rows, width = saved_in.shape[1:]
    rows = micro_count * tok_rows
    gain = ln_gain
    weight_in = w_in[0]
    weight_out = w_out[0]

    widen = saved_in[0].reshape(rows, width).astype(jnp.float32)
    centered = widen - jnp.mean(widen, axis=-1, keepdims=True)
    rstd = lax.rsqrt(jnp.mean(centered * centered, axis=-1, keepdims=True) + 1e-05)
    xhat = centered * rstd
    normed = (xhat * gain).astype(jnp.bfloat16)

    asked = ask_tokens(llm_grad.shape[1], slots, frames, sec, rep, peers)
    normed, asked = lax.optimization_barrier((normed, asked))
    upstream = lax.optimization_barrier(
        fetch_tokens(llm_grad, asked, slots.shape[1], sec, ten, rep, peers)
    )
    activ, slope = lax.optimization_barrier(gelu_and_slope(dot(normed, weight_in, 1, 0)))

    order = from_code(to_code(rep) ^ jnp.arange(peers))
    chunk = width // peers
    order = (order[:, None] * chunk + jnp.arange(chunk)[None, :]).reshape(-1)
    turn = (order[:, None] == jnp.arange(width)[None, :]).astype(jnp.bfloat16)

    x = saved_in[0].reshape(rows, width)

    def pre_gradient(incoming):
        return lax.optimization_barrier(
            (dot(incoming, weight_out, 1, 1) * slope).astype(jnp.bfloat16)
        )

    both = ("section", "tensor")
    first_own = lax.ppermute(got, both, [(0, 2), (1, 3)])
    first_other = lax.ppermute(got, both, [(0, 3), (1, 2)])
    second_other = lax.ppermute(got, both, [(2, 3), (3, 2)])
    half = width // 2
    row = jnp.arange(cap * 4)
    tok, part = row // 4, row % 4
    source = (
        ((part // 2 != ten).astype(jnp.int32) * 2 + part % 2) * (per * peers)
        + ((rep + tok) % peers) * per
        + tok // peers
    )
    spread = (source[:, None] == jnp.arange(4 * per * peers)[None, :]).astype(jnp.bfloat16)
    out = []
    for own, other in ((first_own, first_other), (got, second_other)):
        stacked = jnp.concatenate([own[:, :half], own[:, half:], other[:, :half], other[:, half:]])
        out.append(dot(spread, stacked, 1, 0).astype(jnp.bfloat16))
    return jnp.concatenate(out)


def reordered(left, stream):
    width = left.shape[1]
    sizes, axes = LAYOUTS[stream]
    split = left.reshape((2,) + sizes + (width >> BITS, -1))
    axes = (0,) + tuple(1 + a for a in axes) + (len(axes) + 1, len(axes) + 2)
    return split.transpose(axes).reshape(left.shape)


def after(value, *others):
    return lax.optimization_barrier((value, others))[0]


def reduce_weight_grads(left, right, between):
    width = left.shape[1]
    span = right.shape[2] // BITS
    lefts = [reordered(left, i) for i in range(BITS)]
    received = [[] for _ in range(BITS)]

    def group(i, lo, hi):
        total = lax.dot_general(
            lefts[i][:, lo:hi],
            right[:, :, i * span : (i + 1) * span],
            (((2,), (1,)), ((0,), (0,))),
            preferred_element_type=jnp.float32,
        )
        for piece in received[i]:
            total = total + piece[:, lo:hi].astype(jnp.float32)
        return total.astype(jnp.bfloat16)

    last = None
    for t in range(BITS):
        for streams in SHARED[t]:
            if t:
                for i in streams:
                    received[i][-1] = after(received[i][-1], last)
            sends = [group(i, width >> (t + 1), width >> t) for i in streams]
            last = sends[0] if len(sends) == 1 else jnp.concatenate(sends, axis=2)
            piece = lax.ppermute(last, "dp", neighbour_pairs(ORDERS[streams[0]][t]))
            for k, i in enumerate(streams):
                received[i].append(piece[:, :, k * span : (k + 1) * span])
        if t == 0:
            middle = between(last)
    result = jnp.concatenate([group(i, 0, width >> BITS) for i in range(BITS)], axis=2)
    return result, after(middle, last)


def per_device(llm_grad, slots, frames, saved_in, ln_gain, w_in, w_out):
    peers = lax.axis_size("dp")
    sec = lax.axis_index("section")
    ten = lax.axis_index("tensor")
    rep = lax.axis_index("dp")
    micro_count, tok_rows, width = saved_in.shape[1:]
    rows = micro_count * tok_rows
    gain = ln_gain
    weight_in = w_in[0]
    weight_out = w_out[0]

    widen = saved_in[0].reshape(rows, width).astype(jnp.float32)
    centered = widen - jnp.mean(widen, axis=-1, keepdims=True)
    rstd = lax.rsqrt(jnp.mean(centered * centered, axis=-1, keepdims=True) + 1e-05)
    xhat = centered * rstd
    normed = (xhat * gain).astype(jnp.bfloat16)

    asked = ask_tokens(llm_grad.shape[1], slots, frames, sec, rep, peers)
    normed, asked = lax.optimization_barrier((normed, asked))
    upstream = lax.optimization_barrier(
        fetch_tokens(llm_grad, asked, slots.shape[1], sec, ten, rep, peers)
    )
    activ, slope = lax.optimization_barrier(gelu_and_slope(dot(normed, weight_in, 1, 0)))

    order = from_code(to_code(rep) ^ jnp.arange(peers))
    chunk = width // peers
    order = (order[:, None] * chunk + jnp.arange(chunk)[None, :]).reshape(-1)
    turn = (order[:, None] == jnp.arange(width)[None, :]).astype(jnp.bfloat16)

    x = saved_in[0].reshape(rows, width)

    def pre_gradient(incoming):
        return lax.optimization_barrier(
            (dot(incoming, weight_out, 1, 1) * slope).astype(jnp.bfloat16)
        )

    def operands(incoming, d_pre):
        left = jnp.stack([normed_t, dot(turn, incoming, 1, 1).astype(jnp.bfloat16)])
        return [reordered(left, i) for i in range(BITS)], jnp.stack([d_pre, activ])

    both = ("section", "tensor")
    d_pre = pre_gradient(upstream)
    partial = dot(d_pre, weight_in, 1, 1).astype(jnp.bfloat16)
    other = lax.ppermute(partial, both, [(2, 1), (3, 0)])
    terms, rest = [], ln_gain
    for _ in range(3):
        term = lax.reduce_precision(rest, exponent_bits=8, mantissa_bits=7)
        terms.append(term.astype(jnp.bfloat16))
        rest = rest - term
    packed = jnp.concatenate(
        [partial, upstream, x] + [jnp.broadcast_to(term, (16, width)) for term in terms]
    )
    packed = lax.ppermute(packed, "section", [(1, 0)])
    mine, passed, later_x = (packed[k * rows : (k + 1) * rows] for k in range(3))
    later_gain = sum(
        packed[3 * rows + 16 * k : 3 * rows + 16 * k + 1].astype(jnp.float32) for k in range(3)
    )
    normed_t = dot(turn, after(normed, partial), 1, 1).astype(jnp.bfloat16)
    grad_last = finish(passed, mine, other, later_x, later_gain, tok_rows // 2)

    incoming = jnp.where(sec == 1, upstream, grad_last)
    d_pre = pre_gradient(incoming)
    incoming_t = dot(turn, incoming, 1, 1).astype(jnp.bfloat16)

    def partial_here(last):
        return dot(after(d_pre, last), weight_in, 1, 1).astype(jnp.bfloat16)

    def exchange(last):
        partial = partial_here(last)
        return (
            partial,
            lax.ppermute(partial, both, [(0, 1), (1, 0)]),
            lax.ppermute(after(grad_last, last), "section", [(0, 1)]),
        )

    reduced, (partial, other, returned) = reduce_weight_grads(
        jnp.stack([normed_t, incoming_t]), jnp.stack([d_pre, activ]), exchange
    )
    grad_here = finish(incoming, partial, other, x, ln_gain, tok_rows // 2)
    results = jnp.where(sec == 1, returned, grad_here)
    return (
        results.reshape(1, micro_count, tok_rows, width),
        reduced[0][None],
        reduced[1].T[None],
    )


def solution(mesh):
    return jax.shard_map(
        per_device,
        mesh=mesh,
        in_specs=(
            P(None, "dp", "tensor"),
            P(None, "dp"),
            P(None, "dp"),
            P("section", None, "dp", None),
            P("section", None),
            P("section", None, "tensor"),
            P("section", "tensor", None),
        ),
        out_specs=(
            P("section", None, "dp", None),
            P("section", "dp", "tensor"),
            P("section", "tensor", "dp"),
        ),
        check_vma=False,
    )
```

profile of v0, /device:TPU:0, one launch (start us, length us, event | category | flops | bytes accessed | tf_op | source)
XLA Modules:
  0.0 195.8 jit_solution(11305384126560524694)
XLA Ops:
  0.7 0.9 reduce_sum.38
  3.8 0.7 copy.25
  4.5 9.3 %all-to-all-start = ((s32[32,1,2]{2,1,0:T(1,128)}), s32[32,1,2]{2,1,0:T(1,128)S(1)}, u32[]{:S(2)}, u32[]{:S(2)}) async-start(s32[32,1,2]{2,1,0:T(1,128)} %copy.25), calls=%async_computation | async-start | bytes 32768 | tf_op jit(solution)/shard_map/all_to_all | solution.py:105
  13.9 1.4 convert_reduce_fusion
  15.3 1.6 fusion.33
  17.6 4.4 %all-to-all-done = s32[32,1,2]{2,1,0:T(1,128)S(1)} async-done(((s32[32,1,2]{2,1,0:T(1,128)}), s32[32,1,2]{2,1,0:T(1,128)S(1)}, u32[]{:S(2)}, u32[]{:S(2)}) %all-to-all-start) | async-done | bytes 288 | tf_op jit(solution)/shard_map/all_to_all | solution.py:105
  22.5 0.7 reduce.12
  23.6 0.9 all_to_all.16
  24.5 3.9 %all-to-all-start.1 = ((bf16[32,2,2560]{2,1,0:T(2,128)(2,1)}), bf16[32,2,2560]{2,1,0:T(2,128)(2,1)S(1)}, u32[]{:S(2)}, u32[]{:S(2)}) async-start(bf16[32,2,2560]{2,1,0:T(2,128)(2,1)} %all_to_all.16), calls=%async_computation.1 | async-start | bytes 655360 | tf_op jit(solution)/shard_map/all_to_all | solution.py:114
  28.4 8.7 %add_convert_fusion = (bf16[384,2560]{1,0:T(8,128)(2,1)}, bf16[384,2560]{1,0:T(8,128)(2,1)}) fusion(bf16[384,1280]{1,0:T(8,128)(2,1)S(1)} %multiply_convert_fusion.1, bf16[1,1280,2560]{2,1,0:T(8,128)(2,1)} %param.12), kind=kOutput, calls=%fused_computation.25 | convolution fusion | flops 2534277120 | bytes 11468800 | tf_op jit(solution)/shard_map/dot_general | solution.py:56
  37.1 1.1 all-to-all-done.1
  39.0 4.0 %collective-permute-start.1 = (bf16[64,2560]{1,0:T(8,128)(2,1)S(1)}, bf16[64,2560]{1,0:T(8,128)(2,1)S(1)}, u32[]{:S(2)}, u32[]{:S(2)}) collective-permute-start(bf16[64,2560]{1,0:T(8,128)(2,1)S(1)} %all_to_all.18), channel_id=1, source_target_pairs={{0,3},{1,2},{4,7},{5,6},{8,11},{9,10},{12,15},{13,14},{16,19},{17,... | collective-permute-start | bytes 983048 | tf_op jit(solution)/shard_map/ppermute | solution.py:117
  43.0 1.3 collective-permute-start
  44.4 3.7 %collective-permute-done.1 = bf16[64,2560]{1,0:T(8,128)(2,1)S(1)} collective-permute-done((bf16[64,2560]{1,0:T(8,128)(2,1)S(1)}, bf16[64,2560]{1,0:T(8,128)(2,1)S(1)}, u32[]{:S(2)}, u32[]{:S(2)}) %collective-permute-start.1) | collective-permute-done | bytes 327712 | tf_op jit(solution)/shard_map/ppermute | solution.py:117
  48.8 1.1 copy-done.6
  50.0 5.9 %fusion.16 = bf16[384,2560]{1,0:T(8,128)(2,1)S(1)} fusion(bf16[384,2560]{1,0:T(8,128)(2,1)S(1)} %copy-done.6, bf16[384,1280]{1,0:T(8,128)(2,1)S(1)} %pad_maximum_fusion, bf16[1,2560,1280]{2,1,0:T(8,128)(2,1)} %param.13), kind=kOutput, calls=%fused_computation.23 | convolution fusion | flops 2519531520 | bytes 11468800 | tf_op jit(solution)/shard_map/dot_general | solution.py:56
  55.9 4.0 %constant_dynamic-update-slice_fusion.5 = (bf16[1200,1280]{1,0:T(8,128)(2,1)}, bf16[384,1280]{1,0:T(8,128)(2,1)}) fusion(bf16[384,2560]{1,0:T(8,128)(2,1)S(1)} %fusion.16, bf16[1,1280,2560]{2,1,0:T(8,128)(2,1)S(1)} %bitcast.160), kind=kOutput, calls=%fused_computation.188 | convolution fusion | flops 2517073920 | bytes 10485760 | tf_op jit(solution)/shard_map/dot_general | solution.py:56
  59.9 1.0 constant_dynamic-update-slice_fusion.4
  61.0 1.0 constant_dynamic-update-slice_fusion.3
  63.8 1.3 collective-permute-start.3
  65.4 1.5 collective-permute-start.4
  66.8 3.1 %fusion.24 = bf16[1280,384]{1,0:T(8,128)(2,1)S(1)} fusion(bf16[384,1280]{1,0:T(8,128)(2,1)} %copy-done.5, s32[1280]{0:T(1024)S(1)} %add.428), kind=kOutput, calls=%fused_computation.42 | convolution fusion | flops 1260421120 | bytes 1971200 | tf_op jit(solution)/shard_map/dot_general | solution.py:56
  70.0 3.1 %collective-permute-done.3 = bf16[1200,1280]{1,0:T(8,128)(2,1)} collective-permute-done((bf16[1200,1280]{1,0:T(8,128)(2,1)}, bf16[1200,1280]{1,0:T(8,128)(2,1)}, u32[]{:S(2)}, u32[]{:S(2)}) %collective-permute-start.3) | collective-permute-done | bytes 3072032 | tf_op jit(solution)/shard_map/ppermute | solution.py:335
  73.0 0.8 fusion.175.gain_ref
  73.8 2.1 %fusion.202 = (bf16[384,1280]{1,0:T(8,128)(2,1)S(1)}, bf16[384,1280]{1,0:T(8,128)(2,1)S(1)}, bf16[384,1280]{1,0:T(8,128)(2,1)S(1)}) fusion(bf16[1200,1280]{1,0:T(8,128)(2,1)} %collective-permute-done.3), kind=kLoop, calls=%fused_computation.263 | loop fusion | bytes 5898240 | tf_op jit(solution)/shard_map/slice | solution.py:336
  75.9 7.8 %collective-permute-done.4.other_ref = bf16[384,1280]{1,0:T(8,128)(2,1)S(1)} collective-permute-done((bf16[384,1280]{1,0:T(8,128)(2,1)}, bf16[384,1280]{1,0:T(8,128)(2,1)S(1)}, u32[]{:S(2)}, u32[]{:S(2)}) %collective-permute-start.4) | collective-permute-done | bytes 983072 | tf_op jit(solution)/shard_map/ppermute | solution.py:326
  83.7 1.7 shard_map.94
  85.6 1.4 copy-done.7
  87.0 2.7 %fusion.19 = bf16[384,2560]{1,0:T(8,128)(2,1)S(1)} fusion(bf16[384,2560]{1,0:T(8,128)(2,1)S(1)} %copy-done.7, bf16[384,1280]{1,0:T(8,128)(2,1)S(1)} %broadcast_select_fusion.1.g_ref, bf16[1,2560,1280]{2,1,0:T(8,128)(2,1)S(1)} %bitcast.158), kind=kOutput, calls=%fused_computation.24 | convolution fusion | flops 2519531520 | bytes 11468800 | tf_op jit(solution)/shard_map/dot_general | solution.py:56
  89.7 1.9 fusion.25
  93.1 1.3 copy-done.4
  94.7 0.8 convolution_convert_fusion.3
  95.6 2.8 %collective-permute-start.11 = (bf16[2,640,512]{2,1,0:T(8,128)(2,1)S(1)}, bf16[2,640,512]{2,1,0:T(8,128)(2,1)S(1)}, u32[]{:S(2)}, u32[]{:S(2)}) collective-permute-start(bf16[2,640,512]{2,1,0:T(8,128)(2,1)S(1)} %convolution_convert_fusion.3), channel_id=1, source_target_pairs={{0,96},{4,100},{8,104},{12,108},{16,112},{20,116},{24,120},{28,124... | collective-permute-start | bytes 3932168 | tf_op jit(solution)/shard_map/ppermute | solution.py:274
  98.4 0.8 convolution_convert_fusion.4
  99.5 0.8 convolution_convert_fusion.5
  100.4 2.8 %collective-permute-start.9 = (bf16[2,640,512]{2,1,0:T(8,128)(2,1)S(1)}, bf16[2,640,512]{2,1,0:T(8,128)(2,1)S(1)}, u32[]{:S(2)}, u32[]{:S(2)}) collective-permute-start(bf16[2,640,512]{2,1,0:T(8,128)(2,1)S(1)} %convolution_convert_fusion.5), channel_id=1, source_target_pairs={{0,24},{4,28},{8,16},{12,20},{16,8},{20,12},{24,0},{28,4},{32,56},... | collective-permute-start | bytes 3932168 | tf_op jit(solution)/shard_map/ppermute | solution.py:274
  103.2 0.8 convolution_convert_fusion.6
  104.8 0.8 convolution_convert_fusion.7
  105.6 1.3 collective-permute-start.7
  106.9 19.1 %collective-permute-done.11 = bf16[2,640,512]{2,1,0:T(8,128)(2,1)S(1)} collective-permute-done((bf16[2,640,512]{2,1,0:T(8,128)(2,1)S(1)}, bf16[2,640,512]{2,1,0:T(8,128)(2,1)S(1)}, u32[]{:S(2)}, u32[]{:S(2)}) %collective-permute-start.11) | collective-permute-done | bytes 1310752 | tf_op jit(solution)/shard_map/ppermute | solution.py:274
  126.9 2.7 %collective-permute-done.10 = bf16[2,640,512]{2,1,0:T(8,128)(2,1)S(1)} collective-permute-done((bf16[2,640,512]{2,1,0:T(8,128)(2,1)S(1)}, bf16[2,640,512]{2,1,0:T(8,128)(2,1)S(1)}, u32[]{:S(2)}, u32[]{:S(2)}) %collective-permute-start.10) | collective-permute-done | bytes 1310752 | tf_op jit(solution)/shard_map/ppermute | solution.py:274
  130.8 1.6 collective-permute-done.8
  133.0 0.9 collective-permute-start.16
  133.9 5.6 %fusion.29.mine_ref = bf16[384,1280]{1,0:T(8,128)(2,1)S(1)} fusion(bf16[384,2560]{1,0:T(8,128)(2,1)S(1)} %fusion.19, bf16[1,1280,2560]{2,1,0:T(8,128)(2,1)} %param.12), kind=kOutput, calls=%fused_computation.45 | convolution fusion | flops 2517073920 | bytes 9502720 | tf_op jit(solution)/shard_map/dot_general | solution.py:56
  139.5 3.9 %collective-permute-start.5 = (bf16[384,1280]{1,0:T(8,128)(2,1)S(1)}, bf16[384,1280]{1,0:T(8,128)(2,1)S(1)}, u32[]{:S(2)}, u32[]{:S(2)}) collective-permute-start(bf16[384,1280]{1,0:T(8,128)(2,1)S(1)} %fusion.29.mine_ref), channel_id=1, source_target_pairs={{0,1},{1,0},{4,5},{5,4},{8,9},{9,8},{12,13},{13,12},{16,17},{17,16... | collective-permute-start | bytes 2949128 | tf_op jit(solution)/shard_map/ppermute | solution.py:354
  143.5 1.4 collective-permute-start.6
  146.1 2.1 %collective-permute-done.16 = bf16[2,320,512]{2,1,0:T(8,128)(2,1)S(1)} collective-permute-done((bf16[2,320,512]{2,1,0:T(8,128)(2,1)S(1)}, bf16[2,320,512]{2,1,0:T(8,128)(2,1)S(1)}, u32[]{:S(2)}, u32[]{:S(2)}) %collective-permute-start.16) | collective-permute-done | bytes 655392 | tf_op jit(solution)/shard_map/ppermute | solution.py:274
  148.1 1.1 collective-permute-start.14
  149.2 1.1 collective-permute-start.12
  151.1 12.4 %collective-permute-done.14 = bf16[2,320,512]{2,1,0:T(8,128)(2,1)S(1)} collective-permute-done((bf16[2,320,512]{2,1,0:T(8,128)(2,1)S(1)}, bf16[2,320,512]{2,1,0:T(8,128)(2,1)S(1)}, u32[]{:S(2)}, u32[]{:S(2)}) %collective-permute-start.14) | collective-permute-done | bytes 655392 | tf_op jit(solution)/shard_map/ppermute | solution.py:274
  163.5 1.1 collective-permute-start.19
  165.0 1.2 collective-permute-start.20
  166.5 0.9 collective-permute-start.18
  167.8 5.6 %collective-permute-done.20 = bf16[2,160,512]{2,1,0:T(8,128)(2,1)S(1)} collective-permute-done((bf16[2,160,512]{2,1,0:T(8,128)(2,1)S(1)}, bf16[2,160,512]{2,1,0:T(8,128)(2,1)S(1)}, u32[]{:S(2)}, u32[]{:S(2)}) %collective-permute-start.20) | collective-permute-done | bytes 327712 | tf_op jit(solution)/shard_map/ppermute | solution.py:274
  174.1 3.8 %collective-permute-done.19 = bf16[2,160,1024]{2,1,0:T(8,128)(2,1)S(1)} collective-permute-done((bf16[2,160,1024]{2,1,0:T(8,128)(2,1)S(1)}, bf16[2,160,1024]{2,1,0:T(8,128)(2,1)S(1)}, u32[]{:S(2)}, u32[]{:S(2)}) %collective-permute-start.19) | collective-permute-done | bytes 655392 | tf_op jit(solution)/shard_map/ppermute | solution.py:274
  179.0 1.1 collective-permute-start.22
  180.7 2.2 %collective-permute-start.21 = (bf16[2,80,512]{2,1,0:T(8,128)(2,1)S(1)}, bf16[2,80,512]{2,1,0:T(8,128)(2,1)S(1)}, u32[]{:S(2)}, u32[]{:S(2)}) collective-permute-start(bf16[2,80,512]{2,1,0:T(8,128)(2,1)S(1)} %add_convert_fusion.11), channel_id=1, source_target_pairs={{0,24},{4,28},{8,16},{12,20},{16,8},{20,12},{24,0},{28,4},{32,56},... | collective-permute-start | bytes 491528 | tf_op jit(solution)/shard_map/ppermute | solution.py:274
  182.9 2.6 %collective-permute-done.23 = bf16[2,80,1024]{2,1,0:T(8,128)(2,1)S(1)} collective-permute-done((bf16[2,80,1024]{2,1,0:T(8,128)(2,1)S(1)}, bf16[2,80,1024]{2,1,0:T(8,128)(2,1)S(1)}, u32[]{:S(2)}, u32[]{:S(2)}) %collective-permute-start.23) | collective-permute-done | bytes 327712 | tf_op jit(solution)/shard_map/ppermute | solution.py:274
  186.1 0.9 collective-permute-start.24
  188.0 1.4 collective-permute-start.25
  189.7 1.3 collective-permute-start.26
  191.0 1.7 shard_map.95
  192.7 1.1 broadcast_select_fusion
  195.0 0.8 slice_bitcast_fusion
  (124 shorter events, 21.3 us)
Async XLA Ops:
  0.6 22.7 %copy-start = (bf16[2,64,2560]{2,1,0:T(8,128)(2,1)S(1)}, bf16[2,64,2560]{2,1,0:T(8,128)(2,1)}, u32[]{:S(2)}) copy-start(bf16[2,64,2560]{2,1,0:T(8,128)(2,1)} %param.7) | copy-start | bytes 1966084
  0.6 16.5 %copy-start.2 = (bf16[1,2,192,1280]{3,2,1,0:T(8,128)(2,1)S(1)}, bf16[1,2,192,1280]{3,2,1,0:T(8,128)(2,1)}, u32[]{:S(2)}) copy-start(bf16[1,2,192,1280]{3,2,1,0:T(8,128)(2,1)} %param.10) | copy-start | bytes 2949124
  0.7 16.4 %copy-start.3 = (f32[1,1280]{1,0:T(1,128)S(1)}, f32[1,1280]{1,0:T(1,128)}, u32[]{:S(2)}) copy-start(f32[1,1280]{1,0:T(1,128)} %gain_ref.1) | copy-start | bytes 15364
  4.5 17.5 %all-to-all-start = ((s32[32,1,2]{2,1,0:T(1,128)}), s32[32,1,2]{2,1,0:T(1,128)S(1)}, u32[]{:S(2)}, u32[]{:S(2)}) async-start(s32[32,1,2]{2,1,0:T(1,128)} %copy.25), calls=%async_computation | async-start | bytes 32768 | tf_op jit(solution)/shard_map/all_to_all | solution.py:105
  17.6 19.5 %copy-start.5 = (bf16[384,1280]{1,0:T(8,128)(2,1)}, bf16[384,1280]{1,0:T(8,128)(2,1)S(1)}, u32[]{:S(2)}) copy-start(bf16[384,1280]{1,0:T(8,128)(2,1)S(1)} %multiply_convert_fusion.1) | copy-start | bytes 2949124
  24.5 13.7 %all-to-all-start.1 = ((bf16[32,2,2560]{2,1,0:T(2,128)(2,1)}), bf16[32,2,2560]{2,1,0:T(2,128)(2,1)S(1)}, u32[]{:S(2)}, u32[]{:S(2)}) async-start(bf16[32,2,2560]{2,1,0:T(2,128)(2,1)} %all_to_all.16), calls=%async_computation.1 | async-start | bytes 655360 | tf_op jit(solution)/shard_map/all_to_all | solution.py:114
  38.3 6.0 %collective-permute-start.2 = (bf16[64,2560]{1,0:T(8,128)(2,1)S(1)}, bf16[64,2560]{1,0:T(8,128)(2,1)S(1)}, u32[]{:S(2)}, u32[]{:S(2)}) collective-permute-start(bf16[64,2560]{1,0:T(8,128)(2,1)S(1)} %all_to_all.18), channel_id=1, source_target_pairs={{2,3},{3,2},{6,7},{7,6},{10,11},{11,10},{14,15},{15,14},{18,19},{1... | collective-permute-start | bytes 983048 | tf_op jit(solution)/shard_map/ppermute | solution.py:118
  39.0 9.0 %collective-permute-start.1 = (bf16[64,2560]{1,0:T(8,128)(2,1)S(1)}, bf16[64,2560]{1,0:T(8,128)(2,1)S(1)}, u32[]{:S(2)}, u32[]{:S(2)}) collective-permute-start(bf16[64,2560]{1,0:T(8,128)(2,1)S(1)} %all_to_all.18), channel_id=1, source_target_pairs={{0,3},{1,2},{4,7},{5,6},{8,11},{9,10},{12,15},{13,14},{16,19},{17,... | collective-permute-start | bytes 983048 | tf_op jit(solution)/shard_map/ppermute | solution.py:117
  43.0 5.4 %collective-permute-start = (bf16[64,2560]{1,0:T(8,128)(2,1)S(1)}, bf16[64,2560]{1,0:T(8,128)(2,1)S(1)}, u32[]{:S(2)}, u32[]{:S(2)}) collective-permute-start(bf16[64,2560]{1,0:T(8,128)(2,1)S(1)} %all_to_all.18), channel_id=1, source_target_pairs={{0,2},{1,3},{4,6},{5,7},{8,10},{9,11},{12,14},{13,15},{16,18},{17,... | collective-permute-start | bytes 983048 | tf_op jit(solution)/shard_map/ppermute | solution.py:116
  48.4 1.5 copy-start.6
  48.8 7.1 %slice-start.2 = ((s8[6553600]{0:T(1024)(128)(4,1)}), s8[4194304]{0:T(1024)(128)(4,1)S(1)}, s32[]{:S(2)}) async-start(s8[6553600]{0:T(1024)(128)(4,1)} %bitcast.159), calls=%async_computation.4 | async-start | bytes 8388608
  50.0 5.9 %slice-start.3 = ((s8[6553600]{0:T(1024)(128)(4,1)}), s8[2359296]{0:T(1024)(128)(4,1)S(1)}, s32[]{:S(2)}) async-start(s8[6553600]{0:T(1024)(128)(4,1)} %bitcast.159), calls=%async_computation.5 | async-start | bytes 4718592
  63.8 9.2 %collective-permute-start.3 = (bf16[1200,1280]{1,0:T(8,128)(2,1)}, bf16[1200,1280]{1,0:T(8,128)(2,1)}, u32[]{:S(2)}, u32[]{:S(2)}) collective-permute-start(bf16[1200,1280]{1,0:T(8,128)(2,1)} %constant_dynamic-update-slice_fusion), channel_id=1, source_target_pairs={{2,0},{3,1},{6,4},{7,5},{10,8},{11,9},{14,12},{15,13},{18,16},{19,... | collective-permute-start | bytes 9216008 | tf_op jit(solution)/shard_map/ppermute | solution.py:335
  65.4 18.3 %collective-permute-start.4 = (bf16[384,1280]{1,0:T(8,128)(2,1)}, bf16[384,1280]{1,0:T(8,128)(2,1)S(1)}, u32[]{:S(2)}, u32[]{:S(2)}) collective-permute-start(bf16[384,1280]{1,0:T(8,128)(2,1)} %get-tuple-element.93), channel_id=1, source_target_pairs={{2,1},{3,0},{6,5},{7,4},{10,9},{11,8},{14,13},{15,12},{18,17},{19,... | collective-permute-start | bytes 2949128 | tf_op jit(solution)/shard_map/ppermute | solution.py:326
  73.8 11.8 %slice-start = ((s8[6553600]{0:T(1024)(128)(4,1)}), s8[4194304]{0:T(1024)(128)(4,1)S(1)}, s32[]{:S(2)}) async-start(s8[6553600]{0:T(1024)(128)(4,1)} %bitcast.157), calls=%async_computation.2 | async-start | bytes 8388608
  83.7 1.9 slice-start.1
  85.5 1.5 copy-start.7
  92.8 1.5 copy-start.4
  95.6 30.4 %collective-permute-start.11 = (bf16[2,640,512]{2,1,0:T(8,128)(2,1)S(1)}, bf16[2,640,512]{2,1,0:T(8,128)(2,1)S(1)}, u32[]{:S(2)}, u32[]{:S(2)}) collective-permute-start(bf16[2,640,512]{2,1,0:T(8,128)(2,1)S(1)} %convolution_convert_fusion.3), channel_id=1, source_target_pairs={{0,96},{4,100},{8,104},{12,108},{16,112},{20,116},{24,120},{28,124... | collective-permute-start | bytes 3932168 | tf_op jit(solution)/shard_map/ppermute | solution.py:274
  99.2 30.3 %collective-permute-start.10 = (bf16[2,640,512]{2,1,0:T(8,128)(2,1)S(1)}, bf16[2,640,512]{2,1,0:T(8,128)(2,1)S(1)}, u32[]{:S(2)}, u32[]{:S(2)}) collective-permute-start(bf16[2,640,512]{2,1,0:T(8,128)(2,1)S(1)} %convolution_convert_fusion.4), channel_id=1, source_target_pairs={{0,32},{4,36},{8,40},{12,44},{16,48},{20,52},{24,56},{28,60},{32,0... | collective-permute-start | bytes 3932168 | tf_op jit(solution)/shard_map/ppermute | solution.py:274
  100.4 30.0 %collective-permute-start.9 = (bf16[2,640,512]{2,1,0:T(8,128)(2,1)S(1)}, bf16[2,640,512]{2,1,0:T(8,128)(2,1)S(1)}, u32[]{:S(2)}, u32[]{:S(2)}) collective-permute-start(bf16[2,640,512]{2,1,0:T(8,128)(2,1)S(1)} %convolution_convert_fusion.5), channel_id=1, source_target_pairs={{0,24},{4,28},{8,16},{12,20},{16,8},{20,12},{24,0},{28,4},{32,56},... | collective-permute-start | bytes 3932168 | tf_op jit(solution)/shard_map/ppermute | solution.py:274
  104.0 28.5 %collective-permute-start.8 = (bf16[2,640,512]{2,1,0:T(8,128)(2,1)S(1)}, bf16[2,640,512]{2,1,0:T(8,128)(2,1)S(1)}, u32[]{:S(2)}, u32[]{:S(2)}) collective-permute-start(bf16[2,640,512]{2,1,0:T(8,128)(2,1)S(1)} %convolution_convert_fusion.6), channel_id=1, source_target_pairs={{0,8},{4,12},{8,0},{12,4},{16,24},{20,28},{24,16},{28,20},{32,40},... | collective-permute-start | bytes 3932168 | tf_op jit(solution)/shard_map/ppermute | solution.py:274
  105.6 39.5 %collective-permute-start.7 = (bf16[2,640,512]{2,1,0:T(8,128)(2,1)S(1)}, bf16[2,640,512]{2,1,0:T(8,128)(2,1)S(1)}, u32[]{:S(2)}, u32[]{:S(2)}) collective-permute-start(bf16[2,640,512]{2,1,0:T(8,128)(2,1)S(1)} %convolution_convert_fusion.7), channel_id=1, source_target_pairs={{0,4},{4,0},{8,12},{12,8},{16,20},{20,16},{24,28},{28,24},{32,36},... | collective-permute-start | bytes 3932168 | tf_op jit(solution)/shard_map/ppermute | solution.py:274
  126.5 22.7 %collective-permute-start.15 = (bf16[2,320,512]{2,1,0:T(8,128)(2,1)S(1)}, bf16[2,320,512]{2,1,0:T(8,128)(2,1)S(1)}, u32[]{:S(2)}, u32[]{:S(2)}) collective-permute-start(bf16[2,320,512]{2,1,0:T(8,128)(2,1)S(1)} %add_convert_fusion.5), channel_id=1, source_target_pairs={{0,32},{4,36},{8,40},{12,44},{16,48},{20,52},{24,56},{28,60},{32,0... | collective-permute-start | bytes 1966088 | tf_op jit(solution)/shard_map/ppermute | solution.py:274
  133.0 15.1 %collective-permute-start.16 = (bf16[2,320,512]{2,1,0:T(8,128)(2,1)S(1)}, bf16[2,320,512]{2,1,0:T(8,128)(2,1)S(1)}, u32[]{:S(2)}, u32[]{:S(2)}) collective-permute-start(bf16[2,320,512]{2,1,0:T(8,128)(2,1)S(1)} %add_convert_fusion.2), channel_id=1, source_target_pairs={{0,4},{4,0},{8,12},{12,8},{16,20},{20,16},{24,28},{28,24},{32,36},... | collective-permute-start | bytes 1966088 | tf_op jit(solution)/shard_map/ppermute | solution.py:274
  139.5 51.4 %collective-permute-start.5 = (bf16[384,1280]{1,0:T(8,128)(2,1)S(1)}, bf16[384,1280]{1,0:T(8,128)(2,1)S(1)}, u32[]{:S(2)}, u32[]{:S(2)}) collective-permute-start(bf16[384,1280]{1,0:T(8,128)(2,1)S(1)} %fusion.29.mine_ref), channel_id=1, source_target_pairs={{0,1},{1,0},{4,5},{5,4},{8,9},{9,8},{12,13},{13,12},{16,17},{17,16... | collective-permute-start | bytes 2949128 | tf_op jit(solution)/shard_map/ppermute | solution.py:354
  143.5 47.5 %collective-permute-start.6 = (bf16[384,1280]{1,0:T(8,128)(2,1)S(1)}, bf16[384,1280]{1,0:T(8,128)(2,1)S(1)}, u32[]{:S(2)}, u32[]{:S(2)}) collective-permute-start(bf16[384,1280]{1,0:T(8,128)(2,1)S(1)} %shard_map.94), channel_id=1, source_target_pairs={{0,2},{1,3},{4,6},{5,7},{8,10},{9,11},{12,14},{13,15},{16,18},{17,... | collective-permute-start | bytes 2949128 | tf_op jit(solution)/shard_map/ppermute | solution.py:355
  145.1 19.9 %collective-permute-start.13 = (bf16[2,320,512]{2,1,0:T(8,128)(2,1)S(1)}, bf16[2,320,512]{2,1,0:T(8,128)(2,1)S(1)}, u32[]{:S(2)}, u32[]{:S(2)}) collective-permute-start(bf16[2,320,512]{2,1,0:T(8,128)(2,1)S(1)} %add_convert_fusion.3), channel_id=1, source_target_pairs={{0,8},{4,12},{8,0},{12,4},{16,24},{20,28},{24,16},{28,20},{32,40},... | collective-permute-start | bytes 1966088 | tf_op jit(solution)/shard_map/ppermute | solution.py:274
  148.1 15.4 %collective-permute-start.14 = (bf16[2,320,512]{2,1,0:T(8,128)(2,1)S(1)}, bf16[2,320,512]{2,1,0:T(8,128)(2,1)S(1)}, u32[]{:S(2)}, u32[]{:S(2)}) collective-permute-start(bf16[2,320,512]{2,1,0:T(8,128)(2,1)S(1)} %add_convert_fusion.4), channel_id=1, source_target_pairs={{0,24},{4,28},{8,16},{12,20},{16,8},{20,12},{24,0},{28,4},{32,56},... | collective-permute-start | bytes 1966088 | tf_op jit(solution)/shard_map/ppermute | solution.py:274
  149.2 17.2 %collective-permute-start.12 = (bf16[2,320,512]{2,1,0:T(8,128)(2,1)S(1)}, bf16[2,320,512]{2,1,0:T(8,128)(2,1)S(1)}, u32[]{:S(2)}, u32[]{:S(2)}) collective-permute-start(bf16[2,320,512]{2,1,0:T(8,128)(2,1)S(1)} %add_convert_fusion.1), channel_id=1, source_target_pairs={{0,96},{4,100},{8,104},{12,108},{16,112},{20,116},{24,120},{28,124... | collective-permute-start | bytes 1966088 | tf_op jit(solution)/shard_map/ppermute | solution.py:274
  163.5 14.4 %collective-permute-start.19 = (bf16[2,160,1024]{2,1,0:T(8,128)(2,1)S(1)}, bf16[2,160,1024]{2,1,0:T(8,128)(2,1)S(1)}, u32[]{:S(2)}, u32[]{:S(2)}) collective-permute-start(bf16[2,160,1024]{2,1,0:T(8,128)(2,1)S(1)} %pad_maximum_fusion.2), channel_id=1, source_target_pairs={{0,24},{4,28},{8,16},{12,20},{16,8},{20,12},{24,0},{28,4},{32,56},... | collective-permute-start | bytes 1966088 | tf_op jit(solution)/shard_map/ppermute | solution.py:274
  165.0 8.4 %collective-permute-start.20 = (bf16[2,160,512]{2,1,0:T(8,128)(2,1)S(1)}, bf16[2,160,512]{2,1,0:T(8,128)(2,1)S(1)}, u32[]{:S(2)}, u32[]{:S(2)}) collective-permute-start(bf16[2,160,512]{2,1,0:T(8,128)(2,1)S(1)} %add_convert_fusion.8), channel_id=1, source_target_pairs={{0,96},{4,100},{8,104},{12,108},{16,112},{20,116},{24,120},{28,124... | collective-permute-start | bytes 983048 | tf_op jit(solution)/shard_map/ppermute | solution.py:274
  166.5 11.9 %collective-permute-start.18 = (bf16[2,160,512]{2,1,0:T(8,128)(2,1)S(1)}, bf16[2,160,512]{2,1,0:T(8,128)(2,1)S(1)}, u32[]{:S(2)}, u32[]{:S(2)}) collective-permute-start(bf16[2,160,512]{2,1,0:T(8,128)(2,1)S(1)} %add_convert_fusion.7), channel_id=1, source_target_pairs={{0,4},{4,0},{8,12},{12,8},{16,20},{20,16},{24,28},{28,24},{32,36},... | collective-permute-start | bytes 983048 | tf_op jit(solution)/shard_map/ppermute | solution.py:274
  173.3 7.1 %collective-permute-start.17 = (bf16[2,160,512]{2,1,0:T(8,128)(2,1)S(1)}, bf16[2,160,512]{2,1,0:T(8,128)(2,1)S(1)}, u32[]{:S(2)}, u32[]{:S(2)}) collective-permute-start(bf16[2,160,512]{2,1,0:T(8,128)(2,1)S(1)} %add_convert_fusion.6), channel_id=1, source_target_pairs={{0,32},{4,36},{8,40},{12,44},{16,48},{20,52},{24,56},{28,60},{32,0... | collective-permute-start | bytes 983048 | tf_op jit(solution)/shard_map/ppermute | solution.py:274
  178.3 7.2 %collective-permute-start.23 = (bf16[2,80,1024]{2,1,0:T(8,128)(2,1)S(1)}, bf16[2,80,1024]{2,1,0:T(8,128)(2,1)S(1)}, u32[]{:S(2)}, u32[]{:S(2)}) collective-permute-start(bf16[2,80,1024]{2,1,0:T(8,128)(2,1)S(1)} %pad_maximum_fusion.3), channel_id=1, source_target_pairs={{0,8},{4,12},{8,0},{12,4},{16,24},{20,28},{24,16},{28,20},{32,40},... | collective-permute-start | bytes 983048 | tf_op jit(solution)/shard_map/ppermute | solution.py:274
  179.0 8.4 %collective-permute-start.22 = (bf16[2,80,1024]{2,1,0:T(8,128)(2,1)S(1)}, bf16[2,80,1024]{2,1,0:T(8,128)(2,1)S(1)}, u32[]{:S(2)}, u32[]{:S(2)}) collective-permute-start(bf16[2,80,1024]{2,1,0:T(8,128)(2,1)S(1)} %pad_maximum_fusion.4), channel_id=1, source_target_pairs={{0,96},{4,100},{8,104},{12,108},{16,112},{20,116},{24,120},{28,124... | collective-permute-start | bytes 983048 | tf_op jit(solution)/shard_map/ppermute | solution.py:274
  180.7 8.7 %collective-permute-start.21 = (bf16[2,80,512]{2,1,0:T(8,128)(2,1)S(1)}, bf16[2,80,512]{2,1,0:T(8,128)(2,1)S(1)}, u32[]{:S(2)}, u32[]{:S(2)}) collective-permute-start(bf16[2,80,512]{2,1,0:T(8,128)(2,1)S(1)} %add_convert_fusion.11), channel_id=1, source_target_pairs={{0,24},{4,28},{8,16},{12,20},{16,8},{20,12},{24,0},{28,4},{32,56},... | collective-permute-start | bytes 491528 | tf_op jit(solution)/shard_map/ppermute | solution.py:274
  186.1 7.7 %collective-permute-start.24 = (bf16[2,40,1024]{2,1,0:T(8,128)(2,1)S(1)}, bf16[2,40,1024]{2,1,0:T(8,128)(2,1)S(1)}, u32[]{:S(2)}, u32[]{:S(2)}) collective-permute-start(bf16[2,40,1024]{2,1,0:T(8,128)(2,1)S(1)} %pad_maximum_fusion.5), channel_id=1, source_target_pairs={{0,4},{4,0},{8,12},{12,8},{16,20},{20,16},{24,28},{28,24},{32,36},... | collective-permute-start | bytes 491528 | tf_op jit(solution)/shard_map/ppermute | solution.py:274
  188.0 6.4 %collective-permute-start.25 = (bf16[2,40,1024]{2,1,0:T(8,128)(2,1)S(1)}, bf16[2,40,1024]{2,1,0:T(8,128)(2,1)S(1)}, u32[]{:S(2)}, u32[]{:S(2)}) collective-permute-start(bf16[2,40,1024]{2,1,0:T(8,128)(2,1)S(1)} %pad_maximum_fusion.6), channel_id=1, source_target_pairs={{0,32},{4,36},{8,40},{12,44},{16,48},{20,52},{24,56},{28,60},{32,0... | collective-permute-start | bytes 491528 | tf_op jit(solution)/shard_map/ppermute | solution.py:274
  189.7 5.2 %collective-permute-start.26 = (bf16[2,40,512]{2,1,0:T(8,128)(2,1)S(1)}, bf16[2,40,512]{2,1,0:T(8,128)(2,1)S(1)}, u32[]{:S(2)}, u32[]{:S(2)}) collective-permute-start(bf16[2,40,512]{2,1,0:T(8,128)(2,1)S(1)} %add_convert_fusion.21), channel_id=1, source_target_pairs={{0,8},{4,12},{8,0},{12,4},{16,24},{20,28},{24,16},{28,20},{32,40},... | collective-permute-start | bytes 245768 | tf_op jit(solution)/shard_map/ppermute | solution.py:274
  194.1 1.7 copy-start.1
where the time goes:
time: 197 us; the launch traced here: 196 us
  waiting for transfers between devices  70.8 us (36%)
  starting transfers between devices  49.5 us (25%)
  matrix products  45.4 us (23%)
  local copies, waits for them, and re-layouts  15.7 us (8%)
  other arithmetic  9.54 us (5%)
  Pallas kernels  3.49 us (2%)
    ppermute x20, waiting for transfers between devices, reduce_weight_grads(): piece = lax.ppermute(last, 'dp', neighbour_pairs(ORDERS[streams[0]][t]))  50.8 us
    dot_general x10, matrix products, dot(): lax.dot_general(a, b, (((ca,), (cb,)), ((), ())), preferred_element_type=...  32.9 us
    ppermute x20, starting transfers between devices, reduce_weight_grads(): piece = lax.ppermute(last, 'dp', neighbour_pairs(ORDERS[streams[0]][t]))  22.3 us
    dot_general x30, matrix products, group(): lax.dot_general(lefts[i][:, lo:hi], right[:, :, i * span:(i + 1) * span],...  12.5 us
    all_to_all x1, starting transfers between devices, ask_tokens(): return lax.all_to_all(requests, 'dp', 0, 0, tiled=True).reshape(-1)  9.34 us
    ppermute x1, waiting for transfers between devices, per_device(): other = lax.ppermute(partial, both, [(2, 1), (3, 0)])  7.76 us
    unnamed x28, local copies, waits for them, and re-layouts  7.18 us
    all_to_all x1, waiting for transfers between devices, ask_tokens(): return lax.all_to_all(requests, 'dp', 0, 0, tiled=True).reshape(-1)  4.45 us
  transfers between devices with their start and end apart: 29, of which 16 were waited for; matrix products, arithmetic and copies ran while one was open for 19% of the time, Pallas kernels for 1%

commit v1 on v0

--- a/solution.py
+++ b/solution.py
@@ -144,7 +144,7 @@
     return lax.optimization_barrier((value, others))[0]
 
 
-def reduce_weight_grads(left, right, between):
+def reduce_weight_grads(left, right, first, second):
     width = left.shape[1]
     span = right.shape[2] // BITS
     lefts = [reordered(left, i) for i in range(BITS)]
@@ -161,21 +161,27 @@
             total = total + piece[:, lo:hi].astype(jnp.float32)
         return total.astype(jnp.bfloat16)
 
-    last = None
+    last, turns = None, {}
     for t in range(BITS):
-        for streams in SHARED[t]:
+        for place, streams in enumerate(SHARED[t]):
+            if t == 0 and last is not None:
+                lefts[place] = after(lefts[place], last)
             if t:
                 for i in streams:
-                    received[i][-1] = after(received[i][-1], last)
+                    received[i][-1] = after(received[i][-1], last, turns.get((t, place)))
             sends = [group(i, width >> (t + 1), width >> t) for i in streams]
             last = sends[0] if len(sends) == 1 else jnp.concatenate(sends, axis=2)
             piece = lax.ppermute(last, "dp", neighbour_pairs(ORDERS[streams[0]][t]))
             for k, i in enumerate(streams):
                 received[i].append(piece[:, :, k * span : (k + 1) * span])
         if t == 0:
-            middle = between(last)
+            middle = first(last)
+            turns[1, 0] = middle
+        if t == 2:
+            end = second(middle, last)
+            turns[4, 0] = end[0]
     result = jnp.concatenate([group(i, 0, width >> BITS) for i in range(BITS)], axis=2)
-    return result, after(middle, last)
+    return result, middle, after(end, last)
 
 
 def per_device(llm_grad, slots, frames, saved_in, ln_gain, w_in, w_out):
@@ -246,7 +252,7 @@
     return lax.optimization_barrier((value, others))[0]
 
 
-def reduce_weight_grads(left, right, between):
+def reduce_weight_grads(left, right, first, second):
     width = left.shape[1]
     span = right.shape[2] // BITS
     lefts = [reordered(left, i) for i in range(BITS)]
@@ -263,21 +269,27 @@
             total = total + piece[:, lo:hi].astype(jnp.float32)
         return total.astype(jnp.bfloat16)
 
-    last = None
+    last, turns = None, {}
     for t in range(BITS):
-        for streams in SHARED[t]:
+        for place, streams in enumerate(SHARED[t]):
+            if t == 0 and last is not None:
+                lefts[place] = after(lefts[place], last)
             if t:
                 for i in streams:
-                    received[i][-1] = after(received[i][-1], last)
+                    received[i][-1] = after(received[i][-1], last, turns.get((t, place)))
             sends = [group(i, width >> (t + 1), width >> t) for i in streams]
             last = sends[0] if len(sends) == 1 else jnp.concatenate(sends, axis=2)
             piece = lax.ppermute(last, "dp", neighbour_pairs(ORDERS[streams[0]][t]))
             for k, i in enumerate(streams):
                 received[i].append(piece[:, :, k * span : (k + 1) * span])
         if t == 0:
-            middle = between(last)
+            middle = first(last)
+            turns[1, 0] = middle
+        if t == 2:
+            end = second(middle, last)
+            turns[4, 0] = end[0]
     result = jnp.concatenate([group(i, 0, width >> BITS) for i in range(BITS)], axis=2)
-    return result, after(middle, last)
+    return result, middle, after(end, last)
 
 
 def per_device(llm_grad, slots, frames, saved_in, ln_gain, w_in, w_out):
@@ -327,11 +339,10 @@
     terms, rest = [], ln_gain
     for _ in range(3):
         term = lax.reduce_precision(rest, exponent_bits=8, mantissa_bits=7)
-        terms.append(term.astype(jnp.bfloat16))
+        terms.append(jnp.broadcast_to(term, (16, width)).astype(jnp.bfloat16))
         rest = rest - term
-    packed = jnp.concatenate(
-        [partial, upstream, x] + [jnp.broadcast_to(term, (16, width)) for term in terms]
-    )
+    terms = after(jnp.concatenate(terms), normed)
+    packed = jnp.concatenate([partial, upstream, x, terms])
     packed = lax.ppermute(packed, "section", [(1, 0)])
     mine, passed, later_x = (packed[k * rows : (k + 1) * rows] for k in range(3))
     later_gain = sum(
@@ -347,16 +358,14 @@
     def partial_here(last):
         return dot(after(d_pre, last), weight_in, 1, 1).astype(jnp.bfloat16)
 
-    def exchange(last):
-        partial = partial_here(last)
+    def exchange(partial, last):
         return (
-            partial,
-            lax.ppermute(partial, both, [(0, 1), (1, 0)]),
+            lax.ppermute(after(partial, last), both, [(0, 1), (1, 0)]),
             lax.ppermute(after(grad_last, last), "section", [(0, 1)]),
         )
 
-    reduced, (partial, other, returned) = reduce_weight_grads(
-        jnp.stack([normed_t, incoming_t]), jnp.stack([d_pre, activ]), exchange
+    reduced, partial, (other, returned) = reduce_weight_grads(
+        jnp.stack([normed_t, incoming_t]), jnp.stack([d_pre, activ]), partial_here, exchange
     )
     grad_here = finish(incoming, partial, other, x, ln_gain, tok_rows // 2)
     results = jnp.where(sec == 1, returned, grad_here)

time: 197 us -> 189 us (0.959)
  waiting for transfers between devices: 70.8 us -> 61.5 us
  local copies, waits for them, and re-layouts: 15.7 us -> 11.8 us
  starting transfers between devices: 49.5 us -> 52.7 us
    ppermute x20, waiting for transfers between devices: 50.8 us -> 37 us  [reduce_weight_grads(): piece = lax.ppermute(last, 'dp', neighbour_pairs(ORDERS[streams[0]][t]))]
    ppermute x1, waiting for transfers between devices: 0.01 us -> 4.5 us  [exchange(): lax.ppermute(after(partial, last), both, [(0, 1), (1, 0)])]
    ppermute x20, starting transfers between devices: 22.3 us -> 25.8 us  [reduce_weight_grads(): piece = lax.ppermute(last, 'dp', neighbour_pairs(ORDERS[streams[0]][t]))]
    unnamed x28 -> x26, local copies, waits for them, and re-layouts: 7.18 us -> 3.89 us
    dot_general x30, matrix products: 12.5 us -> 14.6 us  [group(): lax.dot_general(lefts[i][:, lo:hi], right[:, :, i * span:(i + 1) * span],...]
  transfers between devices with their start and end apart: 29 -> 29, of which waited for: 16 -> 16; matrix products, arithmetic and copies ran while one was open for 19% -> 21% of each run, Pallas kernels for 1% -> 1%
where the time goes in v1:
time: 189 us
  waiting for transfers between devices  61.5 us (33%)
  starting transfers between devices  52.7 us (28%)
  matrix products  46.2 us (24%)
  local copies, waits for them, and re-layouts  11.8 us (6%)
  other arithmetic  11.5 us (6%)
  Pallas kernels  3.49 us (2%)
    ppermute x20, waiting for transfers between devices, reduce_weight_grads(): piece = lax.ppermute(last, 'dp', neighbour_pairs(ORDERS[streams[0]][t]))  37 us
    dot_general x10, matrix products, dot(): lax.dot_general(a, b, (((ca,), (cb,)), ((), ())), preferred_element_type=...  31.6 us
    ppermute x20, starting transfers between devices, reduce_weight_grads(): piece = lax.ppermute(last, 'dp', neighbour_pairs(ORDERS[streams[0]][t]))  25.8 us
    dot_general x30, matrix products, group(): lax.dot_general(lefts[i][:, lo:hi], right[:, :, i * span:(i + 1) * span],...  14.6 us
    all_to_all x1, starting transfers between devices, ask_tokens(): return lax.all_to_all(requests, 'dp', 0, 0, tiled=True).reshape(-1)  9.34 us
    ppermute x1, waiting for transfers between devices, per_device(): other = lax.ppermute(partial, both, [(2, 1), (3, 0)])  7.76 us
    ppermute x1, waiting for transfers between devices, exchange(): lax.ppermute(after(partial, last), both, [(0, 1), (1, 0)])  4.5 us
    all_to_all x1, waiting for transfers between devices, ask_tokens(): return lax.all_to_all(requests, 'dp', 0, 0, tiled=True).reshape(-1)  4.39 us
  transfers between devices with their start and end apart: 29, of which 16 were waited for; matrix products, arithmetic and copies ran while one was open for 21% of the time, Pallas kernels for 1%

profile of v1, /device:TPU:0, one launch (start us, length us, event | category | flops | bytes accessed | tf_op | source)
XLA Modules:
  0.0 188.6 jit_solution(15708705020692893647)
XLA Ops:
  0.7 0.9 reduce_sum.38
  4.5 9.3 %all-to-all-start = ((s32[32,1,2]{2,1,0:T(1,128)}), s32[32,1,2]{2,1,0:T(1,128)S(1)}, u32[]{:S(2)}, u32[]{:S(2)}) async-start(s32[32,1,2]{2,1,0:T(1,128)} %copy.25), calls=%async_computation | async-start | bytes 32768 | tf_op jit(solution)/shard_map/all_to_all | solution.py:105
  13.9 1.4 convert_reduce_fusion
  15.3 1.6 fusion.33
  17.6 4.4 %all-to-all-done = s32[32,1,2]{2,1,0:T(1,128)S(1)} async-done(((s32[32,1,2]{2,1,0:T(1,128)}), s32[32,1,2]{2,1,0:T(1,128)S(1)}, u32[]{:S(2)}, u32[]{:S(2)}) %all-to-all-start) | async-done | bytes 288 | tf_op jit(solution)/shard_map/all_to_all | solution.py:105
  23.6 0.9 all_to_all.16
  24.5 4.0 %all-to-all-start.1 = ((bf16[32,2,2560]{2,1,0:T(2,128)(2,1)}), bf16[32,2,2560]{2,1,0:T(2,128)(2,1)S(1)}, u32[]{:S(2)}, u32[]{:S(2)}) async-start(bf16[32,2,2560]{2,1,0:T(2,128)(2,1)} %all_to_all.16), calls=%async_computation.1 | async-start | bytes 655360 | tf_op jit(solution)/shard_map/all_to_all | solution.py:114
  28.5 8.7 %add_convert_fusion = (bf16[384,2560]{1,0:T(8,128)(2,1)}, bf16[384,2560]{1,0:T(8,128)(2,1)}) fusion(bf16[384,1280]{1,0:T(8,128)(2,1)S(1)} %multiply_convert_fusion.1, bf16[1,1280,2560]{2,1,0:T(8,128)(2,1)} %param.12), kind=kOutput, calls=%fused_computation.25 | convolution fusion | flops 2534277120 | bytes 11468800 | tf_op jit(solution)/shard_map/dot_general | solution.py:56
  37.2 1.1 all-to-all-done.1
  39.0 4.0 %collective-permute-start.1 = (bf16[64,2560]{1,0:T(8,128)(2,1)S(1)}, bf16[64,2560]{1,0:T(8,128)(2,1)S(1)}, u32[]{:S(2)}, u32[]{:S(2)}) collective-permute-start(bf16[64,2560]{1,0:T(8,128)(2,1)S(1)} %all_to_all.18), channel_id=1, source_target_pairs={{0,3},{1,2},{4,7},{5,6},{8,11},{9,10},{12,15},{13,14},{16,19},{17,... | collective-permute-start | bytes 983048 | tf_op jit(solution)/shard_map/ppermute | solution.py:117
  43.0 1.3 collective-permute-start
  44.4 3.7 %collective-permute-done.1 = bf16[64,2560]{1,0:T(8,128)(2,1)S(1)} collective-permute-done((bf16[64,2560]{1,0:T(8,128)(2,1)S(1)}, bf16[64,2560]{1,0:T(8,128)(2,1)S(1)}, u32[]{:S(2)}, u32[]{:S(2)}) %collective-permute-start.1) | collective-permute-done | bytes 327712 | tf_op jit(solution)/shard_map/ppermute | solution.py:117
  48.9 1.1 copy-done.7
  50.0 5.9 %fusion.16 = bf16[384,2560]{1,0:T(8,128)(2,1)S(1)} fusion(bf16[384,2560]{1,0:T(8,128)(2,1)S(1)} %copy-done.7, bf16[384,1280]{1,0:T(8,128)(2,1)S(1)} %pad_maximum_fusion.1, bf16[1,2560,1280]{2,1,0:T(8,128)(2,1)} %param.13), kind=kOutput, calls=%fused_computation.23 | convolution fusion | flops 2519531520 | bytes 11468800 | tf_op jit(solution)/shard_map/dot_general | solution.py:56
  56.0 2.7 %fusion.26 = bf16[384,1280]{1,0:T(8,128)(2,1)S(1)} fusion(bf16[384,2560]{1,0:T(8,128)(2,1)S(1)} %fusion.16, bf16[1,1280,2560]{2,1,0:T(8,128)(2,1)S(1)} %bitcast.158), kind=kOutput, calls=%fused_computation.45 | convolution fusion | flops 2517073920 | bytes 9502720 | tf_op jit(solution)/shard_map/dot_general | solution.py:56
  58.7 1.9 %pad_maximum_fusion = bf16[1200,1280]{1,0:T(8,128)(2,1)} fusion(bf16[48,1280]{1,0:T(8,128)(2,1)S(1)} %pad_maximum_fusion.8, bf16[384,1280]{1,0:T(8,128)(2,1)S(1)} %bitcast.105, bf16[384,1280]{1,0:T(8,128)(2,1)S(1)} %pad_maximum_fusion.1, bf16[384,1280]{1,0:T(8,128)(2,1)S(1)} %fusion.26), kind=kLoop, calls=%fused_computation.32 | loop fusion | flops 12288000 | bytes 6144000 | tf_op jit(solution)/shard_map/concatenate | solution.py:345
  60.7 1.3 collective-permute-start.3
  62.2 1.5 collective-permute-start.4
  63.6 3.1 %fusion.24 = bf16[1280,384]{1,0:T(8,128)(2,1)S(1)} fusion(bf16[384,1280]{1,0:T(8,128)(2,1)} %copy-done.5, s32[1280]{0:T(1024)S(1)} %add.428), kind=kOutput, calls=%fused_computation.43 | convolution fusion | flops 1260421120 | bytes 1971200 | tf_op jit(solution)/shard_map/dot_general | solution.py:56
  66.8 3.1 %collective-permute-done.3 = bf16[1200,1280]{1,0:T(8,128)(2,1)} collective-permute-done((bf16[1200,1280]{1,0:T(8,128)(2,1)}, bf16[1200,1280]{1,0:T(8,128)(2,1)}, u32[]{:S(2)}, u32[]{:S(2)}) %collective-permute-start.3) | collective-permute-done | bytes 3072032 | tf_op jit(solution)/shard_map/ppermute | solution.py:346
  69.8 0.8 fusion.175.gain_ref
  70.6 2.1 %fusion.202 = (bf16[384,1280]{1,0:T(8,128)(2,1)S(1)}, bf16[384,1280]{1,0:T(8,128)(2,1)S(1)}, bf16[384,1280]{1,0:T(8,128)(2,1)S(1)}) fusion(bf16[1200,1280]{1,0:T(8,128)(2,1)} %collective-permute-done.3), kind=kLoop, calls=%fused_computation.259 | loop fusion | bytes 5898240 | tf_op jit(solution)/shard_map/slice | solution.py:347
  72.7 7.8 %collective-permute-done.4.other_ref = bf16[384,1280]{1,0:T(8,128)(2,1)S(1)} collective-permute-done((bf16[384,1280]{1,0:T(8,128)(2,1)}, bf16[384,1280]{1,0:T(8,128)(2,1)S(1)}, u32[]{:S(2)}, u32[]{:S(2)}) %collective-permute-start.4) | collective-permute-done | bytes 983072 | tf_op jit(solution)/shard_map/ppermute | solution.py:338
  80.5 1.7 shard_map.94
  82.4 1.4 copy-done.8
  83.8 2.7 %fusion.19 = bf16[384,2560]{1,0:T(8,128)(2,1)S(1)} fusion(bf16[384,2560]{1,0:T(8,128)(2,1)S(1)} %copy-done.8, bf16[384,1280]{1,0:T(8,128)(2,1)S(1)} %broadcast_select_fusion.1.g_ref, bf16[1,2560,1280]{2,1,0:T(8,128)(2,1)S(1)} %bitcast.156), kind=kOutput, calls=%fused_computation.24 | convolution fusion | flops 2519531520 | bytes 11468800 | tf_op jit(solution)/shard_map/dot_general | solution.py:56
  86.5 1.9 %fusion.25 = bf16[1280,384]{1,0:T(8,128)(2,1)S(1)} fusion(bf16[384,1280]{1,0:T(8,128)(2,1)S(1)} %broadcast_select_fusion.1.g_ref, s32[1280]{0:T(1024)S(1)} %add.428), kind=kOutput, calls=%fused_computation.44 | convolution fusion | flops 1260421120 | bytes 1971200 | tf_op jit(solution)/shard_map/dot_general | solution.py:56
  90.3 1.3 copy-done.4
  92.0 0.9 convolution_convert_fusion.7
  92.9 2.8 %collective-permute-start.9 = (bf16[2,640,512]{2,1,0:T(8,128)(2,1)S(1)}, bf16[2,640,512]{2,1,0:T(8,128)(2,1)S(1)}, u32[]{:S(2)}, u32[]{:S(2)}) collective-permute-start(bf16[2,640,512]{2,1,0:T(8,128)(2,1)S(1)} %convolution_convert_fusion.7), channel_id=1, source_target_pairs={{0,96},{4,100},{8,104},{12,108},{16,112},{20,116},{24,120},{28,124... | collective-permute-start | bytes 3932168 | tf_op jit(solution)/shard_map/ppermute | solution.py:282
  95.7 1.9 %convolution_convert_fusion.6 = bf16[2,640,512]{2,1,0:T(8,128)(2,1)} fusion(bf16[2,384,512]{2,1,0:T(8,128)(2,1)S(1)} %get-tuple-element.77, bf16[2,1280,384]{2,1,0:T(8,128)(2,1)S(1)} %bitcast.145), kind=kOutput, calls=%fused_computation.61 | convolution fusion | flops 503971840 | bytes 3080192 | tf_op jit(solution)/shard_map/dot_general | solution.py:262
  97.8 1.9 %convolution_convert_fusion.5 = bf16[2,640,512]{2,1,0:T(8,128)(2,1)} fusion(bf16[2,384,512]{2,1,0:T(8,128)(2,1)S(1)} %get-tuple-element.78, bf16[2,1280,384]{2,1,0:T(8,128)(2,1)S(1)} %bitcast.139), kind=kOutput, calls=%fused_computation.60 | convolution fusion | flops 503971840 | bytes 3080192 | tf_op jit(solution)/shard_map/dot_general | solution.py:262
  99.7 0.8 convolution_convert_fusion.4
  100.6 0.8 convolution_convert_fusion.3
  101.4 1.0 collective-permute-start.5
  102.4 1.5 collective-permute-start.6
  103.9 2.1 %collective-permute-start.7 = (bf16[2,640,512]{2,1,0:T(8,128)(2,1)}, bf16[2,640,512]{2,1,0:T(8,128)(2,1)S(1)}, u32[]{:S(2)}, u32[]{:S(2)}) collective-permute-start(bf16[2,640,512]{2,1,0:T(8,128)(2,1)} %convolution_convert_fusion.5), channel_id=1, source_target_pairs={{0,24},{4,28},{8,16},{12,20},{16,8},{20,12},{24,0},{28,4},{32,56},... | collective-permute-start | bytes 3932168 | tf_op jit(solution)/shard_map/ppermute | solution.py:282
  106.0 5.6 %fusion.29.mine_ref = bf16[384,1280]{1,0:T(8,128)(2,1)S(1)} fusion(bf16[384,2560]{1,0:T(8,128)(2,1)S(1)} %fusion.19, bf16[1,1280,2560]{2,1,0:T(8,128)(2,1)} %param.12), kind=kOutput, calls=%fused_computation.46 | convolution fusion | flops 2517073920 | bytes 9502720 | tf_op jit(solution)/shard_map/dot_general | solution.py:56
  111.6 11.7 %collective-permute-done.9 = bf16[2,640,512]{2,1,0:T(8,128)(2,1)S(1)} collective-permute-done((bf16[2,640,512]{2,1,0:T(8,128)(2,1)S(1)}, bf16[2,640,512]{2,1,0:T(8,128)(2,1)S(1)}, u32[]{:S(2)}, u32[]{:S(2)}) %collective-permute-start.9) | collective-permute-done | bytes 1310752 | tf_op jit(solution)/shard_map/ppermute | solution.py:282
  123.8 2.9 %collective-permute-done.8 = bf16[2,640,512]{2,1,0:T(8,128)(2,1)S(1)} collective-permute-done((bf16[2,640,512]{2,1,0:T(8,128)(2,1)}, bf16[2,640,512]{2,1,0:T(8,128)(2,1)S(1)}, u32[]{:S(2)}, u32[]{:S(2)}) %collective-permute-start.8) | collective-permute-done | bytes 1310752 | tf_op jit(solution)/shard_map/ppermute | solution.py:282
  127.2 6.2 %collective-permute-done.7 = bf16[2,640,512]{2,1,0:T(8,128)(2,1)S(1)} collective-permute-done((bf16[2,640,512]{2,1,0:T(8,128)(2,1)}, bf16[2,640,512]{2,1,0:T(8,128)(2,1)S(1)}, u32[]{:S(2)}, u32[]{:S(2)}) %collective-permute-start.7) | collective-permute-done | bytes 1310752 | tf_op jit(solution)/shard_map/ppermute | solution.py:282
  134.4 1.2 collective-permute-start.14
  135.6 1.7 collective-permute-start.13
  137.6 2.2 %collective-permute-start.12 = (bf16[2,320,512]{2,1,0:T(8,128)(2,1)S(1)}, bf16[2,320,512]{2,1,0:T(8,128)(2,1)S(1)}, u32[]{:S(2)}, u32[]{:S(2)}) collective-permute-start(bf16[2,320,512]{2,1,0:T(8,128)(2,1)S(1)} %add_convert_fusion.4), channel_id=1, source_target_pairs={{0,24},{4,28},{8,16},{12,20},{16,8},{20,12},{24,0},{28,4},{32,56},... | collective-permute-start | bytes 1966088 | tf_op jit(solution)/shard_map/ppermute | solution.py:282
  140.9 6.6 %collective-permute-done.14 = bf16[2,320,512]{2,1,0:T(8,128)(2,1)S(1)} collective-permute-done((bf16[2,320,512]{2,1,0:T(8,128)(2,1)S(1)}, bf16[2,320,512]{2,1,0:T(8,128)(2,1)S(1)}, u32[]{:S(2)}, u32[]{:S(2)}) %collective-permute-start.14) | collective-permute-done | bytes 655392 | tf_op jit(solution)/shard_map/ppermute | solution.py:282
  147.5 1.0 collective-permute-done.13
  149.2 2.2 %collective-permute-start.19 = (bf16[2,160,1024]{2,1,0:T(8,128)(2,1)S(1)}, bf16[2,160,1024]{2,1,0:T(8,128)(2,1)S(1)}, u32[]{:S(2)}, u32[]{:S(2)}) collective-permute-start(bf16[2,160,1024]{2,1,0:T(8,128)(2,1)S(1)} %pad_maximum_fusion.3), channel_id=1, source_target_pairs={{0,24},{4,28},{8,16},{12,20},{16,8},{20,12},{24,0},{28,4},{32,56},... | collective-permute-start | bytes 1966088 | tf_op jit(solution)/shard_map/ppermute | solution.py:282
  151.4 3.0 %collective-permute-done.12 = bf16[2,320,512]{2,1,0:T(8,128)(2,1)S(1)} collective-permute-done((bf16[2,320,512]{2,1,0:T(8,128)(2,1)S(1)}, bf16[2,320,512]{2,1,0:T(8,128)(2,1)S(1)}, u32[]{:S(2)}, u32[]{:S(2)}) %collective-permute-start.12) | collective-permute-done | bytes 655392 | tf_op jit(solution)/shard_map/ppermute | solution.py:282
  155.2 1.7 collective-permute-done.10
  157.4 0.9 collective-permute-start.18
  158.3 3.5 %collective-permute-start.15 = (bf16[384,1280]{1,0:T(8,128)(2,1)S(1)}, bf16[384,1280]{1,0:T(8,128)(2,1)S(1)}, u32[]{:S(2)}, u32[]{:S(2)}) collective-permute-start(bf16[384,1280]{1,0:T(8,128)(2,1)S(1)} %fusion.29.mine_ref), channel_id=1, source_target_pairs={{0,1},{1,0},{4,5},{5,4},{8,9},{9,8},{12,13},{13,12},{16,17},{17,16... | collective-permute-start | bytes 2949128 | tf_op jit(solution)/shard_map/ppermute | solution.py:363
  161.8 1.3 collective-permute-done.20
  163.1 1.3 collective-permute-start.16
  164.7 0.7 collective-permute-done.19
  165.8 1.2 collective-permute-start.23
  168.6 2.5 %collective-permute-start.21 = (bf16[2,80,512]{2,1,0:T(8,128)(2,1)S(1)}, bf16[2,80,512]{2,1,0:T(8,128)(2,1)S(1)}, u32[]{:S(2)}, u32[]{:S(2)}) collective-permute-start(bf16[2,80,512]{2,1,0:T(8,128)(2,1)S(1)} %add_convert_fusion.11), channel_id=1, source_target_pairs={{0,24},{4,28},{8,16},{12,20},{16,8},{20,12},{24,0},{28,4},{32,56},... | collective-permute-start | bytes 491528 | tf_op jit(solution)/shard_map/ppermute | solution.py:282
  171.0 2.0 %collective-permute-done.23 = bf16[2,80,1024]{2,1,0:T(8,128)(2,1)S(1)} collective-permute-done((bf16[2,80,1024]{2,1,0:T(8,128)(2,1)S(1)}, bf16[2,80,1024]{2,1,0:T(8,128)(2,1)S(1)}, u32[]{:S(2)}, u32[]{:S(2)}) %collective-permute-start.23) | collective-permute-done | bytes 327712 | tf_op jit(solution)/shard_map/ppermute | solution.py:282
  173.0 4.5 %collective-permute-done.15.other_ref = bf16[384,1280]{1,0:T(8,128)(2,1)S(1)} collective-permute-done((bf16[384,1280]{1,0:T(8,128)(2,1)S(1)}, bf16[384,1280]{1,0:T(8,128)(2,1)S(1)}, u32[]{:S(2)}, u32[]{:S(2)}) %collective-permute-start.15) | collective-permute-done | bytes 983072 | tf_op jit(solution)/shard_map/ppermute | solution.py:363
  178.1 1.3 collective-permute-start.24
  180.0 2.0 %collective-permute-start.25 = (bf16[2,40,1024]{2,1,0:T(8,128)(2,1)S(1)}, bf16[2,40,1024]{2,1,0:T(8,128)(2,1)S(1)}, u32[]{:S(2)}, u32[]{:S(2)}) collective-permute-start(bf16[2,40,1024]{2,1,0:T(8,128)(2,1)S(1)} %pad_maximum_fusion.7), channel_id=1, source_target_pairs={{0,32},{4,36},{8,40},{12,44},{16,48},{20,52},{24,56},{28,60},{32,0... | collective-permute-start | bytes 491528 | tf_op jit(solution)/shard_map/ppermute | solution.py:282
  182.2 1.5 collective-permute-start.26
  183.8 1.7 shard_map.95
  185.5 1.1 broadcast_select_fusion
  187.8 0.8 slice_bitcast_fusion
  (126 shorter events, 19.7 us)
Async XLA Ops:
  0.6 22.7 %copy-start = (bf16[2,64,2560]{2,1,0:T(8,128)(2,1)S(1)}, bf16[2,64,2560]{2,1,0:T(8,128)(2,1)}, u32[]{:S(2)}) copy-start(bf16[2,64,2560]{2,1,0:T(8,128)(2,1)} %param.7) | copy-start | bytes 1966084
  0.6 16.6 %copy-start.2 = (bf16[1,2,192,1280]{3,2,1,0:T(8,128)(2,1)S(1)}, bf16[1,2,192,1280]{3,2,1,0:T(8,128)(2,1)}, u32[]{:S(2)}) copy-start(bf16[1,2,192,1280]{3,2,1,0:T(8,128)(2,1)} %param.10) | copy-start | bytes 2949124
  0.7 16.4 %copy-start.3 = (f32[1,1280]{1,0:T(1,128)S(1)}, f32[1,1280]{1,0:T(1,128)}, u32[]{:S(2)}) copy-start(f32[1,1280]{1,0:T(1,128)} %gain_ref.1) | copy-start | bytes 15364
  4.5 17.5 %all-to-all-start = ((s32[32,1,2]{2,1,0:T(1,128)}), s32[32,1,2]{2,1,0:T(1,128)S(1)}, u32[]{:S(2)}, u32[]{:S(2)}) async-start(s32[32,1,2]{2,1,0:T(1,128)} %copy.25), calls=%async_computation | async-start | bytes 32768 | tf_op jit(solution)/shard_map/all_to_all | solution.py:105
  17.6 19.5 %copy-start.5 = (bf16[384,1280]{1,0:T(8,128)(2,1)}, bf16[384,1280]{1,0:T(8,128)(2,1)S(1)}, u32[]{:S(2)}) copy-start(bf16[384,1280]{1,0:T(8,128)(2,1)S(1)} %multiply_convert_fusion.1) | copy-start | bytes 2949124
  24.5 13.7 %all-to-all-start.1 = ((bf16[32,2,2560]{2,1,0:T(2,128)(2,1)}), bf16[32,2,2560]{2,1,0:T(2,128)(2,1)S(1)}, u32[]{:S(2)}, u32[]{:S(2)}) async-start(bf16[32,2,2560]{2,1,0:T(2,128)(2,1)} %all_to_all.16), calls=%async_computation.1 | async-start | bytes 655360 | tf_op jit(solution)/shard_map/all_to_all | solution.py:114
  38.4 6.0 %collective-permute-start.2 = (bf16[64,2560]{1,0:T(8,128)(2,1)S(1)}, bf16[64,2560]{1,0:T(8,128)(2,1)S(1)}, u32[]{:S(2)}, u32[]{:S(2)}) collective-permute-start(bf16[64,2560]{1,0:T(8,128)(2,1)S(1)} %all_to_all.18), channel_id=1, source_target_pairs={{2,3},{3,2},{6,7},{7,6},{10,11},{11,10},{14,15},{15,14},{18,19},{1... | collective-permute-start | bytes 983048 | tf_op jit(solution)/shard_map/ppermute | solution.py:118
  39.0 9.0 %collective-permute-start.1 = (bf16[64,2560]{1,0:T(8,128)(2,1)S(1)}, bf16[64,2560]{1,0:T(8,128)(2,1)S(1)}, u32[]{:S(2)}, u32[]{:S(2)}) collective-permute-start(bf16[64,2560]{1,0:T(8,128)(2,1)S(1)} %all_to_all.18), channel_id=1, source_target_pairs={{0,3},{1,2},{4,7},{5,6},{8,11},{9,10},{12,15},{13,14},{16,19},{17,... | collective-permute-start | bytes 983048 | tf_op jit(solution)/shard_map/ppermute | solution.py:117
  43.0 5.4 %collective-permute-start = (bf16[64,2560]{1,0:T(8,128)(2,1)S(1)}, bf16[64,2560]{1,0:T(8,128)(2,1)S(1)}, u32[]{:S(2)}, u32[]{:S(2)}) collective-permute-start(bf16[64,2560]{1,0:T(8,128)(2,1)S(1)} %all_to_all.18), channel_id=1, source_target_pairs={{0,2},{1,3},{4,6},{5,7},{8,10},{9,11},{12,14},{13,15},{16,18},{17,... | collective-permute-start | bytes 983048 | tf_op jit(solution)/shard_map/ppermute | solution.py:116
  48.5 1.5 copy-start.7
  48.8 7.1 %slice-start.2 = ((s8[6553600]{0:T(1024)(128)(4,1)}), s8[4194304]{0:T(1024)(128)(4,1)S(1)}, s32[]{:S(2)}) async-start(s8[6553600]{0:T(1024)(128)(4,1)} %bitcast.157), calls=%async_computation.4 | async-start | bytes 8388608
  50.0 5.9 %slice-start.3 = ((s8[6553600]{0:T(1024)(128)(4,1)}), s8[2359296]{0:T(1024)(128)(4,1)S(1)}, s32[]{:S(2)}) async-start(s8[6553600]{0:T(1024)(128)(4,1)} %bitcast.157), calls=%async_computation.5 | async-start | bytes 4718592
  58.7 2.0 %copy-start.6 = (bf16[384,1280]{1,0:T(8,128)(2,1)}, bf16[384,1280]{1,0:T(8,128)(2,1)S(1)}, u32[]{:S(2)}) copy-start(bf16[384,1280]{1,0:T(8,128)(2,1)S(1)} %fusion.26) | copy-start | bytes 2949124
  60.7 9.2 %collective-permute-start.3 = (bf16[1200,1280]{1,0:T(8,128)(2,1)}, bf16[1200,1280]{1,0:T(8,128)(2,1)}, u32[]{:S(2)}, u32[]{:S(2)}) collective-permute-start(bf16[1200,1280]{1,0:T(8,128)(2,1)} %pad_maximum_fusion), channel_id=1, source_target_pairs={{2,0},{3,1},{6,4},{7,5},{10,8},{11,9},{14,12},{15,13},{18,16},{19,... | collective-permute-start | bytes 9216008 | tf_op jit(solution)/shard_map/ppermute | solution.py:346
  62.2 18.3 %collective-permute-start.4 = (bf16[384,1280]{1,0:T(8,128)(2,1)}, bf16[384,1280]{1,0:T(8,128)(2,1)S(1)}, u32[]{:S(2)}, u32[]{:S(2)}) collective-permute-start(bf16[384,1280]{1,0:T(8,128)(2,1)} %copy-done.6), channel_id=1, source_target_pairs={{2,1},{3,0},{6,5},{7,4},{10,9},{11,8},{14,13},{15,12},{18,17},{19,... | collective-permute-start | bytes 2949128 | tf_op jit(solution)/shard_map/ppermute | solution.py:338
  70.6 11.8 %slice-start = ((s8[6553600]{0:T(1024)(128)(4,1)}), s8[4194304]{0:T(1024)(128)(4,1)S(1)}, s32[]{:S(2)}) async-start(s8[6553600]{0:T(1024)(128)(4,1)} %bitcast.155), calls=%async_computation.2 | async-start | bytes 8388608
  80.5 1.9 %slice-start.1 = ((s8[6553600]{0:T(1024)(128)(4,1)}), s8[2359296]{0:T(1024)(128)(4,1)S(1)}, s32[]{:S(2)}) async-start(s8[6553600]{0:T(1024)(128)(4,1)} %bitcast.155), calls=%async_computation.3 | async-start | bytes 4718592
  82.3 1.5 copy-start.8
  90.1 1.5 copy-start.4
  92.9 30.4 %collective-permute-start.9 = (bf16[2,640,512]{2,1,0:T(8,128)(2,1)S(1)}, bf16[2,640,512]{2,1,0:T(8,128)(2,1)S(1)}, u32[]{:S(2)}, u32[]{:S(2)}) collective-permute-start(bf16[2,640,512]{2,1,0:T(8,128)(2,1)S(1)} %convolution_convert_fusion.7), channel_id=1, source_target_pairs={{0,96},{4,100},{8,104},{12,108},{16,112},{20,116},{24,120},{28,124... | collective-permute-start | bytes 3932168 | tf_op jit(solution)/shard_map/ppermute | solution.py:282
  97.6 29.1 %collective-permute-start.8 = (bf16[2,640,512]{2,1,0:T(8,128)(2,1)}, bf16[2,640,512]{2,1,0:T(8,128)(2,1)S(1)}, u32[]{:S(2)}, u32[]{:S(2)}) collective-permute-start(bf16[2,640,512]{2,1,0:T(8,128)(2,1)} %convolution_convert_fusion.6), channel_id=1, source_target_pairs={{0,32},{4,36},{8,40},{12,44},{16,48},{20,52},{24,56},{28,60},{32,0... | collective-permute-start | bytes 3932168 | tf_op jit(solution)/shard_map/ppermute | solution.py:282
  101.4 38.4 %collective-permute-start.5 = (bf16[2,640,512]{2,1,0:T(8,128)(2,1)S(1)}, bf16[2,640,512]{2,1,0:T(8,128)(2,1)S(1)}, u32[]{:S(2)}, u32[]{:S(2)}) collective-permute-start(bf16[2,640,512]{2,1,0:T(8,128)(2,1)S(1)} %convolution_convert_fusion.3), channel_id=1, source_target_pairs={{0,4},{4,0},{8,12},{12,8},{16,20},{20,16},{24,28},{28,24},{32,36},... | collective-permute-start | bytes 3932168 | tf_op jit(solution)/shard_map/ppermute | solution.py:282
  102.4 31.4 %collective-permute-start.6 = (bf16[2,640,512]{2,1,0:T(8,128)(2,1)S(1)}, bf16[2,640,512]{2,1,0:T(8,128)(2,1)S(1)}, u32[]{:S(2)}, u32[]{:S(2)}) collective-permute-start(bf16[2,640,512]{2,1,0:T(8,128)(2,1)S(1)} %convolution_convert_fusion.4), channel_id=1, source_target_pairs={{0,8},{4,12},{8,0},{12,4},{16,24},{20,28},{24,16},{28,20},{32,40},... | collective-permute-start | bytes 3932168 | tf_op jit(solution)/shard_map/ppermute | solution.py:282
  103.9 29.4 %collective-permute-start.7 = (bf16[2,640,512]{2,1,0:T(8,128)(2,1)}, bf16[2,640,512]{2,1,0:T(8,128)(2,1)S(1)}, u32[]{:S(2)}, u32[]{:S(2)}) collective-permute-start(bf16[2,640,512]{2,1,0:T(8,128)(2,1)} %convolution_convert_fusion.5), channel_id=1, source_target_pairs={{0,24},{4,28},{8,16},{12,20},{16,8},{20,12},{24,0},{28,4},{32,56},... | collective-permute-start | bytes 3932168 | tf_op jit(solution)/shard_map/ppermute | solution.py:282
  134.4 13.1 %collective-permute-start.14 = (bf16[2,320,512]{2,1,0:T(8,128)(2,1)S(1)}, bf16[2,320,512]{2,1,0:T(8,128)(2,1)S(1)}, u32[]{:S(2)}, u32[]{:S(2)}) collective-permute-start(bf16[2,320,512]{2,1,0:T(8,128)(2,1)S(1)} %add_convert_fusion.2), channel_id=1, source_target_pairs={{0,4},{4,0},{8,12},{12,8},{16,20},{20,16},{24,28},{28,24},{32,36},... | collective-permute-start | bytes 1966088 | tf_op jit(solution)/shard_map/ppermute | solution.py:282
  135.6 12.9 %collective-permute-start.13 = (bf16[2,320,512]{2,1,0:T(8,128)(2,1)S(1)}, bf16[2,320,512]{2,1,0:T(8,128)(2,1)S(1)}, u32[]{:S(2)}, u32[]{:S(2)}) collective-permute-start(bf16[2,320,512]{2,1,0:T(8,128)(2,1)S(1)} %add_convert_fusion.5), channel_id=1, source_target_pairs={{0,32},{4,36},{8,40},{12,44},{16,48},{20,52},{24,56},{28,60},{32,0... | collective-permute-start | bytes 1966088 | tf_op jit(solution)/shard_map/ppermute | solution.py:282
  137.6 17.3 %collective-permute-start.11 = (bf16[2,320,512]{2,1,0:T(8,128)(2,1)S(1)}, bf16[2,320,512]{2,1,0:T(8,128)(2,1)S(1)}, u32[]{:S(2)}, u32[]{:S(2)}) collective-permute-start(bf16[2,320,512]{2,1,0:T(8,128)(2,1)S(1)} %add_convert_fusion.3), channel_id=1, source_target_pairs={{0,8},{4,12},{8,0},{12,4},{16,24},{20,28},{24,16},{28,20},{32,40},... | collective-permute-start | bytes 1966088 | tf_op jit(solution)/shard_map/ppermute | solution.py:282
  137.6 16.7 %collective-permute-start.12 = (bf16[2,320,512]{2,1,0:T(8,128)(2,1)S(1)}, bf16[2,320,512]{2,1,0:T(8,128)(2,1)S(1)}, u32[]{:S(2)}, u32[]{:S(2)}) collective-permute-start(bf16[2,320,512]{2,1,0:T(8,128)(2,1)S(1)} %add_convert_fusion.4), channel_id=1, source_target_pairs={{0,24},{4,28},{8,16},{12,20},{16,8},{20,12},{24,0},{28,4},{32,56},... | collective-permute-start | bytes 1966088 | tf_op jit(solution)/shard_map/ppermute | solution.py:282
  140.3 16.6 %collective-permute-start.10 = (bf16[2,320,512]{2,1,0:T(8,128)(2,1)S(1)}, bf16[2,320,512]{2,1,0:T(8,128)(2,1)S(1)}, u32[]{:S(2)}, u32[]{:S(2)}) collective-permute-start(bf16[2,320,512]{2,1,0:T(8,128)(2,1)S(1)} %add_convert_fusion.1), channel_id=1, source_target_pairs={{0,96},{4,100},{8,104},{12,108},{16,112},{20,116},{24,120},{28,124... | collective-permute-start | bytes 1966088 | tf_op jit(solution)/shard_map/ppermute | solution.py:282
  149.2 16.2 %collective-permute-start.19 = (bf16[2,160,1024]{2,1,0:T(8,128)(2,1)S(1)}, bf16[2,160,1024]{2,1,0:T(8,128)(2,1)S(1)}, u32[]{:S(2)}, u32[]{:S(2)}) collective-permute-start(bf16[2,160,1024]{2,1,0:T(8,128)(2,1)S(1)} %pad_maximum_fusion.3), channel_id=1, source_target_pairs={{0,24},{4,28},{8,16},{12,20},{16,8},{20,12},{24,0},{28,4},{32,56},... | collective-permute-start | bytes 1966088 | tf_op jit(solution)/shard_map/ppermute | solution.py:282
  154.7 8.4 %collective-permute-start.20 = (bf16[2,160,512]{2,1,0:T(8,128)(2,1)S(1)}, bf16[2,160,512]{2,1,0:T(8,128)(2,1)S(1)}, u32[]{:S(2)}, u32[]{:S(2)}) collective-permute-start(bf16[2,160,512]{2,1,0:T(8,128)(2,1)S(1)} %add_convert_fusion.8), channel_id=1, source_target_pairs={{0,96},{4,100},{8,104},{12,108},{16,112},{20,116},{24,120},{28,124... | collective-permute-start | bytes 983048 | tf_op jit(solution)/shard_map/ppermute | solution.py:282
  157.3 11.0 %collective-permute-start.17 = (bf16[2,160,512]{2,1,0:T(8,128)(2,1)S(1)}, bf16[2,160,512]{2,1,0:T(8,128)(2,1)S(1)}, u32[]{:S(2)}, u32[]{:S(2)}) collective-permute-start(bf16[2,160,512]{2,1,0:T(8,128)(2,1)S(1)} %add_convert_fusion.6), channel_id=1, source_target_pairs={{0,32},{4,36},{8,40},{12,44},{16,48},{20,52},{24,56},{28,60},{32,0... | collective-permute-start | bytes 983048 | tf_op jit(solution)/shard_map/ppermute | solution.py:282
  157.4 9.6 %collective-permute-start.18 = (bf16[2,160,512]{2,1,0:T(8,128)(2,1)S(1)}, bf16[2,160,512]{2,1,0:T(8,128)(2,1)S(1)}, u32[]{:S(2)}, u32[]{:S(2)}) collective-permute-start(bf16[2,160,512]{2,1,0:T(8,128)(2,1)S(1)} %add_convert_fusion.7), channel_id=1, source_target_pairs={{0,4},{4,0},{8,12},{12,8},{16,20},{20,16},{24,28},{28,24},{32,36},... | collective-permute-start | bytes 983048 | tf_op jit(solution)/shard_map/ppermute | solution.py:282
  158.3 19.2 %collective-permute-start.15 = (bf16[384,1280]{1,0:T(8,128)(2,1)S(1)}, bf16[384,1280]{1,0:T(8,128)(2,1)S(1)}, u32[]{:S(2)}, u32[]{:S(2)}) collective-permute-start(bf16[384,1280]{1,0:T(8,128)(2,1)S(1)} %fusion.29.mine_ref), channel_id=1, source_target_pairs={{0,1},{1,0},{4,5},{5,4},{8,9},{9,8},{12,13},{13,12},{16,17},{17,16... | collective-permute-start | bytes 2949128 | tf_op jit(solution)/shard_map/ppermute | solution.py:363
  163.1 20.7 %collective-permute-start.16 = (bf16[384,1280]{1,0:T(8,128)(2,1)S(1)}, bf16[384,1280]{1,0:T(8,128)(2,1)S(1)}, u32[]{:S(2)}, u32[]{:S(2)}) collective-permute-start(bf16[384,1280]{1,0:T(8,128)(2,1)S(1)} %shard_map.94), channel_id=1, source_target_pairs={{0,2},{1,3},{4,6},{5,7},{8,10},{9,11},{12,14},{13,15},{16,18},{17,... | collective-permute-start | bytes 2949128 | tf_op jit(solution)/shard_map/ppermute | solution.py:364
  165.8 7.2 %collective-permute-start.23 = (bf16[2,80,1024]{2,1,0:T(8,128)(2,1)S(1)}, bf16[2,80,1024]{2,1,0:T(8,128)(2,1)S(1)}, u32[]{:S(2)}, u32[]{:S(2)}) collective-permute-start(bf16[2,80,1024]{2,1,0:T(8,128)(2,1)S(1)} %pad_maximum_fusion.4), channel_id=1, source_target_pairs={{0,8},{4,12},{8,0},{12,4},{16,24},{20,28},{24,16},{28,20},{32,40},... | collective-permute-start | bytes 983048 | tf_op jit(solution)/shard_map/ppermute | solution.py:282
  167.6 11.7 %collective-permute-start.22 = (bf16[2,80,1024]{2,1,0:T(8,128)(2,1)S(1)}, bf16[2,80,1024]{2,1,0:T(8,128)(2,1)S(1)}, u32[]{:S(2)}, u32[]{:S(2)}) collective-permute-start(bf16[2,80,1024]{2,1,0:T(8,128)(2,1)S(1)} %pad_maximum_fusion.5), channel_id=1, source_target_pairs={{0,96},{4,100},{8,104},{12,108},{16,112},{20,116},{24,120},{28,124... | collective-permute-start | bytes 983048 | tf_op jit(solution)/shard_map/ppermute | solution.py:282
  168.6 13.4 %collective-permute-start.21 = (bf16[2,80,512]{2,1,0:T(8,128)(2,1)S(1)}, bf16[2,80,512]{2,1,0:T(8,128)(2,1)S(1)}, u32[]{:S(2)}, u32[]{:S(2)}) collective-permute-start(bf16[2,80,512]{2,1,0:T(8,128)(2,1)S(1)} %add_convert_fusion.11), channel_id=1, source_target_pairs={{0,24},{4,28},{8,16},{12,20},{16,8},{20,12},{24,0},{28,4},{32,56},... | collective-permute-start | bytes 491528 | tf_op jit(solution)/shard_map/ppermute | solution.py:282
  178.1 8.5 %collective-permute-start.24 = (bf16[2,40,1024]{2,1,0:T(8,128)(2,1)S(1)}, bf16[2,40,1024]{2,1,0:T(8,128)(2,1)S(1)}, u32[]{:S(2)}, u32[]{:S(2)}) collective-permute-start(bf16[2,40,1024]{2,1,0:T(8,128)(2,1)S(1)} %pad_maximum_fusion.6), channel_id=1, source_target_pairs={{0,4},{4,0},{8,12},{12,8},{16,20},{20,16},{24,28},{28,24},{32,36},... | collective-permute-start | bytes 491528 | tf_op jit(solution)/shard_map/ppermute | solution.py:282
  180.0 7.2 %collective-permute-start.25 = (bf16[2,40,1024]{2,1,0:T(8,128)(2,1)S(1)}, bf16[2,40,1024]{2,1,0:T(8,128)(2,1)S(1)}, u32[]{:S(2)}, u32[]{:S(2)}) collective-permute-start(bf16[2,40,1024]{2,1,0:T(8,128)(2,1)S(1)} %pad_maximum_fusion.7), channel_id=1, source_target_pairs={{0,32},{4,36},{8,40},{12,44},{16,48},{20,52},{24,56},{28,60},{32,0... | collective-permute-start | bytes 491528 | tf_op jit(solution)/shard_map/ppermute | solution.py:282
  182.2 5.5 %collective-permute-start.26 = (bf16[2,40,512]{2,1,0:T(8,128)(2,1)S(1)}, bf16[2,40,512]{2,1,0:T(8,128)(2,1)S(1)}, u32[]{:S(2)}, u32[]{:S(2)}) collective-permute-start(bf16[2,40,512]{2,1,0:T(8,128)(2,1)S(1)} %add_convert_fusion.21), channel_id=1, source_target_pairs={{0,8},{4,12},{8,0},{12,4},{16,24},{20,28},{24,16},{28,20},{32,40},... | collective-permute-start | bytes 245768 | tf_op jit(solution)/shard_map/ppermute | solution.py:282
  186.9 1.7 copy-start.1

commit v2 on v1

--- a/solution.py
+++ b/solution.py
@@ -1,3 +1,5 @@
+import functools
+
 import jax
 import jax.numpy as jnp
 from jax import lax
@@ -89,29 +91,83 @@
     )(incoming, mine, other, x, gain)
 
 
-def ask_tokens(seq_dev, slots, frames, sec, rep, peers):
+def ask_kernel(ids_ref, frames_ref, slots_ref, out_ref, *, seq_dev):
+    sec, rep = ids_ref[0], ids_ref[1]
+    peers, per = out_ref.shape
+    cap = slots_ref.shape[1]
+    count = frames_ref[sec, 0]
+    for k in range(1, frames_ref.shape[1]):
+        count = count + frames_ref[sec, k]
+    wanted = jnp.where(sec == 0, slots_ref[0:1, :], slots_ref[1:2, :])
+    j = lax.broadcasted_iota(jnp.int32, (1, cap), 1)
+    holder = lax.rem(rep + j, peers)
+    position = jnp.where(j < TPF * count, wanted - seq_dev * holder + 1, 0).astype(jnp.float32)
+    here = lax.broadcasted_iota(jnp.int32, (peers, cap), 0) == holder
+    column = lax.broadcasted_iota(jnp.int32, (peers, per), 1)
+    out = jnp.zeros((peers, per), jnp.float32)
+    for k in range(per):
+        turn = here & (j >= k * peers) & (j < (k + 1) * peers)
+        asked = jnp.sum(jnp.where(turn, position, 0.0), axis=1, keepdims=True)
+        out = jnp.where(column == k, asked, out)
+    out_ref[...] = out.astype(jnp.int32)
+
+
+def ask_tokens(seq_dev, slots, frames, ids, peers):
     cap = slots.shape[1]
     per = -(-cap // peers)
-    counts = TPF * jnp.sum(frames, axis=1)
-    count = lax.dynamic_index_in_dim(counts, sec, 0, keepdims=False)
-    wanted = lax.dynamic_index_in_dim(slots, sec, 0, keepdims=False)
-    wanted = jnp.concatenate([wanted, jnp.zeros((per * peers - cap,), jnp.int32)])
-    j = jnp.arange(per * peers)
-    position = jnp.where(j < count, wanted - seq_dev * ((rep + j) % peers) + 1, 0)
-    position = position.reshape(per, 1, peers)
-    holder = jnp.arange(peers)
-    turned = (jnp.arange(peers)[None, :] == ((holder - rep) % peers)[:, None]).astype(jnp.int32)
-    requests = jnp.sum(position * turned[None], axis=2).T
-    return lax.all_to_all(requests, "dp", 0, 0, tiled=True).reshape(-1)
-
-
-def fetch_tokens(llm_grad, asked, cap, sec, ten, rep, peers):
+    requests = pl.pallas_call(
+        functools.partial(ask_kernel, seq_dev=seq_dev),
+        grid_spec=pltpu.PrefetchScalarGridSpec(
+            num_scalar_prefetch=2,
+            grid=(1,),
+            in_specs=[pl.BlockSpec(slots.shape, lambda i, *_: (0, 0))],
+            out_specs=pl.BlockSpec((peers, per), lambda i, *_: (0, 0)),
+        ),
+        out_shape=jax.ShapeDtypeStruct((peers, per), jnp.int32),
+    )(ids, frames, slots)
+    return lax.all_to_all(requests, "dp", 0, 0, tiled=True)
+
+
+def pick_kernel(ids_ref, asked_ref, held_ref, out_ref):
+    peers, per = asked_ref.shape
+    seq_dev = held_ref.shape[1]
+    row = lax.broadcasted_iota(jnp.int32, (peers * per, 1), 0)
+    spread = lax.broadcasted_iota(jnp.int32, (peers * per, peers), 1) == row // per
+    asked = dot(
+        spread.astype(jnp.float32).astype(jnp.bfloat16),
+        asked_ref[...].astype(jnp.float32).astype(jnp.bfloat16),
+        1,
+        0,
+    )
+    place = jnp.zeros((peers * per, 1), jnp.float32)
+    for k in range(per):
+        place = jnp.where(row % per == k, asked[:, k : k + 1], place)
+    positions = lax.broadcasted_iota(jnp.int32, (peers * per, seq_dev), 1) + 1
+    pick = (place == positions.astype(jnp.float32)).astype(jnp.float32).astype(jnp.bfloat16)
+    out_ref[...] = dot(pick, held_ref[0], 1, 0).astype(jnp.bfloat16)
+
+
+def pick_rows(asked, llm_grad, ids):
     seq_dev, width = llm_grad.shape[1:]
+    return pl.pallas_call(
+        pick_kernel,
+        grid_spec=pltpu.PrefetchScalarGridSpec(
+            num_scalar_prefetch=1,
+            grid=(1,),
+            in_specs=[
+                pl.BlockSpec(asked.shape, lambda i, *_: (0, 0)),
+                pl.BlockSpec((1, seq_dev, width), lambda i, ids: (ids[0], 0, 0)),
+            ],
+            out_specs=pl.BlockSpec((asked.size, width), lambda i, *_: (0, 0)),
+        ),
+        out_shape=jax.ShapeDtypeStruct((asked.size, width), jnp.bfloat16),
+    )(ids, asked, llm_grad)
+
+
+def fetch_tokens(llm_grad, asked, cap, ids, ten, rep, peers):
+    width = llm_grad.shape[2]
     per = -(-cap // peers)
-    pick = (asked[:, None] == jnp.arange(1, seq_dev + 1)[None, :]).astype(jnp.bfloat16)
-    held = lax.dynamic_index_in_dim(llm_grad, sec, 0, keepdims=False)
-    rows = dot(pick, held, 1, 0).astype(jnp.bfloat16)
-    got = lax.all_to_all(rows, "dp", 0, 0, tiled=True)
+    got = lax.all_to_all(pick_rows(asked, llm_grad, ids), "dp", 0, 0, tiled=True)
     both = ("section", "tensor")
     first_own = lax.ppermute(got, both, [(0, 2), (1, 3)])
     first_other = lax.ppermute(got, both, [(0, 3), (1, 2)])
@@ -129,7 +185,7 @@
     for own, other in ((first_own, first_other), (got, second_other)):
         stacked = jnp.concatenate([own[:, :half], own[:, half:], other[:, :half], other[:, half:]])
         out.append(dot(spread, stacked, 1, 0).astype(jnp.bfloat16))
-    return jnp.concatenate(out)
+    return jnp.concatenate(out), got
 
 
 def reordered(left, stream):
@@ -161,21 +217,20 @@
             total = total + piece[:, lo:hi].astype(jnp.float32)
         return total.astype(jnp.bfloat16)
 
-    last, turns = None, {}
+    last, turns, started = None, {}, []
     for t in range(BITS):
         for place, streams in enumerate(SHARED[t]):
-            if t == 0 and last is not None:
-                lefts[place] = after(lefts[place], last)
             if t:
                 for i in streams:
                     received[i][-1] = after(received[i][-1], last, turns.get((t, place)))
             sends = [group(i, width >> (t + 1), width >> t) for i in streams]
             last = sends[0] if len(sends) == 1 else jnp.concatenate(sends, axis=2)
+            started.append(last)
             piece = lax.ppermute(last, "dp", neighbour_pairs(ORDERS[streams[0]][t]))
             for k, i in enumerate(streams):
                 received[i].append(piece[:, :, k * span : (k + 1) * span])
         if t == 0:
-            middle = first(last)
+            middle = first(started)
             turns[1, 0] = middle
         if t == 2:
             end = second(middle, last)
@@ -201,11 +256,10 @@
     xhat = centered * rstd
     normed = (xhat * gain).astype(jnp.bfloat16)
 
-    asked = ask_tokens(llm_grad.shape[1], slots, frames, sec, rep, peers)
+    ids = jnp.stack([sec, rep])
+    asked = ask_tokens(llm_grad.shape[1], slots, frames, ids, peers)
     normed, asked = lax.optimization_barrier((normed, asked))
-    upstream = lax.optimization_barrier(
-        fetch_tokens(llm_grad, asked, slots.shape[1], sec, ten, rep, peers)
-    )
+    upstream, got = fetch_tokens(llm_grad, asked, slots.shape[1], ids, ten, rep, peers)
     activ, slope = lax.optimization_barrier(gelu_and_slope(dot(normed, weight_in, 1, 0)))
 
     order = from_code(to_code(rep) ^ jnp.arange(peers))
@@ -213,114 +267,8 @@
     order = (order[:, None] * chunk + jnp.arange(chunk)[None, :]).reshape(-1)
     turn = (order[:, None] == jnp.arange(width)[None, :]).astype(jnp.bfloat16)
 
-    x = saved_in[0].reshape(rows, width)
-
-    def pre_gradient(incoming):
-        return lax.optimization_barrier(
-            (dot(incoming, weight_out, 1, 1) * slope).astype(jnp.bfloat16)
-        )
-
-    both = ("section", "tensor")
-    first_own = lax.ppermute(got, both, [(0, 2), (1, 3)])
-    first_other = lax.ppermute(got, both, [(0, 3), (1, 2)])
-    second_other = lax.ppermute(got, both, [(2, 3), (3, 2)])
-    half = width // 2
-    row = jnp.arange(cap * 4)
-    tok, part = row // 4, row % 4
-    source = (
-        ((part // 2 != ten).astype(jnp.int32) * 2 + part % 2) * (per * peers)
-        + ((rep + tok) % peers) * per
-        + tok // peers
-    )
-    spread = (source[:, None] == jnp.arange(4 * per * peers)[None, :]).astype(jnp.bfloat16)
-    out = []
-    for own, other in ((first_own, first_other), (got, second_other)):
-        stacked = jnp.concatenate([own[:, :half], own[:, half:], other[:, :half], other[:, half:]])
-        out.append(dot(spread, stacked, 1, 0).astype(jnp.bfloat16))
-    return jnp.concatenate(out)
-
-
-def reordered(left, stream):
-    width = left.shape[1]
-    sizes, axes = LAYOUTS[stream]
-    split = left.reshape((2,) + sizes + (width >> BITS, -1))
-    axes = (0,) + tuple(1 + a for a in axes) + (len(axes) + 1, len(axes) + 2)
-    return split.transpose(axes).reshape(left.shape)
-
-
-def after(value, *others):
-    return lax.optimization_barrier((value, others))[0]
-
-
-def reduce_weight_grads(left, right, first, second):
-    width = left.shape[1]
-    span = right.shape[2] // BITS
-    lefts = [reordered(left, i) for i in range(BITS)]
-    received = [[] for _ in range(BITS)]
-
-    def group(i, lo, hi):
-        total = lax.dot_general(
-            lefts[i][:, lo:hi],
-            right[:, :, i * span : (i + 1) * span],
-            (((2,), (1,)), ((0,), (0,))),
-            preferred_element_type=jnp.float32,
-        )
-        for piece in received[i]:
-            total = total + piece[:, lo:hi].astype(jnp.float32)
-        return total.astype(jnp.bfloat16)
-
-    last, turns = None, {}
-    for t in range(BITS):
-        for place, streams in enumerate(SHARED[t]):
-            if t == 0 and last is not None:
-                lefts[place] = after(lefts[place], last)
-            if t:
-                for i in streams:
-                    received[i][-1] = after(received[i][-1], last, turns.get((t, place)))
-            sends = [group(i, width >> (t + 1), width >> t) for i in streams]
-            last = sends[0] if len(sends) == 1 else jnp.concatenate(sends, axis=2)
-            piece = lax.ppermute(last, "dp", neighbour_pairs(ORDERS[streams[0]][t]))
-            for k, i in enumerate(streams):
-                received[i].append(piece[:, :, k * span : (k + 1) * span])
-        if t == 0:
-            middle = first(last)
-            turns[1, 0] = middle
-        if t == 2:
-            end = second(middle, last)
-            turns[4, 0] = end[0]
-    result = jnp.concatenate([group(i, 0, width >> BITS) for i in range(BITS)], axis=2)
-    return result, middle, after(end, last)
-
-
-def per_device(llm_grad, slots, frames, saved_in, ln_gain, w_in, w_out):
-    peers = lax.axis_size("dp")
-    sec = lax.axis_index("section")
-    ten = lax.axis_index("tensor")
-    rep = lax.axis_index("dp")
-    micro_count, tok_rows, width = saved_in.shape[1:]
-    rows = micro_count * tok_rows
-    gain = ln_gain
-    weight_in = w_in[0]
-    weight_out = w_out[0]
-
-    widen = saved_in[0].reshape(rows, width).astype(jnp.float32)
-    centered = widen - jnp.mean(widen, axis=-1, keepdims=True)
-    rstd = lax.rsqrt(jnp.mean(centered * centered, axis=-1, keepdims=True) + 1e-05)
-    xhat = centered * rstd
-    normed = (xhat * gain).astype(jnp.bfloat16)
-
-    asked = ask_tokens(llm_grad.shape[1], slots, frames, sec, rep, peers)
-    normed, asked = lax.optimization_barrier((normed, asked))
-    upstream = lax.optimization_barrier(
-        fetch_tokens(llm_grad, asked, slots.shape[1], sec, ten, rep, peers)
-    )
-    activ, slope = lax.optimization_barrier(gelu_and_slope(dot(normed, weight_in, 1, 0)))
-
-    order = from_code(to_code(rep) ^ jnp.arange(peers))
-    chunk = width // peers
-    order = (order[:, None] * chunk + jnp.arange(chunk)[None, :]).reshape(-1)
-    turn = (order[:, None] == jnp.arange(width)[None, :]).astype(jnp.bfloat16)
-
+    normed_t = dot(turn, after(normed, got), 1, 1).astype(jnp.bfloat16)
+    upstream = after(upstream, normed_t)
     x = saved_in[0].reshape(rows, width)
 
     def pre_gradient(incoming):
@@ -348,15 +296,14 @@
     later_gain = sum(
         packed[3 * rows + 16 * k : 3 * rows + 16 * k + 1].astype(jnp.float32) for k in range(3)
     )
-    normed_t = dot(turn, after(normed, partial), 1, 1).astype(jnp.bfloat16)
     grad_last = finish(passed, mine, other, later_x, later_gain, tok_rows // 2)
 
     incoming = jnp.where(sec == 1, upstream, grad_last)
     d_pre = pre_gradient(incoming)
     incoming_t = dot(turn, incoming, 1, 1).astype(jnp.bfloat16)
 
-    def partial_here(last):
-        return dot(after(d_pre, last), weight_in, 1, 1).astype(jnp.bfloat16)
+    def partial_here(started):
+        return dot(after(d_pre, *started), weight_in, 1, 1).astype(jnp.bfloat16)
 
     def exchange(partial, last):
         return (

time: 189 us -> 186 us (0.984)
  starting transfers between devices: 52.7 us -> 47.5 us
  Pallas kernels: 3.49 us -> 8.41 us
  matrix products: 46.2 us -> 43.7 us
  waiting for transfers between devices: 61.5 us -> 63.5 us
    pallas_call x0 -> x2, Pallas kernels: none -> 4.92 us  [the longest x1 2.85 us: pick_rows(): pl.pallas_call(pick_kernel, grid_spec=pltpu.PrefetchScalarGridSpec(num_sc...]
    ppermute x20, starting transfers between devices: 25.8 us -> 21.8 us  [reduce_weight_grads(): piece = lax.ppermute(last, 'dp', neighbour_pairs(ORDERS[streams[0]][t]))]
    ppermute x1, waiting for transfers between devices: 3.06 us -> 6.4 us  [per_device(): packed = lax.ppermute(packed, 'section', [(1, 0)])]
    ppermute x20, waiting for transfers between devices: 37 us -> 39.6 us  [reduce_weight_grads(): piece = lax.ppermute(last, 'dp', neighbour_pairs(ORDERS[streams[0]][t]))]
    dot_general x10 -> x9, matrix products: 31.6 us -> 30.1 us  [dot(): lax.dot_general(a, b, (((ca,), (cb,)), ((), ())), preferred_element_type=...]
    unnamed x26 -> x20, local copies, waits for them, and re-layouts: 3.89 us -> 3.89 us
  transfers between devices with their start and end apart: 29 -> 29, of which waited for: 16 -> 14; matrix products, arithmetic and copies ran while one was open for 21% -> 20% of each run, Pallas kernels for 1% -> 1%
where the time goes in v2:
time: 186 us; the launch traced here: 185 us
  waiting for transfers between devices  63.5 us (34%)
  starting transfers between devices  47.5 us (26%)
  matrix products  43.7 us (23%)
  local copies, waits for them, and re-layouts  10.9 us (6%)
  other arithmetic  9.63 us (5%)
  Pallas kernels  8.41 us (5%)
    ppermute x20, waiting for transfers between devices, reduce_weight_grads(): piece = lax.ppermute(last, 'dp', neighbour_pairs(ORDERS[streams[0]][t]))  39.6 us
    dot_general x9, matrix products, dot(): lax.dot_general(a, b, (((ca,), (cb,)), ((), ())), preferred_element_type=...  30.1 us
    ppermute x20, starting transfers between devices, reduce_weight_grads(): piece = lax.ppermute(last, 'dp', neighbour_pairs(ORDERS[streams[0]][t]))  21.8 us
    dot_general x30, matrix products, group(): lax.dot_general(lefts[i][:, lo:hi], right[:, :, i * span:(i + 1) * span],...  13.5 us
    all_to_all x1, starting transfers between devices, ask_tokens(): return lax.all_to_all(requests, 'dp', 0, 0, tiled=True)  9.35 us
    ppermute x1, waiting for transfers between devices, per_device(): other = lax.ppermute(partial, both, [(2, 1), (3, 0)])  7.52 us
    ppermute x1, waiting for transfers between devices, per_device(): packed = lax.ppermute(packed, 'section', [(1, 0)])  6.4 us
    all_to_all x1, waiting for transfers between devices, ask_tokens(): return lax.all_to_all(requests, 'dp', 0, 0, tiled=True)  4.21 us
  transfers between devices with their start and end apart: 29, of which 14 were waited for; matrix products, arithmetic and copies ran while one was open for 20% of the time, Pallas kernels for 1%

profile of v2, /device:TPU:0, one launch (start us, length us, event | category | flops | bytes accessed | tf_op | source)
XLA Modules:
  0.0 185.0 jit_solution(1293696400948193942)
XLA Ops:
  1.3 2.1 %shard_map.94 = s32[32,2]{1,0:T(8,128)} custom-call(s32[2]{0:T(128)} %pad_add_fusion.ids_ref, s32[2,2]{1,0:T(2,128)} %frames_ref.1, s32[2,48]{1,0:T(2,128)} %slots_ref.1), custom_call_target="tpu_custom_call" | custom-call | tf_op jit(solution)/shard_map/pallas_call | solution.py:118
  3.3 9.3 %all-to-all-start = ((s32[32,1,2]{2,1,0:T(1,128)}), s32[32,1,2]{2,1,0:T(1,128)S(1)}, u32[]{:S(2)}, u32[]{:S(2)}) async-start(s32[32,1,2]{2,1,0:T(1,128)} %bitcast.151), calls=%async_computation | async-start | bytes 32768 | tf_op jit(solution)/shard_map/all_to_all | solution.py:128
  12.7 1.4 convert_reduce_fusion
  14.1 1.6 fusion.33
  16.6 4.2 %all-to-all-done = s32[32,1,2]{2,1,0:T(1,128)S(1)} async-done(((s32[32,1,2]{2,1,0:T(1,128)}), s32[32,1,2]{2,1,0:T(1,128)S(1)}, u32[]{:S(2)}, u32[]{:S(2)}) %all-to-all-start) | async-done | bytes 288 | tf_op jit(solution)/shard_map/all_to_all | solution.py:128
  20.9 0.7 copy.19.asked_ref
  21.6 2.8 %shard_map.95 = bf16[64,2560]{1,0:T(8,128)(2,1)} custom-call(s32[2]{0:T(128)} %pad_add_fusion.ids_ref, s32[32,2]{1,0:T(8,128)} %copy.19.asked_ref, bf16[2,64,2560]{2,1,0:T(8,128)(2,1)} %held_ref.1), custom_call_target="tpu_custom_call" | custom-call | tf_op jit(solution)/shard_map/pallas_call | solution.py:152
  24.5 1.8 all_to_all.19
  26.3 4.1 %all-to-all-start.1 = ((bf16[32,2,2560]{2,1,0:T(2,128)(2,1)}), bf16[32,2,2560]{2,1,0:T(2,128)(2,1)S(1)}, u32[]{:S(2)}, u32[]{:S(2)}) async-start(bf16[32,2,2560]{2,1,0:T(2,128)(2,1)} %all_to_all.19), calls=%async_computation.1 | async-start | bytes 655360 | tf_op jit(solution)/shard_map/all_to_all | solution.py:170
  30.4 8.7 %add_convert_fusion = (bf16[384,2560]{1,0:T(8,128)(2,1)}, bf16[384,2560]{1,0:T(8,128)(2,1)}) fusion(bf16[384,1280]{1,0:T(8,128)(2,1)S(1)} %multiply_convert_fusion.1, bf16[1,1280,2560]{2,1,0:T(8,128)(2,1)} %param.12), kind=kOutput, calls=%fused_computation.25 | convolution fusion | flops 2534277120 | bytes 11468800 | tf_op jit(solution)/shard_map/dot_general | solution.py:58
  39.1 1.0 all-to-all-done.1
  40.3 0.7 collective-permute-start.2
  41.0 4.0 %collective-permute-start.1 = (bf16[64,2560]{1,0:T(8,128)(2,1)S(1)}, bf16[64,2560]{1,0:T(8,128)(2,1)S(1)}, u32[]{:S(2)}, u32[]{:S(2)}) collective-permute-start(bf16[64,2560]{1,0:T(8,128)(2,1)S(1)} %all_to_all.21), channel_id=1, source_target_pairs={{0,3},{1,2},{4,7},{5,6},{8,11},{9,10},{12,15},{13,14},{16,19},{17,... | collective-permute-start | bytes 983048 | tf_op jit(solution)/shard_map/ppermute | solution.py:173
  45.0 1.3 collective-permute-start
  46.3 1.9 %fusion.24 = bf16[1280,384]{1,0:T(8,128)(2,1)S(1)} fusion(bf16[384,1280]{1,0:T(8,128)(2,1)S(1)} %multiply_convert_fusion.1, s32[1280]{0:T(1024)S(1)} %add.373), kind=kOutput, calls=%fused_computation.42 | convolution fusion | flops 1260421120 | bytes 1971200 | tf_op jit(solution)/shard_map/dot_general | solution.py:58
  48.3 1.8 collective-permute-done.1
  50.9 1.1 copy-done.4
  52.0 5.9 %fusion.16 = bf16[384,2560]{1,0:T(8,128)(2,1)S(1)} fusion(bf16[384,2560]{1,0:T(8,128)(2,1)S(1)} %copy-done.4, bf16[384,1280]{1,0:T(8,128)(2,1)S(1)} %pad_maximum_fusion.1, bf16[1,2560,1280]{2,1,0:T(8,128)(2,1)} %param.13), kind=kOutput, calls=%fused_computation.23 | convolution fusion | flops 2519531520 | bytes 11468800 | tf_op jit(solution)/shard_map/dot_general | solution.py:58
  57.9 2.7 %fusion.26 = bf16[384,1280]{1,0:T(8,128)(2,1)S(1)} fusion(bf16[384,2560]{1,0:T(8,128)(2,1)S(1)} %fusion.16, bf16[1,1280,2560]{2,1,0:T(8,128)(2,1)S(1)} %bitcast.156), kind=kOutput, calls=%fused_computation.44 | convolution fusion | flops 2517073920 | bytes 9502720 | tf_op jit(solution)/shard_map/dot_general | solution.py:58
  60.7 1.9 %pad_maximum_fusion = bf16[1200,1280]{1,0:T(8,128)(2,1)} fusion(bf16[48,1280]{1,0:T(8,128)(2,1)S(1)} %pad_maximum_fusion.8, bf16[384,1280]{1,0:T(8,128)(2,1)S(1)} %bitcast.102, bf16[384,1280]{1,0:T(8,128)(2,1)S(1)} %pad_maximum_fusion.1, bf16[384,1280]{1,0:T(8,128)(2,1)S(1)} %fusion.26), kind=kLoop, calls=%fused_computation.31 | loop fusion | flops 12288000 | bytes 6144000 | tf_op jit(solution)/shard_map/concatenate | solution.py:293
  62.6 1.3 collective-permute-start.3
  63.9 1.5 collective-permute-start.4
  65.4 6.4 %collective-permute-done.3 = bf16[1200,1280]{1,0:T(8,128)(2,1)} collective-permute-done((bf16[1200,1280]{1,0:T(8,128)(2,1)}, bf16[1200,1280]{1,0:T(8,128)(2,1)}, u32[]{:S(2)}, u32[]{:S(2)}) %collective-permute-start.3) | collective-permute-done | bytes 3072032 | tf_op jit(solution)/shard_map/ppermute | solution.py:294
  71.8 0.8 fusion.169.gain_ref
  72.6 2.1 %fusion.191 = (bf16[384,1280]{1,0:T(8,128)(2,1)S(1)}, bf16[384,1280]{1,0:T(8,128)(2,1)S(1)}, bf16[384,1280]{1,0:T(8,128)(2,1)S(1)}) fusion(bf16[1200,1280]{1,0:T(8,128)(2,1)} %collective-permute-done.3), kind=kLoop, calls=%fused_computation.236 | loop fusion | bytes 5898240 | tf_op jit(solution)/shard_map/slice | solution.py:295
  74.7 7.5 %collective-permute-done.4.other_ref = bf16[384,1280]{1,0:T(8,128)(2,1)S(1)} collective-permute-done((bf16[384,1280]{1,0:T(8,128)(2,1)}, bf16[384,1280]{1,0:T(8,128)(2,1)S(1)}, u32[]{:S(2)}, u32[]{:S(2)}) %collective-permute-start.4) | collective-permute-done | bytes 983072 | tf_op jit(solution)/shard_map/ppermute | solution.py:286
  82.2 1.7 shard_map.96
  84.1 1.4 copy-done.5
  85.5 2.7 %fusion.19 = bf16[384,2560]{1,0:T(8,128)(2,1)S(1)} fusion(bf16[384,2560]{1,0:T(8,128)(2,1)S(1)} %copy-done.5, bf16[384,1280]{1,0:T(8,128)(2,1)S(1)} %broadcast_select_fusion.1.g_ref, bf16[1,2560,1280]{2,1,0:T(8,128)(2,1)S(1)} %bitcast.154), kind=kOutput, calls=%fused_computation.24 | convolution fusion | flops 2519531520 | bytes 11468800 | tf_op jit(solution)/shard_map/dot_general | solution.py:58
  88.3 1.9 %fusion.25 = bf16[1280,384]{1,0:T(8,128)(2,1)S(1)} fusion(bf16[384,1280]{1,0:T(8,128)(2,1)S(1)} %broadcast_select_fusion.1.g_ref, s32[1280]{0:T(1024)S(1)} %add.373), kind=kOutput, calls=%fused_computation.43 | convolution fusion | flops 1260421120 | bytes 1971200 | tf_op jit(solution)/shard_map/dot_general | solution.py:58
  92.1 1.3 copy-done.2
  93.8 0.8 convolution_convert_fusion.3
  94.6 1.6 collective-permute-start.6
  96.2 0.8 convolution_convert_fusion.4
  97.1 2.1 %collective-permute-start.7 = (bf16[2,640,512]{2,1,0:T(8,128)(2,1)S(1)}, bf16[2,640,512]{2,1,0:T(8,128)(2,1)S(1)}, u32[]{:S(2)}, u32[]{:S(2)}) collective-permute-start(bf16[2,640,512]{2,1,0:T(8,128)(2,1)S(1)} %convolution_convert_fusion.4), channel_id=1, source_target_pairs={{0,24},{4,28},{8,16},{12,20},{16,8},{20,12},{24,0},{28,4},{32,56},... | collective-permute-start | bytes 3932168 | tf_op jit(solution)/shard_map/ppermute | solution.py:229
  99.2 0.9 convolution_convert_fusion.6
  100.1 2.8 %collective-permute-start.9 = (bf16[2,640,512]{2,1,0:T(8,128)(2,1)S(1)}, bf16[2,640,512]{2,1,0:T(8,128)(2,1)S(1)}, u32[]{:S(2)}, u32[]{:S(2)}) collective-permute-start(bf16[2,640,512]{2,1,0:T(8,128)(2,1)S(1)} %convolution_convert_fusion.6), channel_id=1, source_target_pairs={{0,96},{4,100},{8,104},{12,108},{16,112},{20,116},{24,120},{28,124... | collective-permute-start | bytes 3932168 | tf_op jit(solution)/shard_map/ppermute | solution.py:229
  102.9 1.9 %convolution_convert_fusion.5 = bf16[2,640,512]{2,1,0:T(8,128)(2,1)} fusion(bf16[2,384,512]{2,1,0:T(8,128)(2,1)S(1)} %get-tuple-element.72, bf16[2,1280,384]{2,1,0:T(8,128)(2,1)S(1)} %bitcast.142), kind=kOutput, calls=%fused_computation.60 | convolution fusion | flops 503971840 | bytes 3080192 | tf_op jit(solution)/shard_map/dot_general | solution.py:210
  105.0 0.8 convolution_convert_fusion.2
  105.8 1.3 collective-permute-start.5
  107.1 5.6 %fusion.29.mine_ref = bf16[384,1280]{1,0:T(8,128)(2,1)S(1)} fusion(bf16[384,2560]{1,0:T(8,128)(2,1)S(1)} %fusion.19, bf16[1,1280,2560]{2,1,0:T(8,128)(2,1)} %param.12), kind=kOutput, calls=%fused_computation.45 | convolution fusion | flops 2517073920 | bytes 9502720 | tf_op jit(solution)/shard_map/dot_general | solution.py:58
  112.7 17.2 %collective-permute-done.9 = bf16[2,640,512]{2,1,0:T(8,128)(2,1)S(1)} collective-permute-done((bf16[2,640,512]{2,1,0:T(8,128)(2,1)S(1)}, bf16[2,640,512]{2,1,0:T(8,128)(2,1)S(1)}, u32[]{:S(2)}, u32[]{:S(2)}) %collective-permute-start.9) | collective-permute-done | bytes 1310752 | tf_op jit(solution)/shard_map/ppermute | solution.py:229
  130.4 2.9 %collective-permute-done.8 = bf16[2,640,512]{2,1,0:T(8,128)(2,1)S(1)} collective-permute-done((bf16[2,640,512]{2,1,0:T(8,128)(2,1)}, bf16[2,640,512]{2,1,0:T(8,128)(2,1)S(1)}, u32[]{:S(2)}, u32[]{:S(2)}) %collective-permute-start.8) | collective-permute-done | bytes 1310752 | tf_op jit(solution)/shard_map/ppermute | solution.py:229
  134.9 1.0 collective-permute-start.14
  136.3 0.6 collective-permute-start.11
  136.9 0.9 collective-permute-start.12
  138.3 1.1 collective-permute-start.10
  139.5 8.8 %collective-permute-done.14 = bf16[2,320,512]{2,1,0:T(8,128)(2,1)S(1)} collective-permute-done((bf16[2,320,512]{2,1,0:T(8,128)(2,1)S(1)}, bf16[2,320,512]{2,1,0:T(8,128)(2,1)S(1)}, u32[]{:S(2)}, u32[]{:S(2)}) %collective-permute-start.14) | collective-permute-done | bytes 655392 | tf_op jit(solution)/shard_map/ppermute | solution.py:229
  149.5 1.2 collective-permute-start.19
  150.8 1.6 collective-permute-done.12
  153.5 1.8 collective-permute-start.18
  155.9 2.2 %collective-permute-start.15 = (bf16[384,1280]{1,0:T(8,128)(2,1)S(1)}, bf16[384,1280]{1,0:T(8,128)(2,1)S(1)}, u32[]{:S(2)}, u32[]{:S(2)}) collective-permute-start(bf16[384,1280]{1,0:T(8,128)(2,1)S(1)} %fusion.29.mine_ref), channel_id=1, source_target_pairs={{0,1},{1,0},{4,5},{5,4},{8,9},{9,8},{12,13},{13,12},{16,17},{17,16... | collective-permute-start | bytes 2949128 | tf_op jit(solution)/shard_map/ppermute | solution.py:310
  158.1 3.0 %collective-permute-done.20 = bf16[2,160,512]{2,1,0:T(8,128)(2,1)S(1)} collective-permute-done((bf16[2,160,512]{2,1,0:T(8,128)(2,1)S(1)}, bf16[2,160,512]{2,1,0:T(8,128)(2,1)S(1)}, u32[]{:S(2)}, u32[]{:S(2)}) %collective-permute-start.20) | collective-permute-done | bytes 327712 | tf_op jit(solution)/shard_map/ppermute | solution.py:229
  161.1 1.3 collective-permute-start.16
  162.7 1.9 %collective-permute-done.19 = bf16[2,160,1024]{2,1,0:T(8,128)(2,1)S(1)} collective-permute-done((bf16[2,160,1024]{2,1,0:T(8,128)(2,1)S(1)}, bf16[2,160,1024]{2,1,0:T(8,128)(2,1)S(1)}, u32[]{:S(2)}, u32[]{:S(2)}) %collective-permute-start.19) | collective-permute-done | bytes 655392 | tf_op jit(solution)/shard_map/ppermute | solution.py:229
  166.0 1.1 collective-permute-start.22
  167.4 1.2 collective-permute-start.21
  168.6 3.6 %collective-permute-done.23 = bf16[2,80,1024]{2,1,0:T(8,128)(2,1)S(1)} collective-permute-done((bf16[2,80,1024]{2,1,0:T(8,128)(2,1)S(1)}, bf16[2,80,1024]{2,1,0:T(8,128)(2,1)S(1)}, u32[]{:S(2)}, u32[]{:S(2)}) %collective-permute-start.23) | collective-permute-done | bytes 327712 | tf_op jit(solution)/shard_map/ppermute | solution.py:229
  172.2 2.9 %collective-permute-done.15.other_ref = bf16[384,1280]{1,0:T(8,128)(2,1)S(1)} collective-permute-done((bf16[384,1280]{1,0:T(8,128)(2,1)S(1)}, bf16[384,1280]{1,0:T(8,128)(2,1)S(1)}, u32[]{:S(2)}, u32[]{:S(2)}) %collective-permute-start.15) | collective-permute-done | bytes 983072 | tf_op jit(solution)/shard_map/ppermute | solution.py:310
  176.8 1.8 collective-permute-start.25
  178.9 1.3 collective-permute-start.26
  180.1 1.7 shard_map.97
  181.9 1.0 broadcast_select_fusion
  184.2 0.8 slice_bitcast_fusion
  (110 shorter events, 15.8 us)
Async XLA Ops:
  0.6 15.5 %copy-start = (bf16[1,2,192,1280]{3,2,1,0:T(8,128)(2,1)S(1)}, bf16[1,2,192,1280]{3,2,1,0:T(8,128)(2,1)}, u32[]{:S(2)}) copy-start(bf16[1,2,192,1280]{3,2,1,0:T(8,128)(2,1)} %param.10) | copy-start | bytes 2949124
  0.6 15.3 %copy-start.1 = (f32[1,1280]{1,0:T(1,128)S(1)}, f32[1,1280]{1,0:T(1,128)}, u32[]{:S(2)}) copy-start(f32[1,1280]{1,0:T(1,128)} %gain_ref.1) | copy-start | bytes 15364
  3.3 17.5 %all-to-all-start = ((s32[32,1,2]{2,1,0:T(1,128)}), s32[32,1,2]{2,1,0:T(1,128)S(1)}, u32[]{:S(2)}, u32[]{:S(2)}) async-start(s32[32,1,2]{2,1,0:T(1,128)} %bitcast.151), calls=%async_computation | async-start | bytes 32768 | tf_op jit(solution)/shard_map/all_to_all | solution.py:128
  26.3 13.9 %all-to-all-start.1 = ((bf16[32,2,2560]{2,1,0:T(2,128)(2,1)}), bf16[32,2,2560]{2,1,0:T(2,128)(2,1)S(1)}, u32[]{:S(2)}, u32[]{:S(2)}) async-start(bf16[32,2,2560]{2,1,0:T(2,128)(2,1)} %all_to_all.19), calls=%async_computation.1 | async-start | bytes 655360 | tf_op jit(solution)/shard_map/all_to_all | solution.py:170
  40.3 7.9 %collective-permute-start.2 = (bf16[64,2560]{1,0:T(8,128)(2,1)S(1)}, bf16[64,2560]{1,0:T(8,128)(2,1)S(1)}, u32[]{:S(2)}, u32[]{:S(2)}) collective-permute-start(bf16[64,2560]{1,0:T(8,128)(2,1)S(1)} %all_to_all.21), channel_id=1, source_target_pairs={{2,3},{3,2},{6,7},{7,6},{10,11},{11,10},{14,15},{15,14},{18,19},{1... | collective-permute-start | bytes 983048 | tf_op jit(solution)/shard_map/ppermute | solution.py:174
  41.0 9.0 %collective-permute-start.1 = (bf16[64,2560]{1,0:T(8,128)(2,1)S(1)}, bf16[64,2560]{1,0:T(8,128)(2,1)S(1)}, u32[]{:S(2)}, u32[]{:S(2)}) collective-permute-start(bf16[64,2560]{1,0:T(8,128)(2,1)S(1)} %all_to_all.21), channel_id=1, source_target_pairs={{0,3},{1,2},{4,7},{5,6},{8,11},{9,10},{12,15},{13,14},{16,19},{17,... | collective-permute-start | bytes 983048 | tf_op jit(solution)/shard_map/ppermute | solution.py:173
  45.0 5.4 %collective-permute-start = (bf16[64,2560]{1,0:T(8,128)(2,1)S(1)}, bf16[64,2560]{1,0:T(8,128)(2,1)S(1)}, u32[]{:S(2)}, u32[]{:S(2)}) collective-permute-start(bf16[64,2560]{1,0:T(8,128)(2,1)S(1)} %all_to_all.21), channel_id=1, source_target_pairs={{0,2},{1,3},{4,6},{5,7},{8,10},{9,11},{12,14},{13,15},{16,18},{17,... | collective-permute-start | bytes 983048 | tf_op jit(solution)/shard_map/ppermute | solution.py:172
  50.5 1.5 copy-start.4
  50.8 7.1 %slice-start.2 = ((s8[6553600]{0:T(1024)(128)(4,1)}), s8[4194304]{0:T(1024)(128)(4,1)S(1)}, s32[]{:S(2)}) async-start(s8[6553600]{0:T(1024)(128)(4,1)} %bitcast.155), calls=%async_computation.4 | async-start | bytes 8388608
  52.0 5.9 %slice-start.3 = ((s8[6553600]{0:T(1024)(128)(4,1)}), s8[2359296]{0:T(1024)(128)(4,1)S(1)}, s32[]{:S(2)}) async-start(s8[6553600]{0:T(1024)(128)(4,1)} %bitcast.155), calls=%async_computation.5 | async-start | bytes 4718592
  60.7 2.0 %copy-start.3 = (bf16[384,1280]{1,0:T(8,128)(2,1)}, bf16[384,1280]{1,0:T(8,128)(2,1)S(1)}, u32[]{:S(2)}) copy-start(bf16[384,1280]{1,0:T(8,128)(2,1)S(1)} %fusion.26) | copy-start | bytes 2949124
  62.6 9.2 %collective-permute-start.3 = (bf16[1200,1280]{1,0:T(8,128)(2,1)}, bf16[1200,1280]{1,0:T(8,128)(2,1)}, u32[]{:S(2)}, u32[]{:S(2)}) collective-permute-start(bf16[1200,1280]{1,0:T(8,128)(2,1)} %pad_maximum_fusion), channel_id=1, source_target_pairs={{2,0},{3,1},{6,4},{7,5},{10,8},{11,9},{14,12},{15,13},{18,16},{19,... | collective-permute-start | bytes 9216008 | tf_op jit(solution)/shard_map/ppermute | solution.py:294
  63.9 18.3 %collective-permute-start.4 = (bf16[384,1280]{1,0:T(8,128)(2,1)}, bf16[384,1280]{1,0:T(8,128)(2,1)S(1)}, u32[]{:S(2)}, u32[]{:S(2)}) collective-permute-start(bf16[384,1280]{1,0:T(8,128)(2,1)} %copy-done.3), channel_id=1, source_target_pairs={{2,1},{3,0},{6,5},{7,4},{10,9},{11,8},{14,13},{15,12},{18,17},{19,... | collective-permute-start | bytes 2949128 | tf_op jit(solution)/shard_map/ppermute | solution.py:286
  72.6 11.6 %slice-start = ((s8[6553600]{0:T(1024)(128)(4,1)}), s8[4194304]{0:T(1024)(128)(4,1)S(1)}, s32[]{:S(2)}) async-start(s8[6553600]{0:T(1024)(128)(4,1)} %bitcast.153), calls=%async_computation.2 | async-start | bytes 8388608
  82.2 1.9 %slice-start.1 = ((s8[6553600]{0:T(1024)(128)(4,1)}), s8[2359296]{0:T(1024)(128)(4,1)S(1)}, s32[]{:S(2)}) async-start(s8[6553600]{0:T(1024)(128)(4,1)} %bitcast.153), calls=%async_computation.3 | async-start | bytes 4718592
  84.0 1.5 copy-start.5
  91.8 1.5 copy-start.2
  94.6 39.7 %collective-permute-start.6 = (bf16[2,640,512]{2,1,0:T(8,128)(2,1)S(1)}, bf16[2,640,512]{2,1,0:T(8,128)(2,1)S(1)}, u32[]{:S(2)}, u32[]{:S(2)}) collective-permute-start(bf16[2,640,512]{2,1,0:T(8,128)(2,1)S(1)} %convolution_convert_fusion.3), channel_id=1, source_target_pairs={{0,8},{4,12},{8,0},{12,4},{16,24},{20,28},{24,16},{28,20},{32,40},... | collective-permute-start | bytes 3932168 | tf_op jit(solution)/shard_map/ppermute | solution.py:229
  97.1 36.8 %collective-permute-start.7 = (bf16[2,640,512]{2,1,0:T(8,128)(2,1)S(1)}, bf16[2,640,512]{2,1,0:T(8,128)(2,1)S(1)}, u32[]{:S(2)}, u32[]{:S(2)}) collective-permute-start(bf16[2,640,512]{2,1,0:T(8,128)(2,1)S(1)} %convolution_convert_fusion.4), channel_id=1, source_target_pairs={{0,24},{4,28},{8,16},{12,20},{16,8},{20,12},{24,0},{28,4},{32,56},... | collective-permute-start | bytes 3932168 | tf_op jit(solution)/shard_map/ppermute | solution.py:229
  100.1 29.9 %collective-permute-start.9 = (bf16[2,640,512]{2,1,0:T(8,128)(2,1)S(1)}, bf16[2,640,512]{2,1,0:T(8,128)(2,1)S(1)}, u32[]{:S(2)}, u32[]{:S(2)}) collective-permute-start(bf16[2,640,512]{2,1,0:T(8,128)(2,1)S(1)} %convolution_convert_fusion.6), channel_id=1, source_target_pairs={{0,96},{4,100},{8,104},{12,108},{16,112},{20,116},{24,120},{28,124... | collective-permute-start | bytes 3932168 | tf_op jit(solution)/shard_map/ppermute | solution.py:229
  104.8 28.5 %collective-permute-start.8 = (bf16[2,640,512]{2,1,0:T(8,128)(2,1)}, bf16[2,640,512]{2,1,0:T(8,128)(2,1)S(1)}, u32[]{:S(2)}, u32[]{:S(2)}) collective-permute-start(bf16[2,640,512]{2,1,0:T(8,128)(2,1)} %convolution_convert_fusion.5), channel_id=1, source_target_pairs={{0,32},{4,36},{8,40},{12,44},{16,48},{20,52},{24,56},{28,60},{32,0... | collective-permute-start | bytes 3932168 | tf_op jit(solution)/shard_map/ppermute | solution.py:229
  105.8 32.0 %collective-permute-start.5 = (bf16[2,640,512]{2,1,0:T(8,128)(2,1)S(1)}, bf16[2,640,512]{2,1,0:T(8,128)(2,1)S(1)}, u32[]{:S(2)}, u32[]{:S(2)}) collective-permute-start(bf16[2,640,512]{2,1,0:T(8,128)(2,1)S(1)} %convolution_convert_fusion.2), channel_id=1, source_target_pairs={{0,4},{4,0},{8,12},{12,8},{16,20},{20,16},{24,28},{28,24},{32,36},... | collective-permute-start | bytes 3932168 | tf_op jit(solution)/shard_map/ppermute | solution.py:229
  134.9 13.4 %collective-permute-start.14 = (bf16[2,320,512]{2,1,0:T(8,128)(2,1)S(1)}, bf16[2,320,512]{2,1,0:T(8,128)(2,1)S(1)}, u32[]{:S(2)}, u32[]{:S(2)}) collective-permute-start(bf16[2,320,512]{2,1,0:T(8,128)(2,1)S(1)} %add_convert_fusion.2), channel_id=1, source_target_pairs={{0,4},{4,0},{8,12},{12,8},{16,20},{20,16},{24,28},{28,24},{32,36},... | collective-permute-start | bytes 1966088 | tf_op jit(solution)/shard_map/ppermute | solution.py:229
  135.8 12.9 %collective-permute-start.13 = (bf16[2,320,512]{2,1,0:T(8,128)(2,1)S(1)}, bf16[2,320,512]{2,1,0:T(8,128)(2,1)S(1)}, u32[]{:S(2)}, u32[]{:S(2)}) collective-permute-start(bf16[2,320,512]{2,1,0:T(8,128)(2,1)S(1)} %add_convert_fusion.5), channel_id=1, source_target_pairs={{0,32},{4,36},{8,40},{12,44},{16,48},{20,52},{24,56},{28,60},{32,0... | collective-permute-start | bytes 1966088 | tf_op jit(solution)/shard_map/ppermute | solution.py:229
  136.3 16.8 %collective-permute-start.11 = (bf16[2,320,512]{2,1,0:T(8,128)(2,1)S(1)}, bf16[2,320,512]{2,1,0:T(8,128)(2,1)S(1)}, u32[]{:S(2)}, u32[]{:S(2)}) collective-permute-start(bf16[2,320,512]{2,1,0:T(8,128)(2,1)S(1)} %add_convert_fusion.3), channel_id=1, source_target_pairs={{0,8},{4,12},{8,0},{12,4},{16,24},{20,28},{24,16},{28,20},{32,40},... | collective-permute-start | bytes 1966088 | tf_op jit(solution)/shard_map/ppermute | solution.py:229
  136.9 15.5 %collective-permute-start.12 = (bf16[2,320,512]{2,1,0:T(8,128)(2,1)S(1)}, bf16[2,320,512]{2,1,0:T(8,128)(2,1)S(1)}, u32[]{:S(2)}, u32[]{:S(2)}) collective-permute-start(bf16[2,320,512]{2,1,0:T(8,128)(2,1)S(1)} %add_convert_fusion.4), channel_id=1, source_target_pairs={{0,24},{4,28},{8,16},{12,20},{16,8},{20,12},{24,0},{28,4},{32,56},... | collective-permute-start | bytes 1966088 | tf_op jit(solution)/shard_map/ppermute | solution.py:229
  138.3 16.9 %collective-permute-start.10 = (bf16[2,320,512]{2,1,0:T(8,128)(2,1)S(1)}, bf16[2,320,512]{2,1,0:T(8,128)(2,1)S(1)}, u32[]{:S(2)}, u32[]{:S(2)}) collective-permute-start(bf16[2,320,512]{2,1,0:T(8,128)(2,1)S(1)} %add_convert_fusion.1), channel_id=1, source_target_pairs={{0,96},{4,100},{8,104},{12,108},{16,112},{20,116},{24,120},{28,124... | collective-permute-start | bytes 1966088 | tf_op jit(solution)/shard_map/ppermute | solution.py:229
  149.5 15.2 %collective-permute-start.19 = (bf16[2,160,1024]{2,1,0:T(8,128)(2,1)S(1)}, bf16[2,160,1024]{2,1,0:T(8,128)(2,1)S(1)}, u32[]{:S(2)}, u32[]{:S(2)}) collective-permute-start(bf16[2,160,1024]{2,1,0:T(8,128)(2,1)S(1)} %pad_maximum_fusion.3), channel_id=1, source_target_pairs={{0,24},{4,28},{8,16},{12,20},{16,8},{20,12},{24,0},{28,4},{32,56},... | collective-permute-start | bytes 1966088 | tf_op jit(solution)/shard_map/ppermute | solution.py:229
  152.7 8.4 %collective-permute-start.20 = (bf16[2,160,512]{2,1,0:T(8,128)(2,1)S(1)}, bf16[2,160,512]{2,1,0:T(8,128)(2,1)S(1)}, u32[]{:S(2)}, u32[]{:S(2)}) collective-permute-start(bf16[2,160,512]{2,1,0:T(8,128)(2,1)S(1)} %add_convert_fusion.8), channel_id=1, source_target_pairs={{0,96},{4,100},{8,104},{12,108},{16,112},{20,116},{24,120},{28,124... | collective-permute-start | bytes 983048 | tf_op jit(solution)/shard_map/ppermute | solution.py:229
  153.5 11.9 %collective-permute-start.18 = (bf16[2,160,512]{2,1,0:T(8,128)(2,1)S(1)}, bf16[2,160,512]{2,1,0:T(8,128)(2,1)S(1)}, u32[]{:S(2)}, u32[]{:S(2)}) collective-permute-start(bf16[2,160,512]{2,1,0:T(8,128)(2,1)S(1)} %add_convert_fusion.7), channel_id=1, source_target_pairs={{0,4},{4,0},{8,12},{12,8},{16,20},{20,16},{24,28},{28,24},{32,36},... | collective-permute-start | bytes 983048 | tf_op jit(solution)/shard_map/ppermute | solution.py:229
  155.6 11.5 %collective-permute-start.17 = (bf16[2,160,512]{2,1,0:T(8,128)(2,1)S(1)}, bf16[2,160,512]{2,1,0:T(8,128)(2,1)S(1)}, u32[]{:S(2)}, u32[]{:S(2)}) collective-permute-start(bf16[2,160,512]{2,1,0:T(8,128)(2,1)S(1)} %add_convert_fusion.6), channel_id=1, source_target_pairs={{0,32},{4,36},{8,40},{12,44},{16,48},{20,52},{24,56},{28,60},{32,0... | collective-permute-start | bytes 983048 | tf_op jit(solution)/shard_map/ppermute | solution.py:229
  155.9 19.2 %collective-permute-start.15 = (bf16[384,1280]{1,0:T(8,128)(2,1)S(1)}, bf16[384,1280]{1,0:T(8,128)(2,1)S(1)}, u32[]{:S(2)}, u32[]{:S(2)}) collective-permute-start(bf16[384,1280]{1,0:T(8,128)(2,1)S(1)} %fusion.29.mine_ref), channel_id=1, source_target_pairs={{0,1},{1,0},{4,5},{5,4},{8,9},{9,8},{12,13},{13,12},{16,17},{17,16... | collective-permute-start | bytes 2949128 | tf_op jit(solution)/shard_map/ppermute | solution.py:310
  161.1 19.0 %collective-permute-start.16 = (bf16[384,1280]{1,0:T(8,128)(2,1)S(1)}, bf16[384,1280]{1,0:T(8,128)(2,1)S(1)}, u32[]{:S(2)}, u32[]{:S(2)}) collective-permute-start(bf16[384,1280]{1,0:T(8,128)(2,1)S(1)} %shard_map.96), channel_id=1, source_target_pairs={{0,2},{1,3},{4,6},{5,7},{8,10},{9,11},{12,14},{13,15},{16,18},{17,... | collective-permute-start | bytes 2949128 | tf_op jit(solution)/shard_map/ppermute | solution.py:311
  165.0 7.2 %collective-permute-start.23 = (bf16[2,80,1024]{2,1,0:T(8,128)(2,1)S(1)}, bf16[2,80,1024]{2,1,0:T(8,128)(2,1)S(1)}, u32[]{:S(2)}, u32[]{:S(2)}) collective-permute-start(bf16[2,80,1024]{2,1,0:T(8,128)(2,1)S(1)} %pad_maximum_fusion.4), channel_id=1, source_target_pairs={{0,8},{4,12},{8,0},{12,4},{16,24},{20,28},{24,16},{28,20},{32,40},... | collective-permute-start | bytes 983048 | tf_op jit(solution)/shard_map/ppermute | solution.py:229
  166.0 10.2 %collective-permute-start.22 = (bf16[2,80,1024]{2,1,0:T(8,128)(2,1)S(1)}, bf16[2,80,1024]{2,1,0:T(8,128)(2,1)S(1)}, u32[]{:S(2)}, u32[]{:S(2)}) collective-permute-start(bf16[2,80,1024]{2,1,0:T(8,128)(2,1)S(1)} %pad_maximum_fusion.5), channel_id=1, source_target_pairs={{0,96},{4,100},{8,104},{12,108},{16,112},{20,116},{24,120},{28,124... | collective-permute-start | bytes 983048 | tf_op jit(solution)/shard_map/ppermute | solution.py:229
  167.4 11.3 %collective-permute-start.21 = (bf16[2,80,512]{2,1,0:T(8,128)(2,1)S(1)}, bf16[2,80,512]{2,1,0:T(8,128)(2,1)S(1)}, u32[]{:S(2)}, u32[]{:S(2)}) collective-permute-start(bf16[2,80,512]{2,1,0:T(8,128)(2,1)S(1)} %add_convert_fusion.11), channel_id=1, source_target_pairs={{0,24},{4,28},{8,16},{12,20},{16,8},{20,12},{24,0},{28,4},{32,56},... | collective-permute-start | bytes 491528 | tf_op jit(solution)/shard_map/ppermute | solution.py:229
  175.7 7.2 %collective-permute-start.24 = (bf16[2,40,1024]{2,1,0:T(8,128)(2,1)S(1)}, bf16[2,40,1024]{2,1,0:T(8,128)(2,1)S(1)}, u32[]{:S(2)}, u32[]{:S(2)}) collective-permute-start(bf16[2,40,1024]{2,1,0:T(8,128)(2,1)S(1)} %pad_maximum_fusion.6), channel_id=1, source_target_pairs={{0,4},{4,0},{8,12},{12,8},{16,20},{20,16},{24,28},{28,24},{32,36},... | collective-permute-start | bytes 491528 | tf_op jit(solution)/shard_map/ppermute | solution.py:229
  176.8 6.8 %collective-permute-start.25 = (bf16[2,40,1024]{2,1,0:T(8,128)(2,1)S(1)}, bf16[2,40,1024]{2,1,0:T(8,128)(2,1)S(1)}, u32[]{:S(2)}, u32[]{:S(2)}) collective-permute-start(bf16[2,40,1024]{2,1,0:T(8,128)(2,1)S(1)} %pad_maximum_fusion.7), channel_id=1, source_target_pairs={{0,32},{4,36},{8,40},{12,44},{16,48},{20,52},{24,56},{28,60},{32,0... | collective-permute-start | bytes 491528 | tf_op jit(solution)/shard_map/ppermute | solution.py:229
  178.9 5.2 %collective-permute-start.26 = (bf16[2,40,512]{2,1,0:T(8,128)(2,1)S(1)}, bf16[2,40,512]{2,1,0:T(8,128)(2,1)S(1)}, u32[]{:S(2)}, u32[]{:S(2)}) collective-permute-start(bf16[2,40,512]{2,1,0:T(8,128)(2,1)S(1)} %add_convert_fusion.21), channel_id=1, source_target_pairs={{0,8},{4,12},{8,0},{12,4},{16,24},{20,28},{24,16},{28,20},{32,40},... | collective-permute-start | bytes 245768 | tf_op jit(solution)/shard_map/ppermute | solution.py:229

commit v3 on v2

--- a/solution.py
+++ b/solution.py
@@ -58,12 +58,16 @@
     return lax.dot_general(a, b, (((ca,), (cb,)), ((), ())), preferred_element_type=jnp.float32)
 
 
-def finish_kernel(g_ref, mine_ref, other_ref, x_ref, gain_ref, out_ref):
+def finish_kernel(g_ref, mine_ref, other_ref, x_ref, *refs):
+    gain_refs, out_ref = refs[:-1], refs[-1]
+    gain = gain_refs[0][0:1, :].astype(jnp.float32)
+    for gain_ref in gain_refs[1:]:
+        gain = gain + gain_ref[0:1, :].astype(jnp.float32)
     x = x_ref[...].astype(jnp.float32)
     centered = x - jnp.mean(x, axis=-1, keepdims=True)
     rstd = lax.rsqrt(jnp.mean(centered * centered, axis=-1, keepdims=True) + 1e-05)
     xhat = centered * rstd
-    scaled = (mine_ref[...].astype(jnp.float32) + other_ref[...].astype(jnp.float32)) * gain_ref[...]
+    scaled = (mine_ref[...].astype(jnp.float32) + other_ref[...].astype(jnp.float32)) * gain
     out_ref[...] = (
         g_ref[...].astype(jnp.float32)
         + rstd
@@ -75,20 +79,25 @@
     ).astype(jnp.bfloat16)
 
 
-def finish(incoming, mine, other, x, gain, tile):
-    rows, width = incoming.shape
-    wide = pl.BlockSpec((tile, width), lambda i: (i, 0))
+def finish(operands, gains, rows, tile):
+    width = operands[0][0].shape[1]
+    wide = [
+        pl.BlockSpec((tile, width), lambda i, k=start // tile: (k + i, 0)) for _, start in operands
+    ]
+    flat = [
+        pl.BlockSpec((size, width), lambda i, k=start // size: (k, 0)) for _, start, size in gains
+    ]
     return pl.pallas_call(
         finish_kernel,
         grid=(rows // tile,),
-        in_specs=[wide, wide, wide, wide, pl.BlockSpec((1, width), lambda i: (0, 0))],
-        out_specs=wide,
+        in_specs=wide + flat,
+        out_specs=pl.BlockSpec((tile, width), lambda i: (i, 0)),
         out_shape=jax.ShapeDtypeStruct((rows, width), jnp.bfloat16),
         compiler_params=pltpu.CompilerParams(vmem_limit_bytes=8 * 1024 * 1024),
         cost_estimate=pl.CostEstimate(
             flops=20 * rows * width, bytes_accessed=10 * rows * width, transcendentals=0
         ),
-    )(incoming, mine, other, x, gain)
+    )(*[array for array, _ in operands], *[array for array, _, _ in gains])
 
 
 def ask_kernel(ids_ref, frames_ref, slots_ref, out_ref, *, seq_dev):
@@ -128,46 +137,12 @@
     return lax.all_to_all(requests, "dp", 0, 0, tiled=True)
 
 
-def pick_kernel(ids_ref, asked_ref, held_ref, out_ref):
-    peers, per = asked_ref.shape
-    seq_dev = held_ref.shape[1]
-    row = lax.broadcasted_iota(jnp.int32, (peers * per, 1), 0)
-    spread = lax.broadcasted_iota(jnp.int32, (peers * per, peers), 1) == row // per
-    asked = dot(
-        spread.astype(jnp.float32).astype(jnp.bfloat16),
-        asked_ref[...].astype(jnp.float32).astype(jnp.bfloat16),
-        1,
-        0,
-    )
-    place = jnp.zeros((peers * per, 1), jnp.float32)
-    for k in range(per):
-        place = jnp.where(row % per == k, asked[:, k : k + 1], place)
-    positions = lax.broadcasted_iota(jnp.int32, (peers * per, seq_dev), 1) + 1
-    pick = (place == positions.astype(jnp.float32)).astype(jnp.float32).astype(jnp.bfloat16)
-    out_ref[...] = dot(pick, held_ref[0], 1, 0).astype(jnp.bfloat16)
-
-
-def pick_rows(asked, llm_grad, ids):
+def fetch_tokens(llm_grad, asked, cap, sec, ten, rep, peers):
     seq_dev, width = llm_grad.shape[1:]
-    return pl.pallas_call(
-        pick_kernel,
-        grid_spec=pltpu.PrefetchScalarGridSpec(
-            num_scalar_prefetch=1,
-            grid=(1,),
-            in_specs=[
-                pl.BlockSpec(asked.shape, lambda i, *_: (0, 0)),
-                pl.BlockSpec((1, seq_dev, width), lambda i, ids: (ids[0], 0, 0)),
-            ],
-            out_specs=pl.BlockSpec((asked.size, width), lambda i, *_: (0, 0)),
-        ),
-        out_shape=jax.ShapeDtypeStruct((asked.size, width), jnp.bfloat16),
-    )(ids, asked, llm_grad)
-
-
-def fetch_tokens(llm_grad, asked, cap, ids, ten, rep, peers):
-    width = llm_grad.shape[2]
     per = -(-cap // peers)
-    got = lax.all_to_all(pick_rows(asked, llm_grad, ids), "dp", 0, 0, tiled=True)
+    pick = (asked.reshape(-1)[:, None] == jnp.arange(1, seq_dev + 1)[None, :]).astype(jnp.bfloat16)
+    held = lax.dynamic_index_in_dim(llm_grad, sec, 0, keepdims=False)
+    got = lax.all_to_all(dot(pick, held, 1, 0).astype(jnp.bfloat16), "dp", 0, 0, tiled=True)
     both = ("section", "tensor")
     first_own = lax.ppermute(got, both, [(0, 2), (1, 3)])
     first_other = lax.ppermute(got, both, [(0, 3), (1, 2)])
@@ -259,7 +234,7 @@
     ids = jnp.stack([sec, rep])
     asked = ask_tokens(llm_grad.shape[1], slots, frames, ids, peers)
     normed, asked = lax.optimization_barrier((normed, asked))
-    upstream, got = fetch_tokens(llm_grad, asked, slots.shape[1], ids, ten, rep, peers)
+    upstream, got = fetch_tokens(llm_grad, asked, slots.shape[1], sec, ten, rep, peers)
     activ, slope = lax.optimization_barrier(gelu_and_slope(dot(normed, weight_in, 1, 0)))
 
     order = from_code(to_code(rep) ^ jnp.arange(peers))
@@ -284,19 +259,13 @@
     d_pre = pre_gradient(upstream)
     partial = dot(d_pre, weight_in, 1, 1).astype(jnp.bfloat16)
     other = lax.ppermute(partial, both, [(2, 1), (3, 0)])
-    terms, rest = [], ln_gain
-    for _ in range(3):
-        term = lax.reduce_precision(rest, exponent_bits=8, mantissa_bits=7)
-        terms.append(jnp.broadcast_to(term, (16, width)).astype(jnp.bfloat16))
-        rest = rest - term
-    terms = after(jnp.concatenate(terms), normed)
-    packed = jnp.concatenate([partial, upstream, x, terms])
-    packed = lax.ppermute(packed, "section", [(1, 0)])
-    mine, passed, later_x = (packed[k * rows : (k + 1) * rows] for k in range(3))
-    later_gain = sum(
-        packed[3 * rows + 16 * k : 3 * rows + 16 * k + 1].astype(jnp.float32) for k in range(3)
-    )
-    grad_last = finish(passed, mine, other, later_x, later_gain, tok_rows // 2)
+    mine, passed, later_x, later_gain = (
+        lax.ppermute(after(value, partial), "section", [(1, 0)])
+        for value in (partial, upstream, x, ln_gain)
+    )
+    grad_last = finish(
+        [(passed, 0), (mine, 0), (other, 0), (later_x, 0)], [(later_gain, 0, 1)], rows, tok_rows // 2
+    )
 
     incoming = jnp.where(sec == 1, upstream, grad_last)
     d_pre = pre_gradient(incoming)
@@ -314,7 +283,9 @@
     reduced, partial, (other, returned) = reduce_weight_grads(
         jnp.stack([normed_t, incoming_t]), jnp.stack([d_pre, activ]), partial_here, exchange
     )
-    grad_here = finish(incoming, partial, other, x, ln_gain, tok_rows // 2)
+    grad_here = finish(
+        [(incoming, 0), (partial, 0), (other, 0), (x, 0)], [(ln_gain, 0, 1)], rows, tok_rows // 2
+    )
     results = jnp.where(sec == 1, returned, grad_here)
     return (
         results.reshape(1, micro_count, tok_rows, width),

time: 186 us -> 191 us (1.027)
  matrix products: 43.7 us -> 50.1 us
  local copies, waits for them, and re-layouts: 10.9 us -> 6.61 us
  starting transfers between devices: 47.5 us -> 51.2 us
    dot_general x9 -> x10, matrix products: 30.1 us -> 35.5 us  [dot(): lax.dot_general(a, b, (((ca,), (cb,)), ((), ())), preferred_element_type=...]
    ppermute x1 -> x4, starting transfers between devices: 1.28 us -> 5.34 us  [per_device(): lax.ppermute(after(value, partial), 'section', [(1, 0)])]
    ppermute x1, waiting for transfers between devices: 7.52 us -> 10 us  [per_device(): other = lax.ppermute(partial, both, [(2, 1), (3, 0)])]
    slice x1 -> x0, local copies, waits for them, and re-layouts: 2.14 us -> none  [per_device(): mine, passed, later_x = (packed[k * rows:(k + 1) * rows] for k in range(3))]
    concatenate x2 -> x0, other arithmetic: 1.94 us -> none  [the longest x1 1.93 us: per_device(): packed = jnp.concatenate([partial, upstream, x, terms])]
    pallas_call x3 -> x2, Pallas kernels: 6.34 us -> 5.41 us  [finish(): pl.pallas_call(finish_kernel, grid=(rows // tile,), in_specs=wide + flat,...]
    ppermute x1 -> x4, waiting for transfers between devices: 6.4 us -> 5.99 us  [per_device(): lax.ppermute(after(value, partial), 'section', [(1, 0)])]
  transfers between devices with their start and end apart: 29 -> 32, of which waited for: 14 -> 14; matrix products, arithmetic and copies ran while one was open for 20% -> 19% of each run, Pallas kernels for 1% -> 1%
where the time goes in v3:
time: 191 us; the launch traced here: 190 us
  waiting for transfers between devices  65.3 us (34%)
  starting transfers between devices  51.2 us (27%)
  matrix products  50.1 us (26%)
  other arithmetic  7.9 us (4%)
  Pallas kernels  7.49 us (4%)
  local copies, waits for them, and re-layouts  6.61 us (3%)
    ppermute x20, waiting for transfers between devices, reduce_weight_grads(): piece = lax.ppermute(last, 'dp', neighbour_pairs(ORDERS[streams[0]][t]))  39.9 us
    dot_general x10, matrix products, dot(): lax.dot_general(a, b, (((ca,), (cb,)), ((), ())), preferred_element_type=...  35.5 us
    ppermute x20, starting transfers between devices, reduce_weight_grads(): piece = lax.ppermute(last, 'dp', neighbour_pairs(ORDERS[streams[0]][t]))  22 us
    dot_general x30, matrix products, group(): lax.dot_general(lefts[i][:, lo:hi], right[:, :, i * span:(i + 1) * span],...  14.6 us
    ppermute x1, waiting for transfers between devices, per_device(): other = lax.ppermute(partial, both, [(2, 1), (3, 0)])  10 us
    all_to_all x1, starting transfers between devices, ask_tokens(): return lax.all_to_all(requests, 'dp', 0, 0, tiled=True)  9.35 us
    ppermute x4, waiting for transfers between devices, per_device(): lax.ppermute(after(value, partial), 'section', [(1, 0)])  5.99 us
    pallas_call x2, Pallas kernels, finish(): pl.pallas_call(finish_kernel, grid=(rows // tile,), in_specs=wide + flat,...  5.41 us
  transfers between devices with their start and end apart: 32, of which 14 were waited for; matrix products, arithmetic and copies ran while one was open for 19% of the time, Pallas kernels for 1%

profile of v3, /device:TPU:0, one launch (start us, length us, event | category | flops | bytes accessed | tf_op | source)
XLA Modules:
  0.0 190.0 jit_solution(13134757234477084047)
XLA Ops:
  0.7 0.6 pad_add_fusion.ids_ref
  1.3 2.1 %shard_map.94 = s32[32,2]{1,0:T(8,128)} custom-call(s32[2]{0:T(128)} %pad_add_fusion.ids_ref, s32[2,2]{1,0:T(2,128)} %frames_ref.1, s32[2,48]{1,0:T(2,128)} %slots_ref.1), custom_call_target="tpu_custom_call" | custom-call | tf_op jit(solution)/shard_map/pallas_call | solution.py:127
  3.4 9.3 %all-to-all-start = ((s32[32,1,2]{2,1,0:T(1,128)}), s32[32,1,2]{2,1,0:T(1,128)S(1)}, u32[]{:S(2)}, u32[]{:S(2)}) async-start(s32[32,1,2]{2,1,0:T(1,128)} %bitcast.154), calls=%async_computation | async-start | bytes 32768 | tf_op jit(solution)/shard_map/all_to_all | solution.py:137
  12.8 1.4 convert_reduce_fusion
  14.2 1.6 fusion.33
  16.6 4.3 %all-to-all-done = s32[32,1,2]{2,1,0:T(1,128)S(1)} async-done(((s32[32,1,2]{2,1,0:T(1,128)}), s32[32,1,2]{2,1,0:T(1,128)S(1)}, u32[]{:S(2)}, u32[]{:S(2)}) %all-to-all-start) | async-done | bytes 288 | tf_op jit(solution)/shard_map/all_to_all | solution.py:137
  21.5 0.9 all_to_all.19
  22.3 4.0 %all-to-all-start.1 = ((bf16[32,2,2560]{2,1,0:T(2,128)(2,1)}), bf16[32,2,2560]{2,1,0:T(2,128)(2,1)S(1)}, u32[]{:S(2)}, u32[]{:S(2)}) async-start(bf16[32,2,2560]{2,1,0:T(2,128)(2,1)} %all_to_all.19), calls=%async_computation.1 | async-start | bytes 655360 | tf_op jit(solution)/shard_map/all_to_all | solution.py:145
  26.4 8.7 %add_convert_fusion = (bf16[384,2560]{1,0:T(8,128)(2,1)}, bf16[384,2560]{1,0:T(8,128)(2,1)}) fusion(bf16[384,1280]{1,0:T(8,128)(2,1)S(1)} %multiply_convert_fusion.1, bf16[1,1280,2560]{2,1,0:T(8,128)(2,1)} %param.12), kind=kOutput, calls=%fused_computation.25 | convolution fusion | flops 2534277120 | bytes 11468800 | tf_op jit(solution)/shard_map/dot_general | solution.py:58
  35.0 1.1 all-to-all-done.1
  36.3 0.7 collective-permute-start.2
  37.0 4.0 %collective-permute-start.1 = (bf16[64,2560]{1,0:T(8,128)(2,1)S(1)}, bf16[64,2560]{1,0:T(8,128)(2,1)S(1)}, u32[]{:S(2)}, u32[]{:S(2)}) collective-permute-start(bf16[64,2560]{1,0:T(8,128)(2,1)S(1)} %all_to_all.21), channel_id=1, source_target_pairs={{0,3},{1,2},{4,7},{5,6},{8,11},{9,10},{12,15},{13,14},{16,19},{17,... | collective-permute-start | bytes 983048 | tf_op jit(solution)/shard_map/ppermute | solution.py:148
  40.9 1.3 collective-permute-start
  42.3 2.9 %fusion.24 = bf16[1280,384]{1,0:T(8,128)(2,1)} fusion(bf16[384,1280]{1,0:T(8,128)(2,1)S(1)} %multiply_convert_fusion.1, s32[1280]{0:T(1024)S(1)} %add.384), kind=kOutput, calls=%fused_computation.42 | convolution fusion | flops 1260421120 | bytes 1971200 | tf_op jit(solution)/shard_map/dot_general | solution.py:58
  45.2 0.8 collective-permute-done.1
  46.8 1.0 pad_maximum_fusion
  48.3 6.2 %fusion.16 = bf16[384,2560]{1,0:T(8,128)(2,1)S(1)} fusion(bf16[384,2560]{1,0:T(8,128)(2,1)S(1)} %copy-done.6, bf16[384,1280]{1,0:T(8,128)(2,1)} %pad_maximum_fusion, bf16[1,2560,1280]{2,1,0:T(8,128)(2,1)} %param.13), kind=kOutput, calls=%fused_computation.23 | convolution fusion | flops 2519531520 | bytes 11468800 | tf_op jit(solution)/shard_map/dot_general | solution.py:58
  54.5 3.7 %fusion.26 = bf16[384,1280]{1,0:T(8,128)(2,1)} fusion(bf16[384,2560]{1,0:T(8,128)(2,1)S(1)} %fusion.16, bf16[1,1280,2560]{2,1,0:T(8,128)(2,1)S(1)} %bitcast.157), kind=kOutput, calls=%fused_computation.44 | convolution fusion | flops 2517073920 | bytes 9502720 | tf_op jit(solution)/shard_map/dot_general | solution.py:58
  58.2 1.3 collective-permute-start.3
  59.5 1.3 collective-permute-start.4
  60.8 1.3 collective-permute-start.6
  62.1 1.3 collective-permute-start.5
  63.4 1.5 collective-permute-start.7
  64.9 6.0 %collective-permute-done.7.refs_0_ = f32[1,1280]{1,0:T(1,128)S(1)} collective-permute-done((f32[1,1280]{1,0:T(1,128)S(1)}, f32[1,1280]{1,0:T(1,128)S(1)}, u32[]{:S(2)}, u32[]{:S(2)}) %collective-permute-start.7) | collective-permute-done | bytes 5152 | tf_op jit(solution)/shard_map/ppermute | solution.py:263
  70.9 10.0 %collective-permute-done.5.other_ref = bf16[384,1280]{1,0:T(8,128)(2,1)} collective-permute-done((bf16[384,1280]{1,0:T(8,128)(2,1)}, bf16[384,1280]{1,0:T(8,128)(2,1)}, u32[]{:S(2)}, u32[]{:S(2)}) %collective-permute-start.5) | collective-permute-done | bytes 983072 | tf_op jit(solution)/shard_map/ppermute | solution.py:261
  80.9 3.7 %shard_map.95 = bf16[384,1280]{1,0:T(8,128)(2,1)S(1)} custom-call(bf16[384,1280]{1,0:T(8,128)(2,1)S(1)} %collective-permute-done.3.g_ref, bf16[384,1280]{1,0:T(8,128)(2,1)} %collective-permute-done.4.mine_ref, bf16[384,1280]{1,0:T(8,128)(2,1)} %collective-permute-done.5.other_ref, bf16[384,1280]{1,0:T(8,128)(2,1)} %collective-permute-done.6.x_ref, ...), custom_call_target="tpu_custom_call" | custom-call | flops 9830400 | bytes 4915200 | tf_op jit(solution)/shard_map/pallas_call | solution.py:90
  84.8 1.4 copy-done.7
  86.2 5.6 %fusion.19 = bf16[384,2560]{1,0:T(8,128)(2,1)S(1)} fusion(bf16[384,2560]{1,0:T(8,128)(2,1)S(1)} %copy-done.7, bf16[384,1280]{1,0:T(8,128)(2,1)S(1)} %broadcast_select_fusion.1.g_ref, bf16[1,2560,1280]{2,1,0:T(8,128)(2,1)} %param.13), kind=kOutput, calls=%fused_computation.24 | convolution fusion | flops 2519531520 | bytes 11468800 | tf_op jit(solution)/shard_map/dot_general | solution.py:58
  91.8 1.9 %fusion.25 = bf16[1280,384]{1,0:T(8,128)(2,1)S(1)} fusion(bf16[384,1280]{1,0:T(8,128)(2,1)S(1)} %broadcast_select_fusion.1.g_ref, s32[1280]{0:T(1024)S(1)} %add.384), kind=kOutput, calls=%fused_computation.43 | convolution fusion | flops 1260421120 | bytes 1971200 | tf_op jit(solution)/shard_map/dot_general | solution.py:58
  95.6 1.3 copy-done.5
  97.3 0.8 convolution_convert_fusion.4
  98.1 1.5 collective-permute-start.9
  99.7 0.8 convolution_convert_fusion.5
  100.5 2.1 %collective-permute-start.10 = (bf16[2,640,512]{2,1,0:T(8,128)(2,1)S(1)}, bf16[2,640,512]{2,1,0:T(8,128)(2,1)S(1)}, u32[]{:S(2)}, u32[]{:S(2)}) collective-permute-start(bf16[2,640,512]{2,1,0:T(8,128)(2,1)S(1)} %convolution_convert_fusion.5), channel_id=1, source_target_pairs={{0,24},{4,28},{8,16},{12,20},{16,8},{20,12},{24,0},{28,4},{32,56},... | collective-permute-start | bytes 3932168 | tf_op jit(solution)/shard_map/ppermute | solution.py:204
  102.7 1.9 %convolution_convert_fusion.7 = bf16[2,640,512]{2,1,0:T(8,128)(2,1)} fusion(bf16[2,384,512]{2,1,0:T(8,128)(2,1)S(1)} %get-tuple-element.74, bf16[1,1280,384]{2,1,0:T(8,128)(2,1)S(1)} %bitcast.111, bf16[1,1280,384]{2,1,0:T(8,128)(2,1)S(1)} %bitcast.121), kind=kOutput, calls=%fused_computation.61 | convolution fusion | flops 504463360 | bytes 4063232 | tf_op jit(solution)/shard_map/dot_general | solution.py:185
  104.6 2.7 %collective-permute-start.12 = (bf16[2,640,512]{2,1,0:T(8,128)(2,1)}, bf16[2,640,512]{2,1,0:T(8,128)(2,1)S(1)}, u32[]{:S(2)}, u32[]{:S(2)}) collective-permute-start(bf16[2,640,512]{2,1,0:T(8,128)(2,1)} %convolution_convert_fusion.7), channel_id=1, source_target_pairs={{0,96},{4,100},{8,104},{12,108},{16,112},{20,116},{24,120},{28,124... | collective-permute-start | bytes 3932168 | tf_op jit(solution)/shard_map/ppermute | solution.py:204
  107.3 2.0 %convolution_convert_fusion.6 = bf16[2,640,512]{2,1,0:T(8,128)(2,1)} fusion(bf16[2,384,512]{2,1,0:T(8,128)(2,1)S(1)} %get-tuple-element.75, bf16[2,1280,384]{2,1,0:T(8,128)(2,1)S(1)} %bitcast.145), kind=kOutput, calls=%fused_computation.60 | convolution fusion | flops 503971840 | bytes 3080192 | tf_op jit(solution)/shard_map/dot_general | solution.py:185
  109.5 0.8 convolution_convert_fusion.3
  110.3 1.3 collective-permute-start.8
  111.6 5.6 %fusion.29.mine_ref = bf16[384,1280]{1,0:T(8,128)(2,1)S(1)} fusion(bf16[384,2560]{1,0:T(8,128)(2,1)S(1)} %fusion.19, bf16[1,1280,2560]{2,1,0:T(8,128)(2,1)} %param.12), kind=kOutput, calls=%fused_computation.45 | convolution fusion | flops 2517073920 | bytes 9502720 | tf_op jit(solution)/shard_map/dot_general | solution.py:58
  117.2 17.6 %collective-permute-done.12 = bf16[2,640,512]{2,1,0:T(8,128)(2,1)S(1)} collective-permute-done((bf16[2,640,512]{2,1,0:T(8,128)(2,1)}, bf16[2,640,512]{2,1,0:T(8,128)(2,1)S(1)}, u32[]{:S(2)}, u32[]{:S(2)}) %collective-permute-start.12) | collective-permute-done | bytes 1310752 | tf_op jit(solution)/shard_map/ppermute | solution.py:204
  135.3 2.7 %collective-permute-done.11 = bf16[2,640,512]{2,1,0:T(8,128)(2,1)S(1)} collective-permute-done((bf16[2,640,512]{2,1,0:T(8,128)(2,1)}, bf16[2,640,512]{2,1,0:T(8,128)(2,1)S(1)}, u32[]{:S(2)}, u32[]{:S(2)}) %collective-permute-start.11) | collective-permute-done | bytes 1310752 | tf_op jit(solution)/shard_map/ppermute | solution.py:204
  139.5 0.9 collective-permute-start.17
  141.0 0.6 collective-permute-start.14
  141.6 0.9 collective-permute-start.15
  143.0 1.1 collective-permute-start.13
  144.1 9.0 %collective-permute-done.17 = bf16[2,320,512]{2,1,0:T(8,128)(2,1)S(1)} collective-permute-done((bf16[2,320,512]{2,1,0:T(8,128)(2,1)S(1)}, bf16[2,320,512]{2,1,0:T(8,128)(2,1)S(1)}, u32[]{:S(2)}, u32[]{:S(2)}) %collective-permute-start.17) | collective-permute-done | bytes 655392 | tf_op jit(solution)/shard_map/ppermute | solution.py:204
  154.4 1.2 collective-permute-start.22
  155.6 1.5 collective-permute-done.15
  157.4 0.8 collective-permute-start.23
  158.6 1.7 collective-permute-start.21
  161.0 1.9 %collective-permute-start.18 = (bf16[384,1280]{1,0:T(8,128)(2,1)S(1)}, bf16[384,1280]{1,0:T(8,128)(2,1)S(1)}, u32[]{:S(2)}, u32[]{:S(2)}) collective-permute-start(bf16[384,1280]{1,0:T(8,128)(2,1)S(1)} %fusion.29.mine_ref), channel_id=1, source_target_pairs={{0,1},{1,0},{4,5},{5,4},{8,9},{9,8},{12,13},{13,12},{16,17},{17,16... | collective-permute-start | bytes 2949128 | tf_op jit(solution)/shard_map/ppermute | solution.py:279
  162.9 2.9 %collective-permute-done.23 = bf16[2,160,512]{2,1,0:T(8,128)(2,1)S(1)} collective-permute-done((bf16[2,160,512]{2,1,0:T(8,128)(2,1)S(1)}, bf16[2,160,512]{2,1,0:T(8,128)(2,1)S(1)}, u32[]{:S(2)}, u32[]{:S(2)}) %collective-permute-start.23) | collective-permute-done | bytes 327712 | tf_op jit(solution)/shard_map/ppermute | solution.py:204
  165.8 1.3 collective-permute-start.19
  167.4 2.1 %collective-permute-done.22 = bf16[2,160,1024]{2,1,0:T(8,128)(2,1)S(1)} collective-permute-done((bf16[2,160,1024]{2,1,0:T(8,128)(2,1)S(1)}, bf16[2,160,1024]{2,1,0:T(8,128)(2,1)S(1)}, u32[]{:S(2)}, u32[]{:S(2)}) %collective-permute-start.22) | collective-permute-done | bytes 655392 | tf_op jit(solution)/shard_map/ppermute | solution.py:204
  170.8 1.1 collective-permute-start.25
  172.2 1.3 collective-permute-start.24
  173.5 3.6 %collective-permute-done.26 = bf16[2,80,1024]{2,1,0:T(8,128)(2,1)S(1)} collective-permute-done((bf16[2,80,1024]{2,1,0:T(8,128)(2,1)S(1)}, bf16[2,80,1024]{2,1,0:T(8,128)(2,1)S(1)}, u32[]{:S(2)}, u32[]{:S(2)}) %collective-permute-start.26) | collective-permute-done | bytes 327712 | tf_op jit(solution)/shard_map/ppermute | solution.py:204
  177.1 3.1 %collective-permute-done.18.other_ref = bf16[384,1280]{1,0:T(8,128)(2,1)S(1)} collective-permute-done((bf16[384,1280]{1,0:T(8,128)(2,1)S(1)}, bf16[384,1280]{1,0:T(8,128)(2,1)S(1)}, u32[]{:S(2)}, u32[]{:S(2)}) %collective-permute-start.18) | collective-permute-done | bytes 983072 | tf_op jit(solution)/shard_map/ppermute | solution.py:279
  181.9 1.8 collective-permute-start.28
  184.0 1.2 collective-permute-start.29
  185.2 1.7 shard_map.96
  187.0 1.0 broadcast_select_fusion
  189.2 0.8 slice_bitcast_fusion
  (109 shorter events, 15.8 us)
Async XLA Ops:
  0.6 20.6 %copy-start = (bf16[2,64,2560]{2,1,0:T(8,128)(2,1)S(1)}, bf16[2,64,2560]{2,1,0:T(8,128)(2,1)}, u32[]{:S(2)}) copy-start(bf16[2,64,2560]{2,1,0:T(8,128)(2,1)} %param.7) | copy-start | bytes 1966084
  0.6 15.5 %copy-start.2 = (bf16[1,2,192,1280]{3,2,1,0:T(8,128)(2,1)S(1)}, bf16[1,2,192,1280]{3,2,1,0:T(8,128)(2,1)}, u32[]{:S(2)}) copy-start(bf16[1,2,192,1280]{3,2,1,0:T(8,128)(2,1)} %param.10) | copy-start | bytes 2949124
  0.7 15.4 %copy-start.3 = (f32[1,1280]{1,0:T(1,128)S(1)}, f32[1,1280]{1,0:T(1,128)}, u32[]{:S(2)}) copy-start(f32[1,1280]{1,0:T(1,128)} %refs_0_.1) | copy-start | bytes 15364
  3.4 17.5 %all-to-all-start = ((s32[32,1,2]{2,1,0:T(1,128)}), s32[32,1,2]{2,1,0:T(1,128)S(1)}, u32[]{:S(2)}, u32[]{:S(2)}) async-start(s32[32,1,2]{2,1,0:T(1,128)} %bitcast.154), calls=%async_computation | async-start | bytes 32768 | tf_op jit(solution)/shard_map/all_to_all | solution.py:137
  22.3 13.8 %all-to-all-start.1 = ((bf16[32,2,2560]{2,1,0:T(2,128)(2,1)}), bf16[32,2,2560]{2,1,0:T(2,128)(2,1)S(1)}, u32[]{:S(2)}, u32[]{:S(2)}) async-start(bf16[32,2,2560]{2,1,0:T(2,128)(2,1)} %all_to_all.19), calls=%async_computation.1 | async-start | bytes 655360 | tf_op jit(solution)/shard_map/all_to_all | solution.py:145
  36.3 8.9 %collective-permute-start.2 = (bf16[64,2560]{1,0:T(8,128)(2,1)S(1)}, bf16[64,2560]{1,0:T(8,128)(2,1)S(1)}, u32[]{:S(2)}, u32[]{:S(2)}) collective-permute-start(bf16[64,2560]{1,0:T(8,128)(2,1)S(1)} %all_to_all.21), channel_id=1, source_target_pairs={{2,3},{3,2},{6,7},{7,6},{10,11},{11,10},{14,15},{15,14},{18,19},{1... | collective-permute-start | bytes 983048 | tf_op jit(solution)/shard_map/ppermute | solution.py:149
  37.0 9.0 %collective-permute-start.1 = (bf16[64,2560]{1,0:T(8,128)(2,1)S(1)}, bf16[64,2560]{1,0:T(8,128)(2,1)S(1)}, u32[]{:S(2)}, u32[]{:S(2)}) collective-permute-start(bf16[64,2560]{1,0:T(8,128)(2,1)S(1)} %all_to_all.21), channel_id=1, source_target_pairs={{0,3},{1,2},{4,7},{5,6},{8,11},{9,10},{12,15},{13,14},{16,19},{17,... | collective-permute-start | bytes 983048 | tf_op jit(solution)/shard_map/ppermute | solution.py:148
  40.9 5.4 %collective-permute-start = (bf16[64,2560]{1,0:T(8,128)(2,1)S(1)}, bf16[64,2560]{1,0:T(8,128)(2,1)S(1)}, u32[]{:S(2)}, u32[]{:S(2)}) collective-permute-start(bf16[64,2560]{1,0:T(8,128)(2,1)S(1)} %all_to_all.21), channel_id=1, source_target_pairs={{0,2},{1,3},{4,6},{5,7},{8,10},{9,11},{12,14},{13,15},{16,18},{17,... | collective-permute-start | bytes 983048 | tf_op jit(solution)/shard_map/ppermute | solution.py:147
  46.4 1.9 %copy-start.6 = (bf16[384,2560]{1,0:T(8,128)(2,1)S(1)}, bf16[384,2560]{1,0:T(8,128)(2,1)}, u32[]{:S(2)}) copy-start(bf16[384,2560]{1,0:T(8,128)(2,1)} %get-tuple-element.42) | copy-start | bytes 5898244
  46.8 7.8 %slice-start = ((s8[6553600]{0:T(1024)(128)(4,1)}), s8[4194304]{0:T(1024)(128)(4,1)S(1)}, s32[]{:S(2)}) async-start(s8[6553600]{0:T(1024)(128)(4,1)} %bitcast.156), calls=%async_computation.2 | async-start | bytes 8388608
  48.3 6.2 %slice-start.1 = ((s8[6553600]{0:T(1024)(128)(4,1)}), s8[2359296]{0:T(1024)(128)(4,1)S(1)}, s32[]{:S(2)}) async-start(s8[6553600]{0:T(1024)(128)(4,1)} %bitcast.156), calls=%async_computation.3 | async-start | bytes 4718592
  58.2 12.7 %collective-permute-start.3 = (bf16[384,1280]{1,0:T(8,128)(2,1)}, bf16[384,1280]{1,0:T(8,128)(2,1)S(1)}, u32[]{:S(2)}, u32[]{:S(2)}) collective-permute-start(bf16[384,1280]{1,0:T(8,128)(2,1)} %pad_maximum_fusion), channel_id=1, source_target_pairs={{2,0},{3,1},{6,4},{7,5},{10,8},{11,9},{14,12},{15,13},{18,16},{19,... | collective-permute-start | bytes 2949128 | tf_op jit(solution)/shard_map/ppermute | solution.py:263
  59.5 11.4 %collective-permute-start.4 = (bf16[384,1280]{1,0:T(8,128)(2,1)}, bf16[384,1280]{1,0:T(8,128)(2,1)}, u32[]{:S(2)}, u32[]{:S(2)}) collective-permute-start(bf16[384,1280]{1,0:T(8,128)(2,1)} %fusion.26), channel_id=1, source_target_pairs={{2,0},{3,1},{6,4},{7,5},{10,8},{11,9},{14,12},{15,13},{18,16},{19,... | collective-permute-start | bytes 2949128 | tf_op jit(solution)/shard_map/ppermute | solution.py:263
  60.8 10.1 %collective-permute-start.6 = (bf16[384,1280]{1,0:T(8,128)(2,1)S(1)}, bf16[384,1280]{1,0:T(8,128)(2,1)}, u32[]{:S(2)}, u32[]{:S(2)}) collective-permute-start(bf16[384,1280]{1,0:T(8,128)(2,1)S(1)} %bitcast.105), channel_id=1, source_target_pairs={{2,0},{3,1},{6,4},{7,5},{10,8},{11,9},{14,12},{15,13},{18,16},{19,... | collective-permute-start | bytes 2949128 | tf_op jit(solution)/shard_map/ppermute | solution.py:263
  62.1 18.8 %collective-permute-start.5 = (bf16[384,1280]{1,0:T(8,128)(2,1)}, bf16[384,1280]{1,0:T(8,128)(2,1)}, u32[]{:S(2)}, u32[]{:S(2)}) collective-permute-start(bf16[384,1280]{1,0:T(8,128)(2,1)} %fusion.26), channel_id=1, source_target_pairs={{2,1},{3,0},{6,5},{7,4},{10,9},{11,8},{14,13},{15,12},{18,17},{19,... | collective-permute-start | bytes 2949128 | tf_op jit(solution)/shard_map/ppermute | solution.py:261
  63.4 7.5 %collective-permute-start.7 = (f32[1,1280]{1,0:T(1,128)S(1)}, f32[1,1280]{1,0:T(1,128)S(1)}, u32[]{:S(2)}, u32[]{:S(2)}) collective-permute-start(f32[1,1280]{1,0:T(1,128)S(1)} %copy-done.3), channel_id=1, source_target_pairs={{2,0},{3,1},{6,4},{7,5},{10,8},{11,9},{14,12},{15,13},{18,16},{19,... | collective-permute-start | bytes 15368 | tf_op jit(solution)/shard_map/ppermute | solution.py:263
  84.6 1.5 copy-start.7
  91.8 1.9 %copy-start.4 = (bf16[1280,384]{1,0:T(8,128)(2,1)S(1)}, bf16[1280,384]{1,0:T(8,128)(2,1)}, u32[]{:S(2)}) copy-start(bf16[1280,384]{1,0:T(8,128)(2,1)} %fusion.24) | copy-start | bytes 2949124
  95.4 1.5 copy-start.5
  98.1 40.9 %collective-permute-start.9 = (bf16[2,640,512]{2,1,0:T(8,128)(2,1)S(1)}, bf16[2,640,512]{2,1,0:T(8,128)(2,1)S(1)}, u32[]{:S(2)}, u32[]{:S(2)}) collective-permute-start(bf16[2,640,512]{2,1,0:T(8,128)(2,1)S(1)} %convolution_convert_fusion.4), channel_id=1, source_target_pairs={{0,8},{4,12},{8,0},{12,4},{16,24},{20,28},{24,16},{28,20},{32,40},... | collective-permute-start | bytes 3932168 | tf_op jit(solution)/shard_map/ppermute | solution.py:204
  100.5 38.0 %collective-permute-start.10 = (bf16[2,640,512]{2,1,0:T(8,128)(2,1)S(1)}, bf16[2,640,512]{2,1,0:T(8,128)(2,1)S(1)}, u32[]{:S(2)}, u32[]{:S(2)}) collective-permute-start(bf16[2,640,512]{2,1,0:T(8,128)(2,1)S(1)} %convolution_convert_fusion.5), channel_id=1, source_target_pairs={{0,24},{4,28},{8,16},{12,20},{16,8},{20,12},{24,0},{28,4},{32,56},... | collective-permute-start | bytes 3932168 | tf_op jit(solution)/shard_map/ppermute | solution.py:204
  104.6 30.2 %collective-permute-start.12 = (bf16[2,640,512]{2,1,0:T(8,128)(2,1)}, bf16[2,640,512]{2,1,0:T(8,128)(2,1)S(1)}, u32[]{:S(2)}, u32[]{:S(2)}) collective-permute-start(bf16[2,640,512]{2,1,0:T(8,128)(2,1)} %convolution_convert_fusion.7), channel_id=1, source_target_pairs={{0,96},{4,100},{8,104},{12,108},{16,112},{20,116},{24,120},{28,124... | collective-permute-start | bytes 3932168 | tf_op jit(solution)/shard_map/ppermute | solution.py:204
  109.3 28.7 %collective-permute-start.11 = (bf16[2,640,512]{2,1,0:T(8,128)(2,1)}, bf16[2,640,512]{2,1,0:T(8,128)(2,1)S(1)}, u32[]{:S(2)}, u32[]{:S(2)}) collective-permute-start(bf16[2,640,512]{2,1,0:T(8,128)(2,1)} %convolution_convert_fusion.6), channel_id=1, source_target_pairs={{0,32},{4,36},{8,40},{12,44},{16,48},{20,52},{24,56},{28,60},{32,0... | collective-permute-start | bytes 3932168 | tf_op jit(solution)/shard_map/ppermute | solution.py:204
  110.3 32.2 %collective-permute-start.8 = (bf16[2,640,512]{2,1,0:T(8,128)(2,1)S(1)}, bf16[2,640,512]{2,1,0:T(8,128)(2,1)S(1)}, u32[]{:S(2)}, u32[]{:S(2)}) collective-permute-start(bf16[2,640,512]{2,1,0:T(8,128)(2,1)S(1)} %convolution_convert_fusion.3), channel_id=1, source_target_pairs={{0,4},{4,0},{8,12},{12,8},{16,20},{20,16},{24,28},{28,24},{32,36},... | collective-permute-start | bytes 3932168 | tf_op jit(solution)/shard_map/ppermute | solution.py:204
  139.5 13.6 %collective-permute-start.17 = (bf16[2,320,512]{2,1,0:T(8,128)(2,1)S(1)}, bf16[2,320,512]{2,1,0:T(8,128)(2,1)S(1)}, u32[]{:S(2)}, u32[]{:S(2)}) collective-permute-start(bf16[2,320,512]{2,1,0:T(8,128)(2,1)S(1)} %add_convert_fusion.2), channel_id=1, source_target_pairs={{0,4},{4,0},{8,12},{12,8},{16,20},{20,16},{24,28},{28,24},{32,36},... | collective-permute-start | bytes 1966088 | tf_op jit(solution)/shard_map/ppermute | solution.py:204
  140.5 13.2 %collective-permute-start.16 = (bf16[2,320,512]{2,1,0:T(8,128)(2,1)S(1)}, bf16[2,320,512]{2,1,0:T(8,128)(2,1)S(1)}, u32[]{:S(2)}, u32[]{:S(2)}) collective-permute-start(bf16[2,320,512]{2,1,0:T(8,128)(2,1)S(1)} %add_convert_fusion.5), channel_id=1, source_target_pairs={{0,32},{4,36},{8,40},{12,44},{16,48},{20,52},{24,56},{28,60},{32,0... | collective-permute-start | bytes 1966088 | tf_op jit(solution)/shard_map/ppermute | solution.py:204
  141.0 17.2 %collective-permute-start.14 = (bf16[2,320,512]{2,1,0:T(8,128)(2,1)S(1)}, bf16[2,320,512]{2,1,0:T(8,128)(2,1)S(1)}, u32[]{:S(2)}, u32[]{:S(2)}) collective-permute-start(bf16[2,320,512]{2,1,0:T(8,128)(2,1)S(1)} %add_convert_fusion.3), channel_id=1, source_target_pairs={{0,8},{4,12},{8,0},{12,4},{16,24},{20,28},{24,16},{28,20},{32,40},... | collective-permute-start | bytes 1966088 | tf_op jit(solution)/shard_map/ppermute | solution.py:204
  141.6 15.5 %collective-permute-start.15 = (bf16[2,320,512]{2,1,0:T(8,128)(2,1)S(1)}, bf16[2,320,512]{2,1,0:T(8,128)(2,1)S(1)}, u32[]{:S(2)}, u32[]{:S(2)}) collective-permute-start(bf16[2,320,512]{2,1,0:T(8,128)(2,1)S(1)} %add_convert_fusion.4), channel_id=1, source_target_pairs={{0,24},{4,28},{8,16},{12,20},{16,8},{20,12},{24,0},{28,4},{32,56},... | collective-permute-start | bytes 1966088 | tf_op jit(solution)/shard_map/ppermute | solution.py:204
  143.0 17.3 %collective-permute-start.13 = (bf16[2,320,512]{2,1,0:T(8,128)(2,1)S(1)}, bf16[2,320,512]{2,1,0:T(8,128)(2,1)S(1)}, u32[]{:S(2)}, u32[]{:S(2)}) collective-permute-start(bf16[2,320,512]{2,1,0:T(8,128)(2,1)S(1)} %add_convert_fusion.1), channel_id=1, source_target_pairs={{0,96},{4,100},{8,104},{12,108},{16,112},{20,116},{24,120},{28,124... | collective-permute-start | bytes 1966088 | tf_op jit(solution)/shard_map/ppermute | solution.py:204
  154.4 15.2 %collective-permute-start.22 = (bf16[2,160,1024]{2,1,0:T(8,128)(2,1)S(1)}, bf16[2,160,1024]{2,1,0:T(8,128)(2,1)S(1)}, u32[]{:S(2)}, u32[]{:S(2)}) collective-permute-start(bf16[2,160,1024]{2,1,0:T(8,128)(2,1)S(1)} %pad_maximum_fusion.2), channel_id=1, source_target_pairs={{0,24},{4,28},{8,16},{12,20},{16,8},{20,12},{24,0},{28,4},{32,56},... | collective-permute-start | bytes 1966088 | tf_op jit(solution)/shard_map/ppermute | solution.py:204
  157.4 8.4 %collective-permute-start.23 = (bf16[2,160,512]{2,1,0:T(8,128)(2,1)S(1)}, bf16[2,160,512]{2,1,0:T(8,128)(2,1)S(1)}, u32[]{:S(2)}, u32[]{:S(2)}) collective-permute-start(bf16[2,160,512]{2,1,0:T(8,128)(2,1)S(1)} %add_convert_fusion.8), channel_id=1, source_target_pairs={{0,96},{4,100},{8,104},{12,108},{16,112},{20,116},{24,120},{28,124... | collective-permute-start | bytes 983048 | tf_op jit(solution)/shard_map/ppermute | solution.py:204
  158.6 11.7 %collective-permute-start.21 = (bf16[2,160,512]{2,1,0:T(8,128)(2,1)S(1)}, bf16[2,160,512]{2,1,0:T(8,128)(2,1)S(1)}, u32[]{:S(2)}, u32[]{:S(2)}) collective-permute-start(bf16[2,160,512]{2,1,0:T(8,128)(2,1)S(1)} %add_convert_fusion.7), channel_id=1, source_target_pairs={{0,4},{4,0},{8,12},{12,8},{16,20},{20,16},{24,28},{28,24},{32,36},... | collective-permute-start | bytes 983048 | tf_op jit(solution)/shard_map/ppermute | solution.py:204
  160.7 11.3 %collective-permute-start.20 = (bf16[2,160,512]{2,1,0:T(8,128)(2,1)S(1)}, bf16[2,160,512]{2,1,0:T(8,128)(2,1)S(1)}, u32[]{:S(2)}, u32[]{:S(2)}) collective-permute-start(bf16[2,160,512]{2,1,0:T(8,128)(2,1)S(1)} %add_convert_fusion.6), channel_id=1, source_target_pairs={{0,32},{4,36},{8,40},{12,44},{16,48},{20,52},{24,56},{28,60},{32,0... | collective-permute-start | bytes 983048 | tf_op jit(solution)/shard_map/ppermute | solution.py:204
  161.0 19.2 %collective-permute-start.18 = (bf16[384,1280]{1,0:T(8,128)(2,1)S(1)}, bf16[384,1280]{1,0:T(8,128)(2,1)S(1)}, u32[]{:S(2)}, u32[]{:S(2)}) collective-permute-start(bf16[384,1280]{1,0:T(8,128)(2,1)S(1)} %fusion.29.mine_ref), channel_id=1, source_target_pairs={{0,1},{1,0},{4,5},{5,4},{8,9},{9,8},{12,13},{13,12},{16,17},{17,16... | collective-permute-start | bytes 2949128 | tf_op jit(solution)/shard_map/ppermute | solution.py:279
  165.8 19.4 %collective-permute-start.19 = (bf16[384,1280]{1,0:T(8,128)(2,1)S(1)}, bf16[384,1280]{1,0:T(8,128)(2,1)S(1)}, u32[]{:S(2)}, u32[]{:S(2)}) collective-permute-start(bf16[384,1280]{1,0:T(8,128)(2,1)S(1)} %shard_map.95), channel_id=1, source_target_pairs={{0,2},{1,3},{4,6},{5,7},{8,10},{9,11},{12,14},{13,15},{16,18},{17,... | collective-permute-start | bytes 2949128 | tf_op jit(solution)/shard_map/ppermute | solution.py:280
  169.9 7.2 %collective-permute-start.26 = (bf16[2,80,1024]{2,1,0:T(8,128)(2,1)S(1)}, bf16[2,80,1024]{2,1,0:T(8,128)(2,1)S(1)}, u32[]{:S(2)}, u32[]{:S(2)}) collective-permute-start(bf16[2,80,1024]{2,1,0:T(8,128)(2,1)S(1)} %pad_maximum_fusion.3), channel_id=1, source_target_pairs={{0,8},{4,12},{8,0},{12,4},{16,24},{20,28},{24,16},{28,20},{32,40},... | collective-permute-start | bytes 983048 | tf_op jit(solution)/shard_map/ppermute | solution.py:204
  170.8 10.4 %collective-permute-start.25 = (bf16[2,80,1024]{2,1,0:T(8,128)(2,1)S(1)}, bf16[2,80,1024]{2,1,0:T(8,128)(2,1)S(1)}, u32[]{:S(2)}, u32[]{:S(2)}) collective-permute-start(bf16[2,80,1024]{2,1,0:T(8,128)(2,1)S(1)} %pad_maximum_fusion.4), channel_id=1, source_target_pairs={{0,96},{4,100},{8,104},{12,108},{16,112},{20,116},{24,120},{28,124... | collective-permute-start | bytes 983048 | tf_op jit(solution)/shard_map/ppermute | solution.py:204
  172.2 11.5 %collective-permute-start.24 = (bf16[2,80,512]{2,1,0:T(8,128)(2,1)S(1)}, bf16[2,80,512]{2,1,0:T(8,128)(2,1)S(1)}, u32[]{:S(2)}, u32[]{:S(2)}) collective-permute-start(bf16[2,80,512]{2,1,0:T(8,128)(2,1)S(1)} %add_convert_fusion.11), channel_id=1, source_target_pairs={{0,24},{4,28},{8,16},{12,20},{16,8},{20,12},{24,0},{28,4},{32,56},... | collective-permute-start | bytes 491528 | tf_op jit(solution)/shard_map/ppermute | solution.py:204
  180.8 7.2 %collective-permute-start.27 = (bf16[2,40,1024]{2,1,0:T(8,128)(2,1)S(1)}, bf16[2,40,1024]{2,1,0:T(8,128)(2,1)S(1)}, u32[]{:S(2)}, u32[]{:S(2)}) collective-permute-start(bf16[2,40,1024]{2,1,0:T(8,128)(2,1)S(1)} %pad_maximum_fusion.5), channel_id=1, source_target_pairs={{0,4},{4,0},{8,12},{12,8},{16,20},{20,16},{24,28},{28,24},{32,36},... | collective-permute-start | bytes 491528 | tf_op jit(solution)/shard_map/ppermute | solution.py:204
  181.9 6.7 %collective-permute-start.28 = (bf16[2,40,1024]{2,1,0:T(8,128)(2,1)S(1)}, bf16[2,40,1024]{2,1,0:T(8,128)(2,1)S(1)}, u32[]{:S(2)}, u32[]{:S(2)}) collective-permute-start(bf16[2,40,1024]{2,1,0:T(8,128)(2,1)S(1)} %pad_maximum_fusion.6), channel_id=1, source_target_pairs={{0,32},{4,36},{8,40},{12,44},{16,48},{20,52},{24,56},{28,60},{32,0... | collective-permute-start | bytes 491528 | tf_op jit(solution)/shard_map/ppermute | solution.py:204
  184.0 5.2 %collective-permute-start.29 = (bf16[2,40,512]{2,1,0:T(8,128)(2,1)S(1)}, bf16[2,40,512]{2,1,0:T(8,128)(2,1)S(1)}, u32[]{:S(2)}, u32[]{:S(2)}) collective-permute-start(bf16[2,40,512]{2,1,0:T(8,128)(2,1)S(1)} %add_convert_fusion.21), channel_id=1, source_target_pairs={{0,8},{4,12},{8,0},{12,4},{16,24},{20,28},{24,16},{28,20},{32,40},... | collective-permute-start | bytes 245768 | tf_op jit(solution)/shard_map/ppermute | solution.py:204
  188.3 1.7 copy-start.1

commit v4 on v2

--- a/solution.py
+++ b/solution.py
@@ -128,46 +128,12 @@
     return lax.all_to_all(requests, "dp", 0, 0, tiled=True)
 
 
-def pick_kernel(ids_ref, asked_ref, held_ref, out_ref):
-    peers, per = asked_ref.shape
-    seq_dev = held_ref.shape[1]
-    row = lax.broadcasted_iota(jnp.int32, (peers * per, 1), 0)
-    spread = lax.broadcasted_iota(jnp.int32, (peers * per, peers), 1) == row // per
-    asked = dot(
-        spread.astype(jnp.float32).astype(jnp.bfloat16),
-        asked_ref[...].astype(jnp.float32).astype(jnp.bfloat16),
-        1,
-        0,
-    )
-    place = jnp.zeros((peers * per, 1), jnp.float32)
-    for k in range(per):
-        place = jnp.where(row % per == k, asked[:, k : k + 1], place)
-    positions = lax.broadcasted_iota(jnp.int32, (peers * per, seq_dev), 1) + 1
-    pick = (place == positions.astype(jnp.float32)).astype(jnp.float32).astype(jnp.bfloat16)
-    out_ref[...] = dot(pick, held_ref[0], 1, 0).astype(jnp.bfloat16)
-
-
-def pick_rows(asked, llm_grad, ids):
+def fetch_tokens(llm_grad, asked, cap, sec, ten, rep, peers):
     seq_dev, width = llm_grad.shape[1:]
-    return pl.pallas_call(
-        pick_kernel,
-        grid_spec=pltpu.PrefetchScalarGridSpec(
-            num_scalar_prefetch=1,
-            grid=(1,),
-            in_specs=[
-                pl.BlockSpec(asked.shape, lambda i, *_: (0, 0)),
-                pl.BlockSpec((1, seq_dev, width), lambda i, ids: (ids[0], 0, 0)),
-            ],
-            out_specs=pl.BlockSpec((asked.size, width), lambda i, *_: (0, 0)),
-        ),
-        out_shape=jax.ShapeDtypeStruct((asked.size, width), jnp.bfloat16),
-    )(ids, asked, llm_grad)
-
-
-def fetch_tokens(llm_grad, asked, cap, ids, ten, rep, peers):
-    width = llm_grad.shape[2]
     per = -(-cap // peers)
-    got = lax.all_to_all(pick_rows(asked, llm_grad, ids), "dp", 0, 0, tiled=True)
+    pick = (asked.reshape(-1)[:, None] == jnp.arange(1, seq_dev + 1)[None, :]).astype(jnp.bfloat16)
+    held = lax.dynamic_index_in_dim(llm_grad, sec, 0, keepdims=False)
+    got = lax.all_to_all(dot(pick, held, 1, 0).astype(jnp.bfloat16), "dp", 0, 0, tiled=True)
     both = ("section", "tensor")
     first_own = lax.ppermute(got, both, [(0, 2), (1, 3)])
     first_other = lax.ppermute(got, both, [(0, 3), (1, 2)])
@@ -259,7 +225,7 @@
     ids = jnp.stack([sec, rep])
     asked = ask_tokens(llm_grad.shape[1], slots, frames, ids, peers)
     normed, asked = lax.optimization_barrier((normed, asked))
-    upstream, got = fetch_tokens(llm_grad, asked, slots.shape[1], ids, ten, rep, peers)
+    upstream, got = fetch_tokens(llm_grad, asked, slots.shape[1], sec, ten, rep, peers)
     activ, slope = lax.optimization_barrier(gelu_and_slope(dot(normed, weight_in, 1, 0)))
 
     order = from_code(to_code(rep) ^ jnp.arange(peers))

time: 186 us -> 188 us (1.011)
  matrix products: 43.7 us -> 50 us
  waiting for transfers between devices: 63.5 us -> 60.6 us
  Pallas kernels: 8.41 us -> 5.57 us
    dot_general x9 -> x10, matrix products: 30.1 us -> 35.4 us  [dot(): lax.dot_general(a, b, (((ca,), (cb,)), ((), ())), preferred_element_type=...]
    pallas_call x1 -> x0, Pallas kernels: 2.85 us -> none  [pick_rows(): pl.pallas_call(pick_kernel, grid_spec=pltpu.PrefetchScalarGridSpec(num_sc...]
    unnamed x20 -> x24, local copies, waits for them, and re-layouts: 3.89 us -> 3.89 us
  transfers between devices with their start and end apart: 29 -> 29, of which waited for: 14 -> 14; matrix products, arithmetic and copies ran while one was open for 20% -> 22% of each run, Pallas kernels for 1% -> 1%
where the time goes in v4:
time: 188 us; the launch traced here: 187 us
  waiting for transfers between devices  60.6 us (32%)
  matrix products  50 us (27%)
  starting transfers between devices  49.2 us (26%)
  other arithmetic  10.7 us (6%)
  local copies, waits for them, and re-layouts  9.25 us (5%)
  Pallas kernels  5.57 us (3%)
    ppermute x20, waiting for transfers between devices, reduce_weight_grads(): piece = lax.ppermute(last, 'dp', neighbour_pairs(ORDERS[streams[0]][t]))  39.3 us
    dot_general x10, matrix products, dot(): lax.dot_general(a, b, (((ca,), (cb,)), ((), ())), preferred_element_type=...  35.4 us
    ppermute x20, starting transfers between devices, reduce_weight_grads(): piece = lax.ppermute(last, 'dp', neighbour_pairs(ORDERS[streams[0]][t]))  21.9 us
    dot_general x30, matrix products, group(): lax.dot_general(lefts[i][:, lo:hi], right[:, :, i * span:(i + 1) * span],...  14.6 us
    all_to_all x1, starting transfers between devices, ask_tokens(): return lax.all_to_all(requests, 'dp', 0, 0, tiled=True)  9.34 us
    ppermute x1, waiting for transfers between devices, per_device(): other = lax.ppermute(partial, both, [(2, 1), (3, 0)])  7.73 us
    ppermute x1, waiting for transfers between devices, per_device(): packed = lax.ppermute(packed, 'section', [(1, 0)])  6.35 us
    all_to_all x1, starting transfers between devices, fetch_tokens(): lax.all_to_all(dot(pick, held, 1, 0).astype(jnp.bfloat16), 'dp', 0, 0, ti...  5.02 us
  transfers between devices with their start and end apart: 29, of which 14 were waited for; matrix products, arithmetic and copies ran while one was open for 22% of the time, Pallas kernels for 1%

profile of v4, /device:TPU:0, one launch (start us, length us, event | category | flops | bytes accessed | tf_op | source)
XLA Modules:
  0.0 186.7 jit_solution(8744416610901088345)
XLA Ops:
  0.7 0.6 pad_add_fusion.ids_ref
  1.3 2.1 %shard_map.94 = s32[32,2]{1,0:T(8,128)} custom-call(s32[2]{0:T(128)} %pad_add_fusion.ids_ref, s32[2,2]{1,0:T(2,128)} %frames_ref.1, s32[2,48]{1,0:T(2,128)} %slots_ref.1), custom_call_target="tpu_custom_call" | custom-call | tf_op jit(solution)/shard_map/pallas_call | solution.py:118
  3.4 9.3 %all-to-all-start = ((s32[32,1,2]{2,1,0:T(1,128)}), s32[32,1,2]{2,1,0:T(1,128)S(1)}, u32[]{:S(2)}, u32[]{:S(2)}) async-start(s32[32,1,2]{2,1,0:T(1,128)} %bitcast.154), calls=%async_computation | async-start | bytes 32768 | tf_op jit(solution)/shard_map/all_to_all | solution.py:128
  12.7 1.4 convert_reduce_fusion
  14.1 1.6 fusion.33
  16.2 1.3 multiply_convert_fusion.1
  17.6 3.3 %all-to-all-done = s32[32,1,2]{2,1,0:T(1,128)S(1)} async-done(((s32[32,1,2]{2,1,0:T(1,128)}), s32[32,1,2]{2,1,0:T(1,128)S(1)}, u32[]{:S(2)}, u32[]{:S(2)}) %all-to-all-start) | async-done | bytes 288 | tf_op jit(solution)/shard_map/all_to_all | solution.py:128
  21.4 0.9 all_to_all.19
  22.3 5.0 %all-to-all-start.1 = ((bf16[32,2,2560]{2,1,0:T(2,128)(2,1)}), bf16[32,2,2560]{2,1,0:T(2,128)(2,1)S(1)}, u32[]{:S(2)}, u32[]{:S(2)}) async-start(bf16[32,2,2560]{2,1,0:T(2,128)(2,1)} %all_to_all.19), calls=%async_computation.1 | async-start | bytes 655360 | tf_op jit(solution)/shard_map/all_to_all | solution.py:136
  27.3 9.2 %add_convert_fusion = (bf16[384,2560]{1,0:T(8,128)(2,1)}, bf16[384,2560]{1,0:T(8,128)(2,1)}) fusion(bf16[384,1280]{1,0:T(8,128)(2,1)} %multiply_convert_fusion.1, bf16[1,1280,2560]{2,1,0:T(8,128)(2,1)} %param.12), kind=kOutput, calls=%fused_computation.25 | convolution fusion | flops 2534277120 | bytes 11468800 | tf_op jit(solution)/shard_map/dot_general | solution.py:58
  36.6 0.5 all-to-all-done.1
  37.3 0.7 collective-permute-start.2
  37.9 4.5 %collective-permute-start.1 = (bf16[64,2560]{1,0:T(8,128)(2,1)S(1)}, bf16[64,2560]{1,0:T(8,128)(2,1)S(1)}, u32[]{:S(2)}, u32[]{:S(2)}) collective-permute-start(bf16[64,2560]{1,0:T(8,128)(2,1)S(1)} %all_to_all.21), channel_id=1, source_target_pairs={{0,3},{1,2},{4,7},{5,6},{8,11},{9,10},{12,15},{13,14},{16,19},{17,... | collective-permute-start | bytes 983048 | tf_op jit(solution)/shard_map/ppermute | solution.py:139
  42.4 1.5 collective-permute-start
  43.9 3.1 %fusion.24 = bf16[1280,384]{1,0:T(8,128)(2,1)S(1)} fusion(bf16[384,1280]{1,0:T(8,128)(2,1)} %multiply_convert_fusion.1, s32[1280]{0:T(1024)S(1)} %add.390), kind=kOutput, calls=%fused_computation.43 | convolution fusion | flops 1260421120 | bytes 1971200 | tf_op jit(solution)/shard_map/dot_general | solution.py:58
  48.3 1.1 copy-done.8
  49.4 6.2 %fusion.16 = bf16[384,2560]{1,0:T(8,128)(2,1)S(1)} fusion(bf16[384,2560]{1,0:T(8,128)(2,1)S(1)} %copy-done.8, bf16[384,1280]{1,0:T(8,128)(2,1)S(1)} %pad_maximum_fusion.1, bf16[1,2560,1280]{2,1,0:T(8,128)(2,1)} %param.13), kind=kOutput, calls=%fused_computation.23 | convolution fusion | flops 2519531520 | bytes 11468800 | tf_op jit(solution)/shard_map/dot_general | solution.py:58
  55.7 2.7 %fusion.26 = bf16[384,1280]{1,0:T(8,128)(2,1)S(1)} fusion(bf16[384,2560]{1,0:T(8,128)(2,1)S(1)} %fusion.16, bf16[1,1280,2560]{2,1,0:T(8,128)(2,1)S(1)} %bitcast.157), kind=kOutput, calls=%fused_computation.45 | convolution fusion | flops 2517073920 | bytes 9502720 | tf_op jit(solution)/shard_map/dot_general | solution.py:58
  58.5 2.0 %pad_maximum_fusion = bf16[1200,1280]{1,0:T(8,128)(2,1)} fusion(bf16[48,1280]{1,0:T(8,128)(2,1)S(1)} %pad_maximum_fusion.8, bf16[384,1280]{1,0:T(8,128)(2,1)S(1)} %bitcast.105, bf16[384,1280]{1,0:T(8,128)(2,1)S(1)} %pad_maximum_fusion.1, bf16[384,1280]{1,0:T(8,128)(2,1)S(1)} %fusion.26), kind=kLoop, calls=%fused_computation.32 | loop fusion | flops 12288000 | bytes 6144000 | tf_op jit(solution)/shard_map/concatenate | solution.py:259
  60.5 1.3 collective-permute-start.3
  61.8 1.5 collective-permute-start.4
  63.3 6.4 %collective-permute-done.3 = bf16[1200,1280]{1,0:T(8,128)(2,1)} collective-permute-done((bf16[1200,1280]{1,0:T(8,128)(2,1)}, bf16[1200,1280]{1,0:T(8,128)(2,1)}, u32[]{:S(2)}, u32[]{:S(2)}) %collective-permute-start.3) | collective-permute-done | bytes 3072032 | tf_op jit(solution)/shard_map/ppermute | solution.py:260
  69.6 0.8 fusion.174.gain_ref
  70.4 2.0 %fusion.197 = (bf16[384,1280]{1,0:T(8,128)(2,1)S(1)}, bf16[384,1280]{1,0:T(8,128)(2,1)S(1)}, bf16[384,1280]{1,0:T(8,128)(2,1)S(1)}) fusion(bf16[1200,1280]{1,0:T(8,128)(2,1)} %collective-permute-done.3), kind=kLoop, calls=%fused_computation.244 | loop fusion | bytes 5898240 | tf_op jit(solution)/shard_map/slice | solution.py:261
  72.4 7.7 %collective-permute-done.4.other_ref = bf16[384,1280]{1,0:T(8,128)(2,1)S(1)} collective-permute-done((bf16[384,1280]{1,0:T(8,128)(2,1)}, bf16[384,1280]{1,0:T(8,128)(2,1)S(1)}, u32[]{:S(2)}, u32[]{:S(2)}) %collective-permute-start.4) | collective-permute-done | bytes 983072 | tf_op jit(solution)/shard_map/ppermute | solution.py:252
  80.1 1.7 shard_map.95
  82.0 1.4 copy-done.9
  83.4 5.6 %fusion.19 = bf16[384,2560]{1,0:T(8,128)(2,1)S(1)} fusion(bf16[384,2560]{1,0:T(8,128)(2,1)S(1)} %copy-done.9, bf16[384,1280]{1,0:T(8,128)(2,1)S(1)} %broadcast_select_fusion.1.g_ref, bf16[1,2560,1280]{2,1,0:T(8,128)(2,1)} %param.13), kind=kOutput, calls=%fused_computation.24 | convolution fusion | flops 2519531520 | bytes 11468800 | tf_op jit(solution)/shard_map/dot_general | solution.py:58
  89.1 1.9 %fusion.25 = bf16[1280,384]{1,0:T(8,128)(2,1)S(1)} fusion(bf16[384,1280]{1,0:T(8,128)(2,1)S(1)} %broadcast_select_fusion.1.g_ref, s32[1280]{0:T(1024)S(1)} %add.390), kind=kOutput, calls=%fused_computation.44 | convolution fusion | flops 1260421120 | bytes 1971200 | tf_op jit(solution)/shard_map/dot_general | solution.py:58
  92.8 1.3 copy-done.6
  94.6 0.8 convolution_convert_fusion.4
  95.4 1.6 collective-permute-start.6
  97.0 0.8 convolution_convert_fusion.5
  97.9 2.2 %collective-permute-start.7 = (bf16[2,640,512]{2,1,0:T(8,128)(2,1)S(1)}, bf16[2,640,512]{2,1,0:T(8,128)(2,1)S(1)}, u32[]{:S(2)}, u32[]{:S(2)}) collective-permute-start(bf16[2,640,512]{2,1,0:T(8,128)(2,1)S(1)} %convolution_convert_fusion.5), channel_id=1, source_target_pairs={{0,24},{4,28},{8,16},{12,20},{16,8},{20,12},{24,0},{28,4},{32,56},... | collective-permute-start | bytes 3932168 | tf_op jit(solution)/shard_map/ppermute | solution.py:195
  100.0 1.9 %convolution_convert_fusion.7 = bf16[2,640,512]{2,1,0:T(8,128)(2,1)} fusion(bf16[2,384,512]{2,1,0:T(8,128)(2,1)S(1)} %get-tuple-element.71, bf16[1,1280,384]{2,1,0:T(8,128)(2,1)S(1)} %bitcast.111, bf16[1,1280,384]{2,1,0:T(8,128)(2,1)S(1)} %bitcast.121), kind=kOutput, calls=%fused_computation.62 | convolution fusion | flops 504463360 | bytes 4063232 | tf_op jit(solution)/shard_map/dot_general | solution.py:176
  101.9 2.7 %collective-permute-start.9 = (bf16[2,640,512]{2,1,0:T(8,128)(2,1)}, bf16[2,640,512]{2,1,0:T(8,128)(2,1)S(1)}, u32[]{:S(2)}, u32[]{:S(2)}) collective-permute-start(bf16[2,640,512]{2,1,0:T(8,128)(2,1)} %convolution_convert_fusion.7), channel_id=1, source_target_pairs={{0,96},{4,100},{8,104},{12,108},{16,112},{20,116},{24,120},{28,124... | collective-permute-start | bytes 3932168 | tf_op jit(solution)/shard_map/ppermute | solution.py:195
  104.7 1.9 %convolution_convert_fusion.6 = bf16[2,640,512]{2,1,0:T(8,128)(2,1)} fusion(bf16[2,384,512]{2,1,0:T(8,128)(2,1)S(1)} %get-tuple-element.72, bf16[2,1280,384]{2,1,0:T(8,128)(2,1)S(1)} %bitcast.145), kind=kOutput, calls=%fused_computation.61 | convolution fusion | flops 503971840 | bytes 3080192 | tf_op jit(solution)/shard_map/dot_general | solution.py:176
  106.8 0.8 convolution_convert_fusion.3
  107.7 1.3 collective-permute-start.5
  109.0 5.6 %fusion.29.mine_ref = bf16[384,1280]{1,0:T(8,128)(2,1)S(1)} fusion(bf16[384,2560]{1,0:T(8,128)(2,1)S(1)} %fusion.19, bf16[1,1280,2560]{2,1,0:T(8,128)(2,1)} %param.12), kind=kOutput, calls=%fused_computation.46 | convolution fusion | flops 2517073920 | bytes 9502720 | tf_op jit(solution)/shard_map/dot_general | solution.py:58
  114.5 17.4 %collective-permute-done.9 = bf16[2,640,512]{2,1,0:T(8,128)(2,1)S(1)} collective-permute-done((bf16[2,640,512]{2,1,0:T(8,128)(2,1)}, bf16[2,640,512]{2,1,0:T(8,128)(2,1)S(1)}, u32[]{:S(2)}, u32[]{:S(2)}) %collective-permute-start.9) | collective-permute-done | bytes 1310752 | tf_op jit(solution)/shard_map/ppermute | solution.py:195
  132.5 2.7 %collective-permute-done.8 = bf16[2,640,512]{2,1,0:T(8,128)(2,1)S(1)} collective-permute-done((bf16[2,640,512]{2,1,0:T(8,128)(2,1)}, bf16[2,640,512]{2,1,0:T(8,128)(2,1)S(1)}, u32[]{:S(2)}, u32[]{:S(2)}) %collective-permute-start.8) | collective-permute-done | bytes 1310752 | tf_op jit(solution)/shard_map/ppermute | solution.py:195
  135.1 0.5 add_convert_fusion.4
  136.7 0.9 collective-permute-start.14
  138.1 0.6 collective-permute-start.11
  138.7 0.9 collective-permute-start.12
  140.1 1.1 collective-permute-start.10
  141.3 8.9 %collective-permute-done.14 = bf16[2,320,512]{2,1,0:T(8,128)(2,1)S(1)} collective-permute-done((bf16[2,320,512]{2,1,0:T(8,128)(2,1)S(1)}, bf16[2,320,512]{2,1,0:T(8,128)(2,1)S(1)}, u32[]{:S(2)}, u32[]{:S(2)}) %collective-permute-start.14) | collective-permute-done | bytes 655392 | tf_op jit(solution)/shard_map/ppermute | solution.py:195
  151.3 1.2 collective-permute-start.19
  152.6 1.5 collective-permute-done.12
  155.1 1.9 collective-permute-start.18
  157.8 2.2 %collective-permute-start.15 = (bf16[384,1280]{1,0:T(8,128)(2,1)S(1)}, bf16[384,1280]{1,0:T(8,128)(2,1)S(1)}, u32[]{:S(2)}, u32[]{:S(2)}) collective-permute-start(bf16[384,1280]{1,0:T(8,128)(2,1)S(1)} %fusion.29.mine_ref), channel_id=1, source_target_pairs={{0,1},{1,0},{4,5},{5,4},{8,9},{9,8},{12,13},{13,12},{16,17},{17,16... | collective-permute-start | bytes 2949128 | tf_op jit(solution)/shard_map/ppermute | solution.py:276
  160.0 2.8 %collective-permute-done.20 = bf16[2,160,512]{2,1,0:T(8,128)(2,1)S(1)} collective-permute-done((bf16[2,160,512]{2,1,0:T(8,128)(2,1)S(1)}, bf16[2,160,512]{2,1,0:T(8,128)(2,1)S(1)}, u32[]{:S(2)}, u32[]{:S(2)}) %collective-permute-start.20) | collective-permute-done | bytes 327712 | tf_op jit(solution)/shard_map/ppermute | solution.py:195
  162.7 1.3 collective-permute-start.16
  164.4 2.0 %collective-permute-done.19 = bf16[2,160,1024]{2,1,0:T(8,128)(2,1)S(1)} collective-permute-done((bf16[2,160,1024]{2,1,0:T(8,128)(2,1)S(1)}, bf16[2,160,1024]{2,1,0:T(8,128)(2,1)S(1)}, u32[]{:S(2)}, u32[]{:S(2)}) %collective-permute-start.19) | collective-permute-done | bytes 655392 | tf_op jit(solution)/shard_map/ppermute | solution.py:195
  167.8 1.1 collective-permute-start.22
  169.2 1.2 collective-permute-start.21
  170.4 3.6 %collective-permute-done.23 = bf16[2,80,1024]{2,1,0:T(8,128)(2,1)S(1)} collective-permute-done((bf16[2,80,1024]{2,1,0:T(8,128)(2,1)S(1)}, bf16[2,80,1024]{2,1,0:T(8,128)(2,1)S(1)}, u32[]{:S(2)}, u32[]{:S(2)}) %collective-permute-start.23) | collective-permute-done | bytes 327712 | tf_op jit(solution)/shard_map/ppermute | solution.py:195
  174.0 3.0 %collective-permute-done.15.other_ref = bf16[384,1280]{1,0:T(8,128)(2,1)S(1)} collective-permute-done((bf16[384,1280]{1,0:T(8,128)(2,1)S(1)}, bf16[384,1280]{1,0:T(8,128)(2,1)S(1)}, u32[]{:S(2)}, u32[]{:S(2)}) %collective-permute-start.15) | collective-permute-done | bytes 983072 | tf_op jit(solution)/shard_map/ppermute | solution.py:276
  178.5 1.6 collective-permute-start.25
  180.4 1.5 collective-permute-start.26
  181.9 1.7 shard_map.96
  183.6 1.0 broadcast_select_fusion
  185.9 0.8 slice_bitcast_fusion
  (115 shorter events, 15.2 us)
Async XLA Ops:
  0.6 20.5 %copy-start = (bf16[2,64,2560]{2,1,0:T(8,128)(2,1)S(1)}, bf16[2,64,2560]{2,1,0:T(8,128)(2,1)}, u32[]{:S(2)}) copy-start(bf16[2,64,2560]{2,1,0:T(8,128)(2,1)} %param.7) | copy-start | bytes 1966084
  0.6 15.5 %copy-start.2 = (bf16[1,2,192,1280]{3,2,1,0:T(8,128)(2,1)S(1)}, bf16[1,2,192,1280]{3,2,1,0:T(8,128)(2,1)}, u32[]{:S(2)}) copy-start(bf16[1,2,192,1280]{3,2,1,0:T(8,128)(2,1)} %param.10) | copy-start | bytes 2949124
  0.7 15.3 %copy-start.3 = (f32[1,1280]{1,0:T(1,128)S(1)}, f32[1,1280]{1,0:T(1,128)}, u32[]{:S(2)}) copy-start(f32[1,1280]{1,0:T(1,128)} %gain_ref.1) | copy-start | bytes 15364
  3.4 17.5 %all-to-all-start = ((s32[32,1,2]{2,1,0:T(1,128)}), s32[32,1,2]{2,1,0:T(1,128)S(1)}, u32[]{:S(2)}, u32[]{:S(2)}) async-start(s32[32,1,2]{2,1,0:T(1,128)} %bitcast.154), calls=%async_computation | async-start | bytes 32768 | tf_op jit(solution)/shard_map/all_to_all | solution.py:128
  22.3 14.8 %all-to-all-start.1 = ((bf16[32,2,2560]{2,1,0:T(2,128)(2,1)}), bf16[32,2,2560]{2,1,0:T(2,128)(2,1)S(1)}, u32[]{:S(2)}, u32[]{:S(2)}) async-start(bf16[32,2,2560]{2,1,0:T(2,128)(2,1)} %all_to_all.19), calls=%async_computation.1 | async-start | bytes 655360 | tf_op jit(solution)/shard_map/all_to_all | solution.py:136
  37.3 9.8 %collective-permute-start.2 = (bf16[64,2560]{1,0:T(8,128)(2,1)S(1)}, bf16[64,2560]{1,0:T(8,128)(2,1)S(1)}, u32[]{:S(2)}, u32[]{:S(2)}) collective-permute-start(bf16[64,2560]{1,0:T(8,128)(2,1)S(1)} %all_to_all.21), channel_id=1, source_target_pairs={{2,3},{3,2},{6,7},{7,6},{10,11},{11,10},{14,15},{15,14},{18,19},{1... | collective-permute-start | bytes 983048 | tf_op jit(solution)/shard_map/ppermute | solution.py:140
  37.9 9.5 %collective-permute-start.1 = (bf16[64,2560]{1,0:T(8,128)(2,1)S(1)}, bf16[64,2560]{1,0:T(8,128)(2,1)S(1)}, u32[]{:S(2)}, u32[]{:S(2)}) collective-permute-start(bf16[64,2560]{1,0:T(8,128)(2,1)S(1)} %all_to_all.21), channel_id=1, source_target_pairs={{0,3},{1,2},{4,7},{5,6},{8,11},{9,10},{12,15},{13,14},{16,19},{17,... | collective-permute-start | bytes 983048 | tf_op jit(solution)/shard_map/ppermute | solution.py:139
  42.4 5.4 %collective-permute-start = (bf16[64,2560]{1,0:T(8,128)(2,1)S(1)}, bf16[64,2560]{1,0:T(8,128)(2,1)S(1)}, u32[]{:S(2)}, u32[]{:S(2)}) collective-permute-start(bf16[64,2560]{1,0:T(8,128)(2,1)S(1)} %all_to_all.21), channel_id=1, source_target_pairs={{0,2},{1,3},{4,6},{5,7},{8,10},{9,11},{12,14},{13,15},{16,18},{17,... | collective-permute-start | bytes 983048 | tf_op jit(solution)/shard_map/ppermute | solution.py:138
  47.9 1.5 copy-start.8
  48.2 7.5 %slice-start = ((s8[6553600]{0:T(1024)(128)(4,1)}), s8[4194304]{0:T(1024)(128)(4,1)S(1)}, s32[]{:S(2)}) async-start(s8[6553600]{0:T(1024)(128)(4,1)} %bitcast.156), calls=%async_computation.2 | async-start | bytes 8388608
  49.4 9.0 %copy-start.4 = (bf16[384,1280]{1,0:T(8,128)(2,1)}, bf16[384,1280]{1,0:T(8,128)(2,1)S(1)}, u32[]{:S(2)}) copy-start(bf16[384,1280]{1,0:T(8,128)(2,1)S(1)} %pad_maximum_fusion.1) | copy-start | bytes 2949124
  49.4 6.3 %slice-start.1 = ((s8[6553600]{0:T(1024)(128)(4,1)}), s8[2359296]{0:T(1024)(128)(4,1)S(1)}, s32[]{:S(2)}) async-start(s8[6553600]{0:T(1024)(128)(4,1)} %bitcast.156), calls=%async_computation.3 | async-start | bytes 4718592
  58.4 2.0 %copy-start.7 = (bf16[384,1280]{1,0:T(8,128)(2,1)}, bf16[384,1280]{1,0:T(8,128)(2,1)S(1)}, u32[]{:S(2)}) copy-start(bf16[384,1280]{1,0:T(8,128)(2,1)S(1)} %fusion.26) | copy-start | bytes 2949124
  60.5 9.2 %collective-permute-start.3 = (bf16[1200,1280]{1,0:T(8,128)(2,1)}, bf16[1200,1280]{1,0:T(8,128)(2,1)}, u32[]{:S(2)}, u32[]{:S(2)}) collective-permute-start(bf16[1200,1280]{1,0:T(8,128)(2,1)} %pad_maximum_fusion), channel_id=1, source_target_pairs={{2,0},{3,1},{6,4},{7,5},{10,8},{11,9},{14,12},{15,13},{18,16},{19,... | collective-permute-start | bytes 9216008 | tf_op jit(solution)/shard_map/ppermute | solution.py:260
  61.8 18.4 %collective-permute-start.4 = (bf16[384,1280]{1,0:T(8,128)(2,1)}, bf16[384,1280]{1,0:T(8,128)(2,1)S(1)}, u32[]{:S(2)}, u32[]{:S(2)}) collective-permute-start(bf16[384,1280]{1,0:T(8,128)(2,1)} %copy-done.7), channel_id=1, source_target_pairs={{2,1},{3,0},{6,5},{7,4},{10,9},{11,8},{14,13},{15,12},{18,17},{19,... | collective-permute-start | bytes 2949128 | tf_op jit(solution)/shard_map/ppermute | solution.py:252
  80.1 1.8 copy-start.5
  81.9 1.5 copy-start.9
  92.6 1.5 copy-start.6
  95.4 40.7 %collective-permute-start.6 = (bf16[2,640,512]{2,1,0:T(8,128)(2,1)S(1)}, bf16[2,640,512]{2,1,0:T(8,128)(2,1)S(1)}, u32[]{:S(2)}, u32[]{:S(2)}) collective-permute-start(bf16[2,640,512]{2,1,0:T(8,128)(2,1)S(1)} %convolution_convert_fusion.4), channel_id=1, source_target_pairs={{0,8},{4,12},{8,0},{12,4},{16,24},{20,28},{24,16},{28,20},{32,40},... | collective-permute-start | bytes 3932168 | tf_op jit(solution)/shard_map/ppermute | solution.py:195
  97.9 37.8 %collective-permute-start.7 = (bf16[2,640,512]{2,1,0:T(8,128)(2,1)S(1)}, bf16[2,640,512]{2,1,0:T(8,128)(2,1)S(1)}, u32[]{:S(2)}, u32[]{:S(2)}) collective-permute-start(bf16[2,640,512]{2,1,0:T(8,128)(2,1)S(1)} %convolution_convert_fusion.5), channel_id=1, source_target_pairs={{0,24},{4,28},{8,16},{12,20},{16,8},{20,12},{24,0},{28,4},{32,56},... | collective-permute-start | bytes 3932168 | tf_op jit(solution)/shard_map/ppermute | solution.py:195
  101.9 30.0 %collective-permute-start.9 = (bf16[2,640,512]{2,1,0:T(8,128)(2,1)}, bf16[2,640,512]{2,1,0:T(8,128)(2,1)S(1)}, u32[]{:S(2)}, u32[]{:S(2)}) collective-permute-start(bf16[2,640,512]{2,1,0:T(8,128)(2,1)} %convolution_convert_fusion.7), channel_id=1, source_target_pairs={{0,96},{4,100},{8,104},{12,108},{16,112},{20,116},{24,120},{28,124... | collective-permute-start | bytes 3932168 | tf_op jit(solution)/shard_map/ppermute | solution.py:195
  106.6 28.5 %collective-permute-start.8 = (bf16[2,640,512]{2,1,0:T(8,128)(2,1)}, bf16[2,640,512]{2,1,0:T(8,128)(2,1)S(1)}, u32[]{:S(2)}, u32[]{:S(2)}) collective-permute-start(bf16[2,640,512]{2,1,0:T(8,128)(2,1)} %convolution_convert_fusion.6), channel_id=1, source_target_pairs={{0,32},{4,36},{8,40},{12,44},{16,48},{20,52},{24,56},{28,60},{32,0... | collective-permute-start | bytes 3932168 | tf_op jit(solution)/shard_map/ppermute | solution.py:195
  107.7 32.0 %collective-permute-start.5 = (bf16[2,640,512]{2,1,0:T(8,128)(2,1)S(1)}, bf16[2,640,512]{2,1,0:T(8,128)(2,1)S(1)}, u32[]{:S(2)}, u32[]{:S(2)}) collective-permute-start(bf16[2,640,512]{2,1,0:T(8,128)(2,1)S(1)} %convolution_convert_fusion.3), channel_id=1, source_target_pairs={{0,4},{4,0},{8,12},{12,8},{16,20},{20,16},{24,28},{28,24},{32,36},... | collective-permute-start | bytes 3932168 | tf_op jit(solution)/shard_map/ppermute | solution.py:195
  136.7 13.5 %collective-permute-start.14 = (bf16[2,320,512]{2,1,0:T(8,128)(2,1)S(1)}, bf16[2,320,512]{2,1,0:T(8,128)(2,1)S(1)}, u32[]{:S(2)}, u32[]{:S(2)}) collective-permute-start(bf16[2,320,512]{2,1,0:T(8,128)(2,1)S(1)} %add_convert_fusion.2), channel_id=1, source_target_pairs={{0,4},{4,0},{8,12},{12,8},{16,20},{20,16},{24,28},{28,24},{32,36},... | collective-permute-start | bytes 1966088 | tf_op jit(solution)/shard_map/ppermute | solution.py:195
  137.6 12.9 %collective-permute-start.13 = (bf16[2,320,512]{2,1,0:T(8,128)(2,1)S(1)}, bf16[2,320,512]{2,1,0:T(8,128)(2,1)S(1)}, u32[]{:S(2)}, u32[]{:S(2)}) collective-permute-start(bf16[2,320,512]{2,1,0:T(8,128)(2,1)S(1)} %add_convert_fusion.5), channel_id=1, source_target_pairs={{0,32},{4,36},{8,40},{12,44},{16,48},{20,52},{24,56},{28,60},{32,0... | collective-permute-start | bytes 1966088 | tf_op jit(solution)/shard_map/ppermute | solution.py:195
  138.1 16.6 %collective-permute-start.11 = (bf16[2,320,512]{2,1,0:T(8,128)(2,1)S(1)}, bf16[2,320,512]{2,1,0:T(8,128)(2,1)S(1)}, u32[]{:S(2)}, u32[]{:S(2)}) collective-permute-start(bf16[2,320,512]{2,1,0:T(8,128)(2,1)S(1)} %add_convert_fusion.3), channel_id=1, source_target_pairs={{0,8},{4,12},{8,0},{12,4},{16,24},{20,28},{24,16},{28,20},{32,40},... | collective-permute-start | bytes 1966088 | tf_op jit(solution)/shard_map/ppermute | solution.py:195
  138.7 15.3 %collective-permute-start.12 = (bf16[2,320,512]{2,1,0:T(8,128)(2,1)S(1)}, bf16[2,320,512]{2,1,0:T(8,128)(2,1)S(1)}, u32[]{:S(2)}, u32[]{:S(2)}) collective-permute-start(bf16[2,320,512]{2,1,0:T(8,128)(2,1)S(1)} %add_convert_fusion.4), channel_id=1, source_target_pairs={{0,24},{4,28},{8,16},{12,20},{16,8},{20,12},{24,0},{28,4},{32,56},... | collective-permute-start | bytes 1966088 | tf_op jit(solution)/shard_map/ppermute | solution.py:195
  140.1 16.9 %collective-permute-start.10 = (bf16[2,320,512]{2,1,0:T(8,128)(2,1)S(1)}, bf16[2,320,512]{2,1,0:T(8,128)(2,1)S(1)}, u32[]{:S(2)}, u32[]{:S(2)}) collective-permute-start(bf16[2,320,512]{2,1,0:T(8,128)(2,1)S(1)} %add_convert_fusion.1), channel_id=1, source_target_pairs={{0,96},{4,100},{8,104},{12,108},{16,112},{20,116},{24,120},{28,124... | collective-permute-start | bytes 1966088 | tf_op jit(solution)/shard_map/ppermute | solution.py:195
  151.3 15.1 %collective-permute-start.19 = (bf16[2,160,1024]{2,1,0:T(8,128)(2,1)S(1)}, bf16[2,160,1024]{2,1,0:T(8,128)(2,1)S(1)}, u32[]{:S(2)}, u32[]{:S(2)}) collective-permute-start(bf16[2,160,1024]{2,1,0:T(8,128)(2,1)S(1)} %pad_maximum_fusion.3), channel_id=1, source_target_pairs={{0,24},{4,28},{8,16},{12,20},{16,8},{20,12},{24,0},{28,4},{32,56},... | collective-permute-start | bytes 1966088 | tf_op jit(solution)/shard_map/ppermute | solution.py:195
  154.4 8.4 %collective-permute-start.20 = (bf16[2,160,512]{2,1,0:T(8,128)(2,1)S(1)}, bf16[2,160,512]{2,1,0:T(8,128)(2,1)S(1)}, u32[]{:S(2)}, u32[]{:S(2)}) collective-permute-start(bf16[2,160,512]{2,1,0:T(8,128)(2,1)S(1)} %add_convert_fusion.8), channel_id=1, source_target_pairs={{0,96},{4,100},{8,104},{12,108},{16,112},{20,116},{24,120},{28,124... | collective-permute-start | bytes 983048 | tf_op jit(solution)/shard_map/ppermute | solution.py:195
  155.1 12.1 %collective-permute-start.18 = (bf16[2,160,512]{2,1,0:T(8,128)(2,1)S(1)}, bf16[2,160,512]{2,1,0:T(8,128)(2,1)S(1)}, u32[]{:S(2)}, u32[]{:S(2)}) collective-permute-start(bf16[2,160,512]{2,1,0:T(8,128)(2,1)S(1)} %add_convert_fusion.7), channel_id=1, source_target_pairs={{0,4},{4,0},{8,12},{12,8},{16,20},{20,16},{24,28},{28,24},{32,36},... | collective-permute-start | bytes 983048 | tf_op jit(solution)/shard_map/ppermute | solution.py:195
  157.3 11.5 %collective-permute-start.17 = (bf16[2,160,512]{2,1,0:T(8,128)(2,1)S(1)}, bf16[2,160,512]{2,1,0:T(8,128)(2,1)S(1)}, u32[]{:S(2)}, u32[]{:S(2)}) collective-permute-start(bf16[2,160,512]{2,1,0:T(8,128)(2,1)S(1)} %add_convert_fusion.6), channel_id=1, source_target_pairs={{0,32},{4,36},{8,40},{12,44},{16,48},{20,52},{24,56},{28,60},{32,0... | collective-permute-start | bytes 983048 | tf_op jit(solution)/shard_map/ppermute | solution.py:195
  157.8 19.2 %collective-permute-start.15 = (bf16[384,1280]{1,0:T(8,128)(2,1)S(1)}, bf16[384,1280]{1,0:T(8,128)(2,1)S(1)}, u32[]{:S(2)}, u32[]{:S(2)}) collective-permute-start(bf16[384,1280]{1,0:T(8,128)(2,1)S(1)} %fusion.29.mine_ref), channel_id=1, source_target_pairs={{0,1},{1,0},{4,5},{5,4},{8,9},{9,8},{12,13},{13,12},{16,17},{17,16... | collective-permute-start | bytes 2949128 | tf_op jit(solution)/shard_map/ppermute | solution.py:276
  162.7 19.1 %collective-permute-start.16 = (bf16[384,1280]{1,0:T(8,128)(2,1)S(1)}, bf16[384,1280]{1,0:T(8,128)(2,1)S(1)}, u32[]{:S(2)}, u32[]{:S(2)}) collective-permute-start(bf16[384,1280]{1,0:T(8,128)(2,1)S(1)} %shard_map.95), channel_id=1, source_target_pairs={{0,2},{1,3},{4,6},{5,7},{8,10},{9,11},{12,14},{13,15},{16,18},{17,... | collective-permute-start | bytes 2949128 | tf_op jit(solution)/shard_map/ppermute | solution.py:277
  166.8 7.2 %collective-permute-start.23 = (bf16[2,80,1024]{2,1,0:T(8,128)(2,1)S(1)}, bf16[2,80,1024]{2,1,0:T(8,128)(2,1)S(1)}, u32[]{:S(2)}, u32[]{:S(2)}) collective-permute-start(bf16[2,80,1024]{2,1,0:T(8,128)(2,1)S(1)} %pad_maximum_fusion.4), channel_id=1, source_target_pairs={{0,8},{4,12},{8,0},{12,4},{16,24},{20,28},{24,16},{28,20},{32,40},... | collective-permute-start | bytes 983048 | tf_op jit(solution)/shard_map/ppermute | solution.py:195
  167.8 10.1 %collective-permute-start.22 = (bf16[2,80,1024]{2,1,0:T(8,128)(2,1)S(1)}, bf16[2,80,1024]{2,1,0:T(8,128)(2,1)S(1)}, u32[]{:S(2)}, u32[]{:S(2)}) collective-permute-start(bf16[2,80,1024]{2,1,0:T(8,128)(2,1)S(1)} %pad_maximum_fusion.5), channel_id=1, source_target_pairs={{0,96},{4,100},{8,104},{12,108},{16,112},{20,116},{24,120},{28,124... | collective-permute-start | bytes 983048 | tf_op jit(solution)/shard_map/ppermute | solution.py:195
  169.2 10.9 %collective-permute-start.21 = (bf16[2,80,512]{2,1,0:T(8,128)(2,1)S(1)}, bf16[2,80,512]{2,1,0:T(8,128)(2,1)S(1)}, u32[]{:S(2)}, u32[]{:S(2)}) collective-permute-start(bf16[2,80,512]{2,1,0:T(8,128)(2,1)S(1)} %add_convert_fusion.11), channel_id=1, source_target_pairs={{0,24},{4,28},{8,16},{12,20},{16,8},{20,12},{24,0},{28,4},{32,56},... | collective-permute-start | bytes 491528 | tf_op jit(solution)/shard_map/ppermute | solution.py:195
  177.6 7.1 %collective-permute-start.24 = (bf16[2,40,1024]{2,1,0:T(8,128)(2,1)S(1)}, bf16[2,40,1024]{2,1,0:T(8,128)(2,1)S(1)}, u32[]{:S(2)}, u32[]{:S(2)}) collective-permute-start(bf16[2,40,1024]{2,1,0:T(8,128)(2,1)S(1)} %pad_maximum_fusion.6), channel_id=1, source_target_pairs={{0,4},{4,0},{8,12},{12,8},{16,20},{20,16},{24,28},{28,24},{32,36},... | collective-permute-start | bytes 491528 | tf_op jit(solution)/shard_map/ppermute | solution.py:195
  178.5 6.8 %collective-permute-start.25 = (bf16[2,40,1024]{2,1,0:T(8,128)(2,1)S(1)}, bf16[2,40,1024]{2,1,0:T(8,128)(2,1)S(1)}, u32[]{:S(2)}, u32[]{:S(2)}) collective-permute-start(bf16[2,40,1024]{2,1,0:T(8,128)(2,1)S(1)} %pad_maximum_fusion.7), channel_id=1, source_target_pairs={{0,32},{4,36},{8,40},{12,44},{16,48},{20,52},{24,56},{28,60},{32,0... | collective-permute-start | bytes 491528 | tf_op jit(solution)/shard_map/ppermute | solution.py:195
  180.4 5.5 %collective-permute-start.26 = (bf16[2,40,512]{2,1,0:T(8,128)(2,1)S(1)}, bf16[2,40,512]{2,1,0:T(8,128)(2,1)S(1)}, u32[]{:S(2)}, u32[]{:S(2)}) collective-permute-start(bf16[2,40,512]{2,1,0:T(8,128)(2,1)S(1)} %add_convert_fusion.21), channel_id=1, source_target_pairs={{0,8},{4,12},{8,0},{12,4},{16,24},{20,28},{24,16},{28,20},{32,40},... | collective-permute-start | bytes 245768 | tf_op jit(solution)/shard_map/ppermute | solution.py:195
  185.0 1.7 copy-start.1

commit v5 on v2

--- a/solution.py
+++ b/solution.py
@@ -222,7 +222,7 @@
         for place, streams in enumerate(SHARED[t]):
             if t:
                 for i in streams:
-                    received[i][-1] = after(received[i][-1], last, turns.get((t, place)))
+                    received[i][-1] = after(received[i][-1], last if t > 1 else None, turns.get((t, place)))
             sends = [group(i, width >> (t + 1), width >> t) for i in streams]
             last = sends[0] if len(sends) == 1 else jnp.concatenate(sends, axis=2)
             started.append(last)

time: 186 us -> 186 us (level)
  starting transfers between devices: 47.5 us -> 52 us
  waiting for transfers between devices: 63.5 us -> 59.6 us
    ppermute x20, waiting for transfers between devices: 39.6 us -> 33.9 us  [reduce_weight_grads(): piece = lax.ppermute(last, 'dp', neighbour_pairs(ORDERS[streams[0]][t]))]
    ppermute x20, starting transfers between devices: 21.8 us -> 25.3 us  [reduce_weight_grads(): piece = lax.ppermute(last, 'dp', neighbour_pairs(ORDERS[streams[0]][t]))]
  transfers between devices with their start and end apart: 29 -> 29, of which waited for: 14 -> 13; matrix products, arithmetic and copies ran while one was open for 20% -> 20% of each run, Pallas kernels for 1% -> 1%
where the time goes in v5:
time: 186 us
  waiting for transfers between devices  59.6 us (32%)
  starting transfers between devices  52 us (28%)
  matrix products  43.7 us (23%)
  local copies, waits for them, and re-layouts  10.9 us (6%)
  other arithmetic  9.63 us (5%)
  Pallas kernels  8.41 us (5%)
    ppermute x20, waiting for transfers between devices, reduce_weight_grads(): piece = lax.ppermute(last, 'dp', neighbour_pairs(ORDERS[streams[0]][t]))  33.9 us
    dot_general x9, matrix products, dot(): lax.dot_general(a, b, (((ca,), (cb,)), ((), ())), preferred_element_type=...  30.1 us
    ppermute x20, starting transfers between devices, reduce_weight_grads(): piece = lax.ppermute(last, 'dp', neighbour_pairs(ORDERS[streams[0]][t]))  25.3 us
    dot_general x30, matrix products, group(): lax.dot_general(lefts[i][:, lo:hi], right[:, :, i * span:(i + 1) * span],...  13.5 us
    all_to_all x1, starting transfers between devices, ask_tokens(): return lax.all_to_all(requests, 'dp', 0, 0, tiled=True)  9.35 us
    ppermute x1, waiting for transfers between devices, per_device(): other = lax.ppermute(partial, both, [(2, 1), (3, 0)])  7.52 us
    ppermute x1, waiting for transfers between devices, per_device(): packed = lax.ppermute(packed, 'section', [(1, 0)])  6.4 us
    ppermute x1, waiting for transfers between devices, exchange(): lax.ppermute(after(partial, last), both, [(0, 1), (1, 0)])  4.78 us
  transfers between devices with their start and end apart: 29, of which 13 were waited for; matrix products, arithmetic and copies ran while one was open for 20% of the time, Pallas kernels for 1%

profile of v5, /device:TPU:0, one launch (start us, length us, event | category | flops | bytes accessed | tf_op | source)
XLA Modules:
  0.0 185.6 jit_solution(271328934821492955)
XLA Ops:
  1.3 2.1 %shard_map.94 = s32[32,2]{1,0:T(8,128)} custom-call(s32[2]{0:T(128)} %pad_add_fusion.ids_ref, s32[2,2]{1,0:T(2,128)} %frames_ref.1, s32[2,48]{1,0:T(2,128)} %slots_ref.1), custom_call_target="tpu_custom_call" | custom-call | tf_op jit(solution)/shard_map/pallas_call | solution.py:118
  3.3 9.3 %all-to-all-start = ((s32[32,1,2]{2,1,0:T(1,128)}), s32[32,1,2]{2,1,0:T(1,128)S(1)}, u32[]{:S(2)}, u32[]{:S(2)}) async-start(s32[32,1,2]{2,1,0:T(1,128)} %bitcast.151), calls=%async_computation | async-start | bytes 32768 | tf_op jit(solution)/shard_map/all_to_all | solution.py:128
  12.7 1.4 convert_reduce_fusion
  14.1 1.6 fusion.33
  16.6 4.2 %all-to-all-done = s32[32,1,2]{2,1,0:T(1,128)S(1)} async-done(((s32[32,1,2]{2,1,0:T(1,128)}), s32[32,1,2]{2,1,0:T(1,128)S(1)}, u32[]{:S(2)}, u32[]{:S(2)}) %all-to-all-start) | async-done | bytes 288 | tf_op jit(solution)/shard_map/all_to_all | solution.py:128
  20.9 0.7 copy.19.asked_ref
  21.6 2.8 %shard_map.95 = bf16[64,2560]{1,0:T(8,128)(2,1)} custom-call(s32[2]{0:T(128)} %pad_add_fusion.ids_ref, s32[32,2]{1,0:T(8,128)} %copy.19.asked_ref, bf16[2,64,2560]{2,1,0:T(8,128)(2,1)} %held_ref.1), custom_call_target="tpu_custom_call" | custom-call | tf_op jit(solution)/shard_map/pallas_call | solution.py:152
  24.5 1.8 all_to_all.19
  26.3 4.1 %all-to-all-start.1 = ((bf16[32,2,2560]{2,1,0:T(2,128)(2,1)}), bf16[32,2,2560]{2,1,0:T(2,128)(2,1)S(1)}, u32[]{:S(2)}, u32[]{:S(2)}) async-start(bf16[32,2,2560]{2,1,0:T(2,128)(2,1)} %all_to_all.19), calls=%async_computation.1 | async-start | bytes 655360 | tf_op jit(solution)/shard_map/all_to_all | solution.py:170
  30.4 8.7 %add_convert_fusion = (bf16[384,2560]{1,0:T(8,128)(2,1)}, bf16[384,2560]{1,0:T(8,128)(2,1)}) fusion(bf16[384,1280]{1,0:T(8,128)(2,1)S(1)} %multiply_convert_fusion.1, bf16[1,1280,2560]{2,1,0:T(8,128)(2,1)} %param.12), kind=kOutput, calls=%fused_computation.25 | convolution fusion | flops 2534277120 | bytes 11468800 | tf_op jit(solution)/shard_map/dot_general | solution.py:58
  39.1 1.0 all-to-all-done.1
  41.0 4.0 %collective-permute-start.1 = (bf16[64,2560]{1,0:T(8,128)(2,1)S(1)}, bf16[64,2560]{1,0:T(8,128)(2,1)S(1)}, u32[]{:S(2)}, u32[]{:S(2)}) collective-permute-start(bf16[64,2560]{1,0:T(8,128)(2,1)S(1)} %all_to_all.21), channel_id=1, source_target_pairs={{0,3},{1,2},{4,7},{5,6},{8,11},{9,10},{12,15},{13,14},{16,19},{17,... | collective-permute-start | bytes 983048 | tf_op jit(solution)/shard_map/ppermute | solution.py:173
  45.0 1.3 collective-permute-start
  46.3 1.9 %fusion.24 = bf16[1280,384]{1,0:T(8,128)(2,1)S(1)} fusion(bf16[384,1280]{1,0:T(8,128)(2,1)S(1)} %multiply_convert_fusion.1, s32[1280]{0:T(1024)S(1)} %add.373), kind=kOutput, calls=%fused_computation.42 | convolution fusion | flops 1260421120 | bytes 1971200 | tf_op jit(solution)/shard_map/dot_general | solution.py:58
  48.3 1.8 collective-permute-done.1
  50.9 1.1 copy-done.4
  52.0 5.9 %fusion.16 = bf16[384,2560]{1,0:T(8,128)(2,1)S(1)} fusion(bf16[384,2560]{1,0:T(8,128)(2,1)S(1)} %copy-done.4, bf16[384,1280]{1,0:T(8,128)(2,1)S(1)} %pad_maximum_fusion.1, bf16[1,2560,1280]{2,1,0:T(8,128)(2,1)} %param.13), kind=kOutput, calls=%fused_computation.23 | convolution fusion | flops 2519531520 | bytes 11468800 | tf_op jit(solution)/shard_map/dot_general | solution.py:58
  57.9 2.7 %fusion.26 = bf16[384,1280]{1,0:T(8,128)(2,1)S(1)} fusion(bf16[384,2560]{1,0:T(8,128)(2,1)S(1)} %fusion.16, bf16[1,1280,2560]{2,1,0:T(8,128)(2,1)S(1)} %bitcast.156), kind=kOutput, calls=%fused_computation.44 | convolution fusion | flops 2517073920 | bytes 9502720 | tf_op jit(solution)/shard_map/dot_general | solution.py:58
  60.7 1.9 %pad_maximum_fusion = bf16[1200,1280]{1,0:T(8,128)(2,1)} fusion(bf16[48,1280]{1,0:T(8,128)(2,1)S(1)} %pad_maximum_fusion.8, bf16[384,1280]{1,0:T(8,128)(2,1)S(1)} %bitcast.102, bf16[384,1280]{1,0:T(8,128)(2,1)S(1)} %pad_maximum_fusion.1, bf16[384,1280]{1,0:T(8,128)(2,1)S(1)} %fusion.26), kind=kLoop, calls=%fused_computation.31 | loop fusion | flops 12288000 | bytes 6144000 | tf_op jit(solution)/shard_map/concatenate | solution.py:293
  62.6 1.3 collective-permute-start.3
  63.9 1.5 collective-permute-start.4
  65.4 6.4 %collective-permute-done.3 = bf16[1200,1280]{1,0:T(8,128)(2,1)} collective-permute-done((bf16[1200,1280]{1,0:T(8,128)(2,1)}, bf16[1200,1280]{1,0:T(8,128)(2,1)}, u32[]{:S(2)}, u32[]{:S(2)}) %collective-permute-start.3) | collective-permute-done | bytes 3072032 | tf_op jit(solution)/shard_map/ppermute | solution.py:294
  71.8 0.8 fusion.169.gain_ref
  72.6 2.1 %fusion.191 = (bf16[384,1280]{1,0:T(8,128)(2,1)S(1)}, bf16[384,1280]{1,0:T(8,128)(2,1)S(1)}, bf16[384,1280]{1,0:T(8,128)(2,1)S(1)}) fusion(bf16[1200,1280]{1,0:T(8,128)(2,1)} %collective-permute-done.3), kind=kLoop, calls=%fused_computation.236 | loop fusion | bytes 5898240 | tf_op jit(solution)/shard_map/slice | solution.py:295
  74.7 7.5 %collective-permute-done.4.other_ref = bf16[384,1280]{1,0:T(8,128)(2,1)S(1)} collective-permute-done((bf16[384,1280]{1,0:T(8,128)(2,1)}, bf16[384,1280]{1,0:T(8,128)(2,1)S(1)}, u32[]{:S(2)}, u32[]{:S(2)}) %collective-permute-start.4) | collective-permute-done | bytes 983072 | tf_op jit(solution)/shard_map/ppermute | solution.py:286
  82.2 1.7 shard_map.96
  84.1 1.4 copy-done.5
  85.5 2.7 %fusion.19 = bf16[384,2560]{1,0:T(8,128)(2,1)S(1)} fusion(bf16[384,2560]{1,0:T(8,128)(2,1)S(1)} %copy-done.5, bf16[384,1280]{1,0:T(8,128)(2,1)S(1)} %broadcast_select_fusion.1.g_ref, bf16[1,2560,1280]{2,1,0:T(8,128)(2,1)S(1)} %bitcast.154), kind=kOutput, calls=%fused_computation.24 | convolution fusion | flops 2519531520 | bytes 11468800 | tf_op jit(solution)/shard_map/dot_general | solution.py:58
  88.3 1.9 %fusion.25 = bf16[1280,384]{1,0:T(8,128)(2,1)S(1)} fusion(bf16[384,1280]{1,0:T(8,128)(2,1)S(1)} %broadcast_select_fusion.1.g_ref, s32[1280]{0:T(1024)S(1)} %add.373), kind=kOutput, calls=%fused_computation.43 | convolution fusion | flops 1260421120 | bytes 1971200 | tf_op jit(solution)/shard_map/dot_general | solution.py:58
  92.1 1.3 copy-done.2
  93.8 0.8 convolution_convert_fusion.3
  94.6 1.6 collective-permute-start.13
  96.2 0.8 convolution_convert_fusion.4
  97.1 2.1 %collective-permute-start.7 = (bf16[2,640,512]{2,1,0:T(8,128)(2,1)S(1)}, bf16[2,640,512]{2,1,0:T(8,128)(2,1)S(1)}, u32[]{:S(2)}, u32[]{:S(2)}) collective-permute-start(bf16[2,640,512]{2,1,0:T(8,128)(2,1)S(1)} %convolution_convert_fusion.4), channel_id=1, source_target_pairs={{0,24},{4,28},{8,16},{12,20},{16,8},{20,12},{24,0},{28,4},{32,56},... | collective-permute-start | bytes 3932168 | tf_op jit(solution)/shard_map/ppermute | solution.py:229
  99.2 0.8 convolution_convert_fusion.5
  100.0 1.6 collective-permute-start.9
  101.6 1.9 %convolution_convert_fusion.6 = bf16[2,640,512]{2,1,0:T(8,128)(2,1)} fusion(bf16[2,384,512]{2,1,0:T(8,128)(2,1)S(1)} %get-tuple-element.63, bf16[1,1280,384]{2,1,0:T(8,128)(2,1)S(1)} %bitcast.108, bf16[1,1280,384]{2,1,0:T(8,128)(2,1)S(1)} %bitcast.118), kind=kOutput, calls=%fused_computation.61 | convolution fusion | flops 504463360 | bytes 4063232 | tf_op jit(solution)/shard_map/dot_general | solution.py:210
  103.5 2.1 %collective-permute-start.11 = (bf16[2,640,512]{2,1,0:T(8,128)(2,1)}, bf16[2,640,512]{2,1,0:T(8,128)(2,1)S(1)}, u32[]{:S(2)}, u32[]{:S(2)}) collective-permute-start(bf16[2,640,512]{2,1,0:T(8,128)(2,1)} %convolution_convert_fusion.6), channel_id=1, source_target_pairs={{0,96},{4,100},{8,104},{12,108},{16,112},{20,116},{24,120},{28,124... | collective-permute-start | bytes 3932168 | tf_op jit(solution)/shard_map/ppermute | solution.py:229
  105.6 0.8 convolution_convert_fusion.2
  106.5 1.3 collective-permute-start.5
  107.7 5.6 %fusion.29.mine_ref = bf16[384,1280]{1,0:T(8,128)(2,1)S(1)} fusion(bf16[384,2560]{1,0:T(8,128)(2,1)S(1)} %fusion.19, bf16[1,1280,2560]{2,1,0:T(8,128)(2,1)} %param.12), kind=kOutput, calls=%fused_computation.45 | convolution fusion | flops 2517073920 | bytes 9502720 | tf_op jit(solution)/shard_map/dot_general | solution.py:58
  113.6 10.3 %collective-permute-done.13 = bf16[2,640,512]{2,1,0:T(8,128)(2,1)S(1)} collective-permute-done((bf16[2,640,512]{2,1,0:T(8,128)(2,1)S(1)}, bf16[2,640,512]{2,1,0:T(8,128)(2,1)S(1)}, u32[]{:S(2)}, u32[]{:S(2)}) %collective-permute-start.13) | collective-permute-done | bytes 1310752 | tf_op jit(solution)/shard_map/ppermute | solution.py:229
  124.4 1.0 collective-permute-start.14
  125.3 7.9 %collective-permute-done.11 = bf16[2,640,512]{2,1,0:T(8,128)(2,1)S(1)} collective-permute-done((bf16[2,640,512]{2,1,0:T(8,128)(2,1)}, bf16[2,640,512]{2,1,0:T(8,128)(2,1)S(1)}, u32[]{:S(2)}, u32[]{:S(2)}) %collective-permute-start.11) | collective-permute-done | bytes 1310752 | tf_op jit(solution)/shard_map/ppermute | solution.py:229
  135.5 1.0 collective-permute-start.10
  136.5 2.0 %collective-permute-done.5 = bf16[2,640,512]{2,1,0:T(8,128)(2,1)S(1)} collective-permute-done((bf16[2,640,512]{2,1,0:T(8,128)(2,1)S(1)}, bf16[2,640,512]{2,1,0:T(8,128)(2,1)S(1)}, u32[]{:S(2)}, u32[]{:S(2)}) %collective-permute-start.5) | collective-permute-done | bytes 1310752 | tf_op jit(solution)/shard_map/ppermute | solution.py:229
  139.0 1.2 collective-permute-start.6
  140.2 8.6 %collective-permute-done.14 = bf16[2,320,512]{2,1,0:T(8,128)(2,1)S(1)} collective-permute-done((bf16[2,320,512]{2,1,0:T(8,128)(2,1)S(1)}, bf16[2,320,512]{2,1,0:T(8,128)(2,1)S(1)}, u32[]{:S(2)}, u32[]{:S(2)}) %collective-permute-start.14) | collective-permute-done | bytes 655392 | tf_op jit(solution)/shard_map/ppermute | solution.py:229
  149.6 1.2 collective-permute-start.19
  151.2 2.0 %collective-permute-start.20 = (bf16[2,160,512]{2,1,0:T(8,128)(2,1)S(1)}, bf16[2,160,512]{2,1,0:T(8,128)(2,1)S(1)}, u32[]{:S(2)}, u32[]{:S(2)}) collective-permute-start(bf16[2,160,512]{2,1,0:T(8,128)(2,1)S(1)} %add_convert_fusion.8), channel_id=1, source_target_pairs={{0,96},{4,100},{8,104},{12,108},{16,112},{20,116},{24,120},{28,124... | collective-permute-start | bytes 983048 | tf_op jit(solution)/shard_map/ppermute | solution.py:229
  153.6 0.8 collective-permute-start.18
  154.7 2.3 %collective-permute-start.17 = (bf16[2,160,512]{2,1,0:T(8,128)(2,1)S(1)}, bf16[2,160,512]{2,1,0:T(8,128)(2,1)S(1)}, u32[]{:S(2)}, u32[]{:S(2)}) collective-permute-start(bf16[2,160,512]{2,1,0:T(8,128)(2,1)S(1)} %add_convert_fusion.6), channel_id=1, source_target_pairs={{0,32},{4,36},{8,40},{12,44},{16,48},{20,52},{24,56},{28,60},{32,0... | collective-permute-start | bytes 983048 | tf_op jit(solution)/shard_map/ppermute | solution.py:229
  157.1 3.1 %collective-permute-start.15 = (bf16[384,1280]{1,0:T(8,128)(2,1)S(1)}, bf16[384,1280]{1,0:T(8,128)(2,1)S(1)}, u32[]{:S(2)}, u32[]{:S(2)}) collective-permute-start(bf16[384,1280]{1,0:T(8,128)(2,1)S(1)} %fusion.29.mine_ref), channel_id=1, source_target_pairs={{0,1},{1,0},{4,5},{5,4},{8,9},{9,8},{12,13},{13,12},{16,17},{17,16... | collective-permute-start | bytes 2949128 | tf_op jit(solution)/shard_map/ppermute | solution.py:310
  160.2 1.4 collective-permute-start.16
  161.9 2.1 %collective-permute-done.19 = bf16[2,160,1024]{2,1,0:T(8,128)(2,1)S(1)} collective-permute-done((bf16[2,160,1024]{2,1,0:T(8,128)(2,1)S(1)}, bf16[2,160,1024]{2,1,0:T(8,128)(2,1)S(1)}, u32[]{:S(2)}, u32[]{:S(2)}) %collective-permute-start.19) | collective-permute-done | bytes 655392 | tf_op jit(solution)/shard_map/ppermute | solution.py:229
  165.3 2.2 %collective-permute-start.22 = (bf16[2,80,1024]{2,1,0:T(8,128)(2,1)S(1)}, bf16[2,80,1024]{2,1,0:T(8,128)(2,1)S(1)}, u32[]{:S(2)}, u32[]{:S(2)}) collective-permute-start(bf16[2,80,1024]{2,1,0:T(8,128)(2,1)S(1)} %pad_maximum_fusion.5), channel_id=1, source_target_pairs={{0,96},{4,100},{8,104},{12,108},{16,112},{20,116},{24,120},{28,124... | collective-permute-start | bytes 983048 | tf_op jit(solution)/shard_map/ppermute | solution.py:229
  167.7 1.2 collective-permute-start.21
  168.9 2.5 %collective-permute-done.23 = bf16[2,80,1024]{2,1,0:T(8,128)(2,1)S(1)} collective-permute-done((bf16[2,80,1024]{2,1,0:T(8,128)(2,1)S(1)}, bf16[2,80,1024]{2,1,0:T(8,128)(2,1)S(1)}, u32[]{:S(2)}, u32[]{:S(2)}) %collective-permute-start.23) | collective-permute-done | bytes 327712 | tf_op jit(solution)/shard_map/ppermute | solution.py:229
  171.5 4.8 %collective-permute-done.15.other_ref = bf16[384,1280]{1,0:T(8,128)(2,1)S(1)} collective-permute-done((bf16[384,1280]{1,0:T(8,128)(2,1)S(1)}, bf16[384,1280]{1,0:T(8,128)(2,1)S(1)}, u32[]{:S(2)}, u32[]{:S(2)}) %collective-permute-start.15) | collective-permute-done | bytes 983072 | tf_op jit(solution)/shard_map/ppermute | solution.py:310
  176.9 1.3 collective-permute-start.24
  179.2 1.2 collective-permute-start.26
  180.4 1.7 shard_map.97
  182.1 1.0 broadcast_select_fusion
  184.9 0.8 slice_bitcast_fusion
  (110 shorter events, 15.7 us)
Async XLA Ops:
  0.6 15.5 %copy-start = (bf16[1,2,192,1280]{3,2,1,0:T(8,128)(2,1)S(1)}, bf16[1,2,192,1280]{3,2,1,0:T(8,128)(2,1)}, u32[]{:S(2)}) copy-start(bf16[1,2,192,1280]{3,2,1,0:T(8,128)(2,1)} %param.10) | copy-start | bytes 2949124
  0.6 15.3 %copy-start.1 = (f32[1,1280]{1,0:T(1,128)S(1)}, f32[1,1280]{1,0:T(1,128)}, u32[]{:S(2)}) copy-start(f32[1,1280]{1,0:T(1,128)} %gain_ref.1) | copy-start | bytes 15364
  3.3 17.5 %all-to-all-start = ((s32[32,1,2]{2,1,0:T(1,128)}), s32[32,1,2]{2,1,0:T(1,128)S(1)}, u32[]{:S(2)}, u32[]{:S(2)}) async-start(s32[32,1,2]{2,1,0:T(1,128)} %bitcast.151), calls=%async_computation | async-start | bytes 32768 | tf_op jit(solution)/shard_map/all_to_all | solution.py:128
  26.3 13.9 %all-to-all-start.1 = ((bf16[32,2,2560]{2,1,0:T(2,128)(2,1)}), bf16[32,2,2560]{2,1,0:T(2,128)(2,1)S(1)}, u32[]{:S(2)}, u32[]{:S(2)}) async-start(bf16[32,2,2560]{2,1,0:T(2,128)(2,1)} %all_to_all.19), calls=%async_computation.1 | async-start | bytes 655360 | tf_op jit(solution)/shard_map/all_to_all | solution.py:170
  40.3 7.9 %collective-permute-start.2 = (bf16[64,2560]{1,0:T(8,128)(2,1)S(1)}, bf16[64,2560]{1,0:T(8,128)(2,1)S(1)}, u32[]{:S(2)}, u32[]{:S(2)}) collective-permute-start(bf16[64,2560]{1,0:T(8,128)(2,1)S(1)} %all_to_all.21), channel_id=1, source_target_pairs={{2,3},{3,2},{6,7},{7,6},{10,11},{11,10},{14,15},{15,14},{18,19},{1... | collective-permute-start | bytes 983048 | tf_op jit(solution)/shard_map/ppermute | solution.py:174
  41.0 9.0 %collective-permute-start.1 = (bf16[64,2560]{1,0:T(8,128)(2,1)S(1)}, bf16[64,2560]{1,0:T(8,128)(2,1)S(1)}, u32[]{:S(2)}, u32[]{:S(2)}) collective-permute-start(bf16[64,2560]{1,0:T(8,128)(2,1)S(1)} %all_to_all.21), channel_id=1, source_target_pairs={{0,3},{1,2},{4,7},{5,6},{8,11},{9,10},{12,15},{13,14},{16,19},{17,... | collective-permute-start | bytes 983048 | tf_op jit(solution)/shard_map/ppermute | solution.py:173
  45.0 5.4 %collective-permute-start = (bf16[64,2560]{1,0:T(8,128)(2,1)S(1)}, bf16[64,2560]{1,0:T(8,128)(2,1)S(1)}, u32[]{:S(2)}, u32[]{:S(2)}) collective-permute-start(bf16[64,2560]{1,0:T(8,128)(2,1)S(1)} %all_to_all.21), channel_id=1, source_target_pairs={{0,2},{1,3},{4,6},{5,7},{8,10},{9,11},{12,14},{13,15},{16,18},{17,... | collective-permute-start | bytes 983048 | tf_op jit(solution)/shard_map/ppermute | solution.py:172
  50.5 1.5 copy-start.4
  50.8 7.1 %slice-start.2 = ((s8[6553600]{0:T(1024)(128)(4,1)}), s8[4194304]{0:T(1024)(128)(4,1)S(1)}, s32[]{:S(2)}) async-start(s8[6553600]{0:T(1024)(128)(4,1)} %bitcast.155), calls=%async_computation.4 | async-start | bytes 8388608
  52.0 5.9 %slice-start.3 = ((s8[6553600]{0:T(1024)(128)(4,1)}), s8[2359296]{0:T(1024)(128)(4,1)S(1)}, s32[]{:S(2)}) async-start(s8[6553600]{0:T(1024)(128)(4,1)} %bitcast.155), calls=%async_computation.5 | async-start | bytes 4718592
  60.7 2.0 %copy-start.3 = (bf16[384,1280]{1,0:T(8,128)(2,1)}, bf16[384,1280]{1,0:T(8,128)(2,1)S(1)}, u32[]{:S(2)}) copy-start(bf16[384,1280]{1,0:T(8,128)(2,1)S(1)} %fusion.26) | copy-start | bytes 2949124
  62.6 9.2 %collective-permute-start.3 = (bf16[1200,1280]{1,0:T(8,128)(2,1)}, bf16[1200,1280]{1,0:T(8,128)(2,1)}, u32[]{:S(2)}, u32[]{:S(2)}) collective-permute-start(bf16[1200,1280]{1,0:T(8,128)(2,1)} %pad_maximum_fusion), channel_id=1, source_target_pairs={{2,0},{3,1},{6,4},{7,5},{10,8},{11,9},{14,12},{15,13},{18,16},{19,... | collective-permute-start | bytes 9216008 | tf_op jit(solution)/shard_map/ppermute | solution.py:294
  63.9 18.3 %collective-permute-start.4 = (bf16[384,1280]{1,0:T(8,128)(2,1)}, bf16[384,1280]{1,0:T(8,128)(2,1)S(1)}, u32[]{:S(2)}, u32[]{:S(2)}) collective-permute-start(bf16[384,1280]{1,0:T(8,128)(2,1)} %copy-done.3), channel_id=1, source_target_pairs={{2,1},{3,0},{6,5},{7,4},{10,9},{11,8},{14,13},{15,12},{18,17},{19,... | collective-permute-start | bytes 2949128 | tf_op jit(solution)/shard_map/ppermute | solution.py:286
  72.6 11.6 %slice-start = ((s8[6553600]{0:T(1024)(128)(4,1)}), s8[4194304]{0:T(1024)(128)(4,1)S(1)}, s32[]{:S(2)}) async-start(s8[6553600]{0:T(1024)(128)(4,1)} %bitcast.153), calls=%async_computation.2 | async-start | bytes 8388608
  82.2 1.9 %slice-start.1 = ((s8[6553600]{0:T(1024)(128)(4,1)}), s8[2359296]{0:T(1024)(128)(4,1)S(1)}, s32[]{:S(2)}) async-start(s8[6553600]{0:T(1024)(128)(4,1)} %bitcast.153), calls=%async_computation.3 | async-start | bytes 4718592
  84.0 1.5 copy-start.5
  91.8 1.5 copy-start.2
  94.6 29.2 %collective-permute-start.13 = (bf16[2,640,512]{2,1,0:T(8,128)(2,1)S(1)}, bf16[2,640,512]{2,1,0:T(8,128)(2,1)S(1)}, u32[]{:S(2)}, u32[]{:S(2)}) collective-permute-start(bf16[2,640,512]{2,1,0:T(8,128)(2,1)S(1)} %convolution_convert_fusion.3), channel_id=1, source_target_pairs={{0,8},{4,12},{8,0},{12,4},{16,24},{20,28},{24,16},{28,20},{32,40},... | collective-permute-start | bytes 3932168 | tf_op jit(solution)/shard_map/ppermute | solution.py:229
  97.1 36.8 %collective-permute-start.7 = (bf16[2,640,512]{2,1,0:T(8,128)(2,1)S(1)}, bf16[2,640,512]{2,1,0:T(8,128)(2,1)S(1)}, u32[]{:S(2)}, u32[]{:S(2)}) collective-permute-start(bf16[2,640,512]{2,1,0:T(8,128)(2,1)S(1)} %convolution_convert_fusion.4), channel_id=1, source_target_pairs={{0,24},{4,28},{8,16},{12,20},{16,8},{20,12},{24,0},{28,4},{32,56},... | collective-permute-start | bytes 3932168 | tf_op jit(solution)/shard_map/ppermute | solution.py:229
  100.0 35.0 %collective-permute-start.9 = (bf16[2,640,512]{2,1,0:T(8,128)(2,1)S(1)}, bf16[2,640,512]{2,1,0:T(8,128)(2,1)S(1)}, u32[]{:S(2)}, u32[]{:S(2)}) collective-permute-start(bf16[2,640,512]{2,1,0:T(8,128)(2,1)S(1)} %convolution_convert_fusion.5), channel_id=1, source_target_pairs={{0,32},{4,36},{8,40},{12,44},{16,48},{20,52},{24,56},{28,60},{32,0... | collective-permute-start | bytes 3932168 | tf_op jit(solution)/shard_map/ppermute | solution.py:229
  103.5 29.7 %collective-permute-start.11 = (bf16[2,640,512]{2,1,0:T(8,128)(2,1)}, bf16[2,640,512]{2,1,0:T(8,128)(2,1)S(1)}, u32[]{:S(2)}, u32[]{:S(2)}) collective-permute-start(bf16[2,640,512]{2,1,0:T(8,128)(2,1)} %convolution_convert_fusion.6), channel_id=1, source_target_pairs={{0,96},{4,100},{8,104},{12,108},{16,112},{20,116},{24,120},{28,124... | collective-permute-start | bytes 3932168 | tf_op jit(solution)/shard_map/ppermute | solution.py:229
  106.5 32.0 %collective-permute-start.5 = (bf16[2,640,512]{2,1,0:T(8,128)(2,1)S(1)}, bf16[2,640,512]{2,1,0:T(8,128)(2,1)S(1)}, u32[]{:S(2)}, u32[]{:S(2)}) collective-permute-start(bf16[2,640,512]{2,1,0:T(8,128)(2,1)S(1)} %convolution_convert_fusion.2), channel_id=1, source_target_pairs={{0,4},{4,0},{8,12},{12,8},{16,20},{20,16},{24,28},{28,24},{32,36},... | collective-permute-start | bytes 3932168 | tf_op jit(solution)/shard_map/ppermute | solution.py:229
  124.4 24.5 %collective-permute-start.14 = (bf16[2,320,512]{2,1,0:T(8,128)(2,1)S(1)}, bf16[2,320,512]{2,1,0:T(8,128)(2,1)S(1)}, u32[]{:S(2)}, u32[]{:S(2)}) collective-permute-start(bf16[2,320,512]{2,1,0:T(8,128)(2,1)S(1)} %add_convert_fusion.1), channel_id=1, source_target_pairs={{0,4},{4,0},{8,12},{12,8},{16,20},{20,16},{24,28},{28,24},{32,36},... | collective-permute-start | bytes 1966088 | tf_op jit(solution)/shard_map/ppermute | solution.py:229
  133.8 15.1 %collective-permute-start.12 = (bf16[2,320,512]{2,1,0:T(8,128)(2,1)S(1)}, bf16[2,320,512]{2,1,0:T(8,128)(2,1)S(1)}, u32[]{:S(2)}, u32[]{:S(2)}) collective-permute-start(bf16[2,320,512]{2,1,0:T(8,128)(2,1)S(1)} %add_convert_fusion.2), channel_id=1, source_target_pairs={{0,32},{4,36},{8,40},{12,44},{16,48},{20,52},{24,56},{28,60},{32,0... | collective-permute-start | bytes 1966088 | tf_op jit(solution)/shard_map/ppermute | solution.py:229
  134.4 18.9 %collective-permute-start.8 = (bf16[2,320,512]{2,1,0:T(8,128)(2,1)S(1)}, bf16[2,320,512]{2,1,0:T(8,128)(2,1)S(1)}, u32[]{:S(2)}, u32[]{:S(2)}) collective-permute-start(bf16[2,320,512]{2,1,0:T(8,128)(2,1)S(1)} %add_convert_fusion.4), channel_id=1, source_target_pairs={{0,8},{4,12},{8,0},{12,4},{16,24},{20,28},{24,16},{28,20},{32,40},... | collective-permute-start | bytes 1966088 | tf_op jit(solution)/shard_map/ppermute | solution.py:229
  135.5 15.3 %collective-permute-start.10 = (bf16[2,320,512]{2,1,0:T(8,128)(2,1)S(1)}, bf16[2,320,512]{2,1,0:T(8,128)(2,1)S(1)}, u32[]{:S(2)}, u32[]{:S(2)}) collective-permute-start(bf16[2,320,512]{2,1,0:T(8,128)(2,1)S(1)} %add_convert_fusion.3), channel_id=1, source_target_pairs={{0,24},{4,28},{8,16},{12,20},{16,8},{20,12},{24,0},{28,4},{32,56},... | collective-permute-start | bytes 1966088 | tf_op jit(solution)/shard_map/ppermute | solution.py:229
  139.0 15.4 %collective-permute-start.6 = (bf16[2,320,512]{2,1,0:T(8,128)(2,1)S(1)}, bf16[2,320,512]{2,1,0:T(8,128)(2,1)S(1)}, u32[]{:S(2)}, u32[]{:S(2)}) collective-permute-start(bf16[2,320,512]{2,1,0:T(8,128)(2,1)S(1)} %add_convert_fusion.5), channel_id=1, source_target_pairs={{0,96},{4,100},{8,104},{12,108},{16,112},{20,116},{24,120},{28,124... | collective-permute-start | bytes 1966088 | tf_op jit(solution)/shard_map/ppermute | solution.py:229
  149.6 14.3 %collective-permute-start.19 = (bf16[2,160,1024]{2,1,0:T(8,128)(2,1)S(1)}, bf16[2,160,1024]{2,1,0:T(8,128)(2,1)S(1)}, u32[]{:S(2)}, u32[]{:S(2)}) collective-permute-start(bf16[2,160,1024]{2,1,0:T(8,128)(2,1)S(1)} %pad_maximum_fusion.3), channel_id=1, source_target_pairs={{0,24},{4,28},{8,16},{12,20},{16,8},{20,12},{24,0},{28,4},{32,56},... | collective-permute-start | bytes 1966088 | tf_op jit(solution)/shard_map/ppermute | solution.py:229
  151.2 9.0 %collective-permute-start.20 = (bf16[2,160,512]{2,1,0:T(8,128)(2,1)S(1)}, bf16[2,160,512]{2,1,0:T(8,128)(2,1)S(1)}, u32[]{:S(2)}, u32[]{:S(2)}) collective-permute-start(bf16[2,160,512]{2,1,0:T(8,128)(2,1)S(1)} %add_convert_fusion.8), channel_id=1, source_target_pairs={{0,96},{4,100},{8,104},{12,108},{16,112},{20,116},{24,120},{28,124... | collective-permute-start | bytes 983048 | tf_op jit(solution)/shard_map/ppermute | solution.py:229
  153.6 11.1 %collective-permute-start.18 = (bf16[2,160,512]{2,1,0:T(8,128)(2,1)S(1)}, bf16[2,160,512]{2,1,0:T(8,128)(2,1)S(1)}, u32[]{:S(2)}, u32[]{:S(2)}) collective-permute-start(bf16[2,160,512]{2,1,0:T(8,128)(2,1)S(1)} %add_convert_fusion.7), channel_id=1, source_target_pairs={{0,4},{4,0},{8,12},{12,8},{16,20},{20,16},{24,28},{28,24},{32,36},... | collective-permute-start | bytes 983048 | tf_op jit(solution)/shard_map/ppermute | solution.py:229
  154.7 12.7 %collective-permute-start.17 = (bf16[2,160,512]{2,1,0:T(8,128)(2,1)S(1)}, bf16[2,160,512]{2,1,0:T(8,128)(2,1)S(1)}, u32[]{:S(2)}, u32[]{:S(2)}) collective-permute-start(bf16[2,160,512]{2,1,0:T(8,128)(2,1)S(1)} %add_convert_fusion.6), channel_id=1, source_target_pairs={{0,32},{4,36},{8,40},{12,44},{16,48},{20,52},{24,56},{28,60},{32,0... | collective-permute-start | bytes 983048 | tf_op jit(solution)/shard_map/ppermute | solution.py:229
  157.1 19.2 %collective-permute-start.15 = (bf16[384,1280]{1,0:T(8,128)(2,1)S(1)}, bf16[384,1280]{1,0:T(8,128)(2,1)S(1)}, u32[]{:S(2)}, u32[]{:S(2)}) collective-permute-start(bf16[384,1280]{1,0:T(8,128)(2,1)S(1)} %fusion.29.mine_ref), channel_id=1, source_target_pairs={{0,1},{1,0},{4,5},{5,4},{8,9},{9,8},{12,13},{13,12},{16,17},{17,16... | collective-permute-start | bytes 2949128 | tf_op jit(solution)/shard_map/ppermute | solution.py:310
  160.2 20.2 %collective-permute-start.16 = (bf16[384,1280]{1,0:T(8,128)(2,1)S(1)}, bf16[384,1280]{1,0:T(8,128)(2,1)S(1)}, u32[]{:S(2)}, u32[]{:S(2)}) collective-permute-start(bf16[384,1280]{1,0:T(8,128)(2,1)S(1)} %shard_map.96), channel_id=1, source_target_pairs={{0,2},{1,3},{4,6},{5,7},{8,10},{9,11},{12,14},{13,15},{16,18},{17,... | collective-permute-start | bytes 2949128 | tf_op jit(solution)/shard_map/ppermute | solution.py:311
  164.3 7.2 %collective-permute-start.23 = (bf16[2,80,1024]{2,1,0:T(8,128)(2,1)S(1)}, bf16[2,80,1024]{2,1,0:T(8,128)(2,1)S(1)}, u32[]{:S(2)}, u32[]{:S(2)}) collective-permute-start(bf16[2,80,1024]{2,1,0:T(8,128)(2,1)S(1)} %pad_maximum_fusion.4), channel_id=1, source_target_pairs={{0,8},{4,12},{8,0},{12,4},{16,24},{20,28},{24,16},{28,20},{32,40},... | collective-permute-start | bytes 983048 | tf_op jit(solution)/shard_map/ppermute | solution.py:229
  165.3 12.9 %collective-permute-start.22 = (bf16[2,80,1024]{2,1,0:T(8,128)(2,1)S(1)}, bf16[2,80,1024]{2,1,0:T(8,128)(2,1)S(1)}, u32[]{:S(2)}, u32[]{:S(2)}) collective-permute-start(bf16[2,80,1024]{2,1,0:T(8,128)(2,1)S(1)} %pad_maximum_fusion.5), channel_id=1, source_target_pairs={{0,96},{4,100},{8,104},{12,108},{16,112},{20,116},{24,120},{28,124... | collective-permute-start | bytes 983048 | tf_op jit(solution)/shard_map/ppermute | solution.py:229
  167.7 11.2 %collective-permute-start.21 = (bf16[2,80,512]{2,1,0:T(8,128)(2,1)S(1)}, bf16[2,80,512]{2,1,0:T(8,128)(2,1)S(1)}, u32[]{:S(2)}, u32[]{:S(2)}) collective-permute-start(bf16[2,80,512]{2,1,0:T(8,128)(2,1)S(1)} %add_convert_fusion.11), channel_id=1, source_target_pairs={{0,24},{4,28},{8,16},{12,20},{16,8},{20,12},{24,0},{28,4},{32,56},... | collective-permute-start | bytes 491528 | tf_op jit(solution)/shard_map/ppermute | solution.py:229
  176.9 6.3 %collective-permute-start.24 = (bf16[2,40,1024]{2,1,0:T(8,128)(2,1)S(1)}, bf16[2,40,1024]{2,1,0:T(8,128)(2,1)S(1)}, u32[]{:S(2)}, u32[]{:S(2)}) collective-permute-start(bf16[2,40,1024]{2,1,0:T(8,128)(2,1)S(1)} %pad_maximum_fusion.6), channel_id=1, source_target_pairs={{0,4},{4,0},{8,12},{12,8},{16,20},{20,16},{24,28},{28,24},{32,36},... | collective-permute-start | bytes 491528 | tf_op jit(solution)/shard_map/ppermute | solution.py:229
  178.8 5.4 %collective-permute-start.25 = (bf16[2,40,1024]{2,1,0:T(8,128)(2,1)S(1)}, bf16[2,40,1024]{2,1,0:T(8,128)(2,1)S(1)}, u32[]{:S(2)}, u32[]{:S(2)}) collective-permute-start(bf16[2,40,1024]{2,1,0:T(8,128)(2,1)S(1)} %pad_maximum_fusion.7), channel_id=1, source_target_pairs={{0,32},{4,36},{8,40},{12,44},{16,48},{20,52},{24,56},{28,60},{32,0... | collective-permute-start | bytes 491528 | tf_op jit(solution)/shard_map/ppermute | solution.py:229
  179.2 5.6 %collective-permute-start.26 = (bf16[2,40,512]{2,1,0:T(8,128)(2,1)S(1)}, bf16[2,40,512]{2,1,0:T(8,128)(2,1)S(1)}, u32[]{:S(2)}, u32[]{:S(2)}) collective-permute-start(bf16[2,40,512]{2,1,0:T(8,128)(2,1)S(1)} %add_convert_fusion.21), channel_id=1, source_target_pairs={{0,8},{4,12},{8,0},{12,4},{16,24},{20,28},{24,16},{28,20},{32,40},... | collective-permute-start | bytes 245768 | tf_op jit(solution)/shard_map/ppermute | solution.py:229
